TPU v7x, 32 devices: a whole 2x2x4 slice. The times are simulated.
32 devices in a mesh: parts: 2 (over x), route: 16 (over z, y, core).
Axes of the slice: x: 2, y: 2, z: 4, core: 2. Of those that a mesh axis runs over, the one named last changes fastest.
Arguments:
- codes: float32 [16384, 256], P(('parts', 'route')), parts along dimension 0, may hold values from -256 to 256
- labels: int32 [16384], P(('parts', 'route')), parts along dimension 0, may hold values from 0 to 31, as said below
- centroids: bfloat16 [64, 1024, 256], P(('parts', 'route')), parts along dimension 0, may hold values from -6 to 6
- sharpness: bfloat16 [64], P(('parts', 'route')), parts along dimension 0, may hold values from 0.04 to 0.1
Outputs:
- soft_labels: bfloat16 [16384, 1024], P(('parts', 'route')), parts along dimension 0
- new_centroids: float32 [64, 1024, 256], P(('parts', 'route')), parts along dimension 0
There are 2 independent parts, one for each index of `parts`. A program takes and returns all parts, laid end to end along the dimension named above; each array names one. Nothing has to cross between parts.
Inputs may be any that keep to these rules, and one draw needn't show every extreme that they name: Counting frames from 0 within each device, frame i is handled by the device of index 4 * (labels // 8) + i mod 4; cluster c belongs to the device of index c // 2. At most 64 frames of one device are handled by any one device, and in every draw some 4 devices each handle exactly 64 frames of every device.
All inputs are finite; a program needn't handle non-finite values.
Results may differ from a plain program's by a relative error of at most 0.007.
Values may be sent and summed in bfloat16 or wider, within the bound.
No kernel may reach another device: no remote copies, remote signals or barrier semaphores. Data moves between devices by JAX's collectives and lax.ppermute only.
A program may use at most 128 MiB of HBM per device.

v0:
```python
import jax
import jax.numpy as jnp
from jax import lax
from jax.sharding import PartitionSpec as P

GRP = 4


def rows_per_block(row_count):
    return min(512, max(8, row_count // 8))


def refine_rows(row_codes, local_ids, centres, sharp_vals, block_size):
    clusters = centres.shape[0]
    fine_count = centres.shape[1]
    row_count = row_codes.shape[0]
    block_count = -(-row_count // block_size) + clusters
    onehot = (local_ids[:, None] == jnp.arange(clusters, dtype=jnp.int32)[None, :]).astype(
        jnp.int32
    )
    before = jnp.cumsum(onehot, axis=0) - onehot
    rank_in = jnp.sum(before * onehot, axis=1)
    counts = jnp.sum(onehot, axis=0)
    padded = (counts + block_size - 1) // block_size * block_size
    seg_ends = jnp.cumsum(padded)
    starts = seg_ends - padded
    live_row = local_ids >= 0
    slot_index = jnp.where(
        live_row, jnp.sum(starts[None, :] * onehot, axis=1) + rank_in, block_count * block_size
    )
    buffer = (
        jnp.zeros((block_count * block_size, row_codes.shape[1]), row_codes.dtype)
        .at[slot_index]
        .set(row_codes, mode="drop")
    )
    live_mask = (
        jnp.zeros((block_count * block_size,), jnp.bfloat16)
        .at[slot_index]
        .set(jnp.ones((row_count,), jnp.bfloat16), mode="drop")
    )
    block_start = jnp.arange(block_count, dtype=jnp.int32) * block_size
    owners = jnp.minimum(
        jnp.sum((seg_ends[None, :] <= block_start[:, None]).astype(jnp.int32), axis=1), clusters - 1
    )
    used_blocks = seg_ends[-1] // block_size
    half_norm = 0.5 * jnp.einsum(
        "kfd,kfd->kf", centres, centres, preferred_element_type=jnp.float32
    )
    scale_vals = sharp_vals.astype(jnp.float32)

    def advance(block_index, state_in):
        weighted, mass_sum, soft_buf = state_in
        cluster_id = owners[block_index]
        row_start = block_index * block_size
        block_codes = lax.dynamic_slice_in_dim(buffer, row_start, block_size, 0)
        keep_mask = lax.dynamic_slice_in_dim(live_mask, row_start, block_size, 0)
        centre = centres[cluster_id]
        dot_terms = lax.dot_general(
            block_codes, centre, (((1,), (1,)), ((), ())), preferred_element_type=jnp.float32
        )
        logits = scale_vals[cluster_id] * (dot_terms - half_norm[cluster_id][None, :])
        shifted = jnp.exp(logits - jnp.max(logits, axis=1, keepdims=True))
        soft_vals = (float(fine_count) * shifted / jnp.sum(shifted, axis=1, keepdims=True)).astype(
            jnp.bfloat16
        )
        masked = soft_vals * keep_mask[:, None]
        update = lax.dot_general(
            masked, block_codes, (((0,), (0,)), ((), ())), preferred_element_type=jnp.float32
        )
        weighted = weighted.at[cluster_id].add(update)
        mass_sum = mass_sum.at[cluster_id].add(jnp.sum(masked.astype(jnp.float32), axis=0))
        soft_buf = lax.dynamic_update_slice_in_dim(soft_buf, soft_vals, row_start, 0)
        return (weighted, mass_sum, soft_buf)

    start_state = (
        jnp.zeros((clusters, fine_count, row_codes.shape[1]), jnp.float32),
        jnp.zeros((clusters, fine_count), jnp.float32),
        jnp.zeros((block_count * block_size, fine_count), jnp.bfloat16),
    )
    weighted, mass_sum, soft_buf = lax.fori_loop(jnp.int32(0), used_blocks, advance, start_state)
    soft_rows = jnp.take(soft_buf, jnp.minimum(slot_index, block_count * block_size - 1), axis=0)
    return (soft_rows, weighted, mass_sum)


def pack_rows(rounded, target, local_id, route_count, capacity):
    onehot = (target[:, None] == jnp.arange(route_count, dtype=jnp.int32)[None, :]).astype(
        jnp.int32
    )
    slot_num = jnp.sum((jnp.cumsum(onehot, axis=0) - onehot) * onehot, axis=1)
    flat_slot = target * capacity + slot_num
    send_codes = (
        jnp.zeros((route_count * capacity, rounded.shape[1]), jnp.bfloat16)
        .at[flat_slot]
        .set(rounded)
    )
    send_ids = jnp.full((route_count * capacity,), -1, jnp.int32).at[flat_slot].set(local_id)
    return (
        send_codes.reshape(route_count, capacity, rounded.shape[1]),
        send_ids.reshape(route_count, capacity),
        flat_slot,
    )


def shards(codes, labels, centroids, sharpness):
    route_count = lax.axis_size("route")
    frame_count = codes.shape[0]
    code_width = codes.shape[1]
    per_device = centroids.shape[0]
    fine_count = centroids.shape[1]
    capacity = max(8, 2 * frame_count // route_count)
    rounded = codes.astype(jnp.bfloat16)
    owner = labels // per_device
    room = capacity * GRP
    local_id = labels - owner * per_device
    send_codes, send_ids, flat_slot = pack_rows(rounded, owner, local_id, route_count, room)
    recv_codes, recv_ids = (
        lax.all_to_all(send_codes, "route", split_axis=0, concat_axis=0, tiled=True),
        lax.all_to_all(send_ids, "route", split_axis=0, concat_axis=0, tiled=True),
    )
    row_count = route_count * room
    soft_rows, weighted, mass_sum = refine_rows(
        recv_codes.reshape(row_count, code_width),
        recv_ids.reshape(row_count),
        centroids,
        sharpness,
        rows_per_block(row_count),
    )
    returned = lax.all_to_all(
        soft_rows.reshape(route_count, room, fine_count),
        "route",
        split_axis=0,
        concat_axis=0,
        tiled=True,
    )
    soft_labels = jnp.take(returned.reshape(route_count * room, fine_count), flat_slot, axis=0)
    new_centroids = (weighted + centroids.astype(jnp.float32)) / (mass_sum[:, :, None] + 1.0)
    return (soft_labels, new_centroids)


def solution(mesh):
    placed = (
        P(("parts", "route"), None),
        P(("parts", "route")),
        P(("parts", "route"), None, None),
        P(("parts", "route")),
    )
    return jax.shard_map(
        shards,
        mesh=mesh,
        in_specs=placed,
        out_specs=(P(("parts", "route"), None), P(("parts", "route"), None, None)),
        check_vma=False,
    )
```

profile of v0, /device:TPU:8, one launch (start us, length us, event | category | flops | bytes accessed | tf_op | source)
XLA Modules:
  0.0 373.2 jit_solution(17700122314846987146)
XLA Ops:
  0.6 0.7 multiply_subtract_fusion
  1.3 1.2 reduce-window.16
  2.5 0.2 slice_reduce_fusion.1
  2.9 3.0 scatter_custom_fusion
  5.9 6.3 %all-to-all-start = ((s32[16,1,256]{2,1,0:T(1,128)}), s32[16,1,256]{2,1,0:T(1,128)S(1)}, u32[]{:S(2)}, u32[]{:S(2)}) async-start(s32[16,1,256]{2,1,0:T(1,128)} %bitcast.9), calls=%async_computation | async-start | bytes 32768 | tf_op jit(solution)/shard_map/all_to_all | solution.py:118
  12.2 4.5 %scatter_custom_fusion.1 = bf16[4096,256]{1,0:T(8,128)(2,1)} fusion(s32[512]{0:T(512)S(1)} %get-tuple-element.116, bf16[]{:T(256)} %constant.168.clone.1, f32[512,256]{1,0:T(8,128)} %param.10), kind=kCustom, calls=%fused_computation.36 | custom fusion | flops 131072 | bytes 2621442 | tf_op jit(solution)/shard_map/scatter | solution.py:94
  16.7 0.5 all-to-all-done
  17.2 5.6 %all-to-all-start.1 = ((bf16[16,256,256]{2,1,0:T(8,128)(2,1)}), bf16[16,256,256]{2,1,0:T(8,128)(2,1)S(1)}, u32[]{:S(2)}, u32[]{:S(2)}) async-start(bf16[16,256,256]{2,1,0:T(8,128)(2,1)} %bitcast.19), calls=%async_computation.1 | async-start | bytes 4194304 | tf_op jit(solution)/shard_map/all_to_all | solution.py:117
  22.9 0.4 fusion.12
  23.2 0.1 convert_reduce_fusion.1
  23.4 0.2 reduce-window.20
  23.6 0.7 slice.53
  26.3 0.6 reduce-window.21
  26.9 0.2 slice_reduce_fusion
  27.1 0.2 reduce-window.24
  28.4 28.7 %scatter_custom_fusion.3 = bf16[5120]{0:T(1024)(128)(2,1)S(1)} fusion(s32[4096]{0:T(1024)S(1)} %bitcast.106, bf16[4096]{0:T(1024)(128)(2,1)S(1)} %broadcast.331, bf16[]{:T(256)} %constant.168.clone.1), kind=kCustom, calls=%fused_computation.70 | custom fusion | bytes 10242 | tf_op jit(solution)/shard_map/scatter | solution.py:39
  57.3 11.4 %all-to-all-done.1 = bf16[16,256,256]{2,1,0:T(8,128)(2,1)S(1)} async-done(((bf16[16,256,256]{2,1,0:T(8,128)(2,1)}), bf16[16,256,256]{2,1,0:T(8,128)(2,1)S(1)}, u32[]{:S(2)}, u32[]{:S(2)}) %all-to-all-start.1) | async-done | bytes 2097184 | tf_op jit(solution)/shard_map/all_to_all | solution.py:117
  68.7 19.8 %scatter_custom_fusion.2 = bf16[5120,256]{1,0:T(8,128)(2,1)} fusion(s32[4096]{0:T(1024)S(1)} %bitcast.107, bf16[4096,256]{1,0:T(8,128)(2,1)S(1)} %bitcast.93, bf16[]{:T(256)} %constant.168.clone.1), kind=kCustom, calls=%fused_computation.34 | custom fusion | bytes 2621442 | tf_op jit(solution)/shard_map/scatter | solution.py:34
  88.5 5.3 %broadcast_in_dim.75 = bf16[5120,1024]{1,0:T(8,128)(2,1)} broadcast(bf16[]{:T(256)} %constant.168.clone.1), dimensions={} | broadcast | bytes 10485762 | tf_op jit(solution)/shard_map/broadcast_in_dim | solution.py:78
  94.0 0.5 copy-done.1
  94.5 26.5 %while.16 = (s32[]{:T(128)}, f32[2,1024,256]{2,1,0:T(8,128)S(1)}, f32[2,1024]{1,0:T(2,128)S(1)}, bf16[5120,1024]{1,0:T(8,128)(2,1)}, s32[]{:T(128)}, /*index=5*/...) while((s32[]{:T(128)}, f32[2,1024,256]{2,1,0:T(8,128)S(1)}, ...), condition=%wide.region_20.21_spmd, body=%wide.region_14.20_spmd.sunk | while | flops 546308096 | bytes 13693830 | solution.py:80
  94.5 0.6 dynamic_slice.42
  97.0 0.6 dynamic_slice.43
  97.6 2.1 fusion.41
  99.7 1.2 fusion.42
  100.9 2.2 constant_dynamic-update-slice_fusion.2
  103.0 0.7 and_reduce_fusion.4
  103.8 2.3 fusion.43
  106.1 0.3 convert_reduce_fusion.3
  106.4 0.7 and_reduce_fusion.5
  107.1 0.6 broadcast_select_fusion.5
  107.7 0.6 dynamic_slice.42
  110.3 0.6 dynamic_slice.43
  110.9 2.1 fusion.41
  112.9 1.2 fusion.42
  114.1 2.2 constant_dynamic-update-slice_fusion.2
  116.3 0.7 and_reduce_fusion.4
  117.1 2.3 fusion.43
  119.4 0.3 convert_reduce_fusion.3
  119.6 0.7 and_reduce_fusion.5
  120.4 0.6 broadcast_select_fusion.5
  121.0 26.2 %gather_fusion = bf16[4096,1024]{1,0:T(8,128)(2,1)} fusion(bf16[5120,1024]{1,0:T(8,128)(2,1)} %get-tuple-element.86, s32[4096]{0:T(1024)S(1)} %broadcast_clamp_fusion), kind=kCustom, calls=%fused_computation | custom fusion | bytes 16793600 | tf_op jit(solution)/shard_map/jit(_take)/gather | solution.py:81
  147.2 7.3 %broadcast_select_fusion.1 = bf16[16,256,1024]{2,1,0:T(8,128)(2,1)} fusion(bf16[16,256,1024]{2,1,0:T(8,128)(2,1)} %bitcast.92, pred[16,256]{1,0:T(8,128)(4,1)S(1)} %get-tuple-element.117), kind=kLoop, calls=%fused_computation.29 | loop fusion | flops 4194304 | bytes 16781312 | tf_op jit(solution)/shard_map/jit(_take)/select_n | solution.py:81
  154.5 29.6 %all-to-all-start.2 = ((bf16[16,256,1024]{2,1,0:T(8,128)(2,1)}), bf16[16,256,1024]{2,1,0:T(8,128)(2,1)}, u32[]{:S(2)}, u32[]{:S(2)}) async-start(bf16[16,256,1024]{2,1,0:T(8,128)(2,1)} %broadcast_select_fusion.1), calls=%async_computation.2 | async-start | bytes 16777216 | tf_op jit(solution)/shard_map/all_to_all | solution.py:128
  184.2 1.7 fusion.13
  185.8 179.0 %all-to-all-done.2 = bf16[16,256,1024]{2,1,0:T(8,128)(2,1)} async-done(((bf16[16,256,1024]{2,1,0:T(8,128)(2,1)}), bf16[16,256,1024]{2,1,0:T(8,128)(2,1)}, u32[]{:S(2)}, u32[]{:S(2)}) %all-to-all-start.2) | async-done | bytes 8388640 | tf_op jit(solution)/shard_map/all_to_all | solution.py:128
  364.9 7.2 %gather_fusion.1 = bf16[512,1024]{1,0:T(8,128)(2,1)S(1)} fusion(bf16[4096,1024]{1,0:T(8,128)(2,1)} %bitcast.23, s32[1024]{0:T(1024)S(1)} %pad_clamp_fusion), kind=kCustom, calls=%fused_computation.1 | custom fusion | bytes 2099200 | tf_op jit(solution)/shard_map/jit(_take)/gather | solution.py:135
  372.1 1.1 broadcast_select_fusion.2
  (39 shorter events, 1.0 us)
Async XLA Ops:
  5.9 11.3 %all-to-all-start = ((s32[16,1,256]{2,1,0:T(1,128)}), s32[16,1,256]{2,1,0:T(1,128)S(1)}, u32[]{:S(2)}, u32[]{:S(2)}) async-start(s32[16,1,256]{2,1,0:T(1,128)} %bitcast.9), calls=%async_computation | async-start | bytes 32768 | tf_op jit(solution)/shard_map/all_to_all | solution.py:118
  17.2 5.6 %copy-start.3 = (bf16[2]{0:T(256)(128)(2,1)S(1)}, bf16[2]{0:T(256)(128)(2,1)}, u32[]{:S(2)}) copy-start(bf16[2]{0:T(256)(128)(2,1)} %param.13) | copy-start | bytes 16
  17.2 5.7 %copy-start = (bf16[2,1024,256]{2,1,0:T(8,128)(2,1)S(1)}, bf16[2,1024,256]{2,1,0:T(8,128)(2,1)}, u32[]{:S(2)}) copy-start(bf16[2,1024,256]{2,1,0:T(8,128)(2,1)} %param.12) | copy-start | bytes 3145732
  17.2 51.5 %all-to-all-start.1 = ((bf16[16,256,256]{2,1,0:T(8,128)(2,1)}), bf16[16,256,256]{2,1,0:T(8,128)(2,1)S(1)}, u32[]{:S(2)}, u32[]{:S(2)}) async-start(bf16[16,256,256]{2,1,0:T(8,128)(2,1)} %bitcast.19), calls=%async_computation.1 | async-start | bytes 4194304 | tf_op jit(solution)/shard_map/all_to_all | solution.py:117
  93.8 0.7 copy-start.1
  93.8 0.7 copy-start.2
  154.5 210.3 %all-to-all-start.2 = ((bf16[16,256,1024]{2,1,0:T(8,128)(2,1)}), bf16[16,256,1024]{2,1,0:T(8,128)(2,1)}, u32[]{:S(2)}, u32[]{:S(2)}) async-start(bf16[16,256,1024]{2,1,0:T(8,128)(2,1)} %broadcast_select_fusion.1), calls=%async_computation.2 | async-start | bytes 16777216 | tf_op jit(solution)/shard_map/all_to_all | solution.py:128
where the time goes:
time: 378 us; the launch traced here: 373 us
  waiting for transfers between devices  191 us (51%)
  local copies, waits for them, and re-layouts  94.6 us (25%)
  starting transfers between devices  41.5 us (11%)
  other arithmetic  29.7 us (8%)
  matrix products  8.68 us (2%)
  loops' own time  4 us (1%)
    all_to_all x1, waiting for transfers between devices, shards(): lax.all_to_all(soft_rows.reshape(route_count, room, fine_count), 'route',...  179 us
    all_to_all x1, starting transfers between devices, shards(): lax.all_to_all(soft_rows.reshape(route_count, room, fine_count), 'route',...  29.6 us
    scatter x1, local copies, waits for them, and re-layouts, refine_rows(): live_mask = jnp.zeros((block_count * block_size,), jnp.bfloat16).at[slot_...  28.7 us
    gather x1, local copies, waits for them, and re-layouts, refine_rows(): jnp.take(soft_buf, jnp.minimum(slot_index, block_count * block_size - 1),...  26.2 us
    scatter x1, local copies, waits for them, and re-layouts, refine_rows(): buffer = jnp.zeros((block_count * block_size, row_codes.shape[1]), row_co...  19.8 us
    all_to_all x1, waiting for transfers between devices, shards(): lax.all_to_all(send_codes, 'route', split_axis=0, concat_axis=0, tiled=True)  11.4 us
  transfers between devices with their start and end apart: 3, of which 3 were waited for; matrix products, arithmetic and copies ran while one was open for 10% of the time, Pallas kernels for 0%

commit v1 on v0

v1 whole, which is shorter than its diff:
```python
import functools

import jax
import jax.numpy as jnp
from jax import lax
from jax.experimental import pallas as pl
from jax.experimental.pallas import tpu as pltpu
from jax.sharding import PartitionSpec as P

GRP = 4
META = 16
BF = jnp.bfloat16
F32 = jnp.float32
VMEM = pl.BlockSpec(memory_space=pltpu.VMEM)
SMEM = pl.BlockSpec(memory_space=pltpu.SMEM)


def call(body, out_shape, n_in, flops, nbytes, in_specs=None, scratch=()):
    many = isinstance(out_shape, (list, tuple))
    return pl.pallas_call(
        body,
        out_shape=out_shape,
        in_specs=in_specs or [VMEM] * n_in,
        out_specs=[VMEM] * len(out_shape) if many else VMEM,
        scratch_shapes=list(scratch),
        compiler_params=pltpu.CompilerParams(vmem_limit_bytes=40 * 1024 * 1024),
        cost_estimate=pl.CostEstimate(flops=flops, bytes_accessed=nbytes, transcendentals=0),
    )


def three(value):
    first = value.astype(BF)
    rest = value - first.astype(F32)
    second = rest.astype(BF)
    third = (rest - second.astype(F32)).astype(BF)
    return first, second, third


def cluster_lanes(shape):
    lane = lax.broadcasted_iota(jnp.int32, shape, 1)
    part = lane & 15
    pair = (lane >> 4) & 3
    norm = (lane < 64) & (part < 6)
    sharp = (lane >= 64) & (lane < 128) & ((part == 6) | (part == 7))
    plain = (lane >= 128) & (lane < 128 + 2 * GRP)
    cluster = jnp.where(
        plain,
        lane - 128,
        2 * pair + jnp.where(norm, (part >= 3).astype(jnp.int32), (part == 7).astype(jnp.int32)),
    )
    return cluster, norm | sharp | plain


def pack_body(groups, rows, key_row, key_col, codes, *outs):
    frames, width = codes.shape
    kr, kc = key_row[...], key_col[...]
    lane = lax.broadcasted_iota(jnp.int32, (1, frames), 1)
    sub = lax.broadcasted_iota(jnp.int32, (frames, 1), 0)
    ur, uc = kr * frames + lane, kc * frames + sub
    gr = kr >> 3
    base_r = gr * (8 * frames)
    rank = jnp.sum(((uc < ur) & (uc >= base_r)).astype(jnp.int32), axis=0, keepdims=True)
    slot = gr * rows + rank
    rounded = codes[...].astype(BF)
    place = lax.broadcasted_iota(jnp.int32, (rows, frames), 0)
    cluster, used = cluster_lanes((1, width))
    row = lax.broadcasted_iota(jnp.int32, (META, width), 0)
    for k in range(groups):
        pick = (slot == place + k * rows).astype(F32).astype(BF)
        outs[k][:rows, :] = jnp.dot(pick, rounded, preferred_element_type=F32).astype(BF)
        inside = kc >= 8 * k
        first = jnp.sum((inside & (kc < 8 * k + cluster)).astype(F32), axis=0, keepdims=True)
        last = jnp.sum((inside & (kc < 8 * k + cluster + 1)).astype(F32), axis=0, keepdims=True)
        last = jnp.where(used, last, first)
        bounds = jnp.where(row == 0, first, jnp.where(row == 1, last, 0.0))
        outs[k][rows:, :] = bounds.astype(BF)
    gc = kc >> 3
    base_c = gc * (8 * frames)
    rank_c = jnp.sum(((ur < uc) & (ur >= base_c)).astype(jnp.int32), axis=1, keepdims=True)
    outs[groups][...] = gc * rows + rank_c


def norm_body(sharp, centres, out):
    row = lax.broadcasted_iota(jnp.int32, (META, centres.shape[1]), 0)
    ones = jnp.ones((8, centres.shape[2]), BF)
    total = jnp.zeros(row.shape, F32)
    for c in range(centres.shape[0]):
        wide = centres[c].astype(F32)
        square = wide * wide
        high = square.astype(BF)
        low = (square - high.astype(F32)).astype(BF)
        dims = (((1,), (1,)), ((), ()))
        norm = lax.dot_general(ones, high, dims, preferred_element_type=F32)
        norm = norm + lax.dot_general(ones, low, dims, preferred_element_type=F32)
        terms = three(-0.5 * norm[0:1, :])
        for t in range(3):
            total = jnp.where(row == 3 * c + t, terms[t].astype(F32), total)
        total = jnp.where(row == 6 + c, sharp[c], total)
    out[...] = total.astype(BF)


def member_lanes(block, rows):
    bounds = block[rows:, :].astype(F32)
    row = lax.broadcasted_iota(jnp.int32, (rows, block.shape[1]), 0).astype(F32)
    return ((row >= bounds[0:1, :]) & (row < bounds[1:2, :])).astype(F32)


def soft_body(rows, block, c0, c1, c2, c3, m0, m1, m2, m3, out):
    centres = (c0, c1, c2, c3)
    member = member_lanes(block, rows)
    member_bf = member.astype(BF)
    table = jnp.concatenate([m0[...], m1[...], m2[...], m3[...]], axis=0)
    codes = block[:rows, :]
    logits = jnp.dot(member_bf[:, :64], table, preferred_element_type=F32)
    for r in range(2 * GRP):
        chosen = codes * member_bf[:, 128 + r : 129 + r]
        logits = logits + lax.dot_general(
            chosen, centres[r // 2][r % 2], (((1,), (1,)), ((), ())), preferred_element_type=F32
        )
    scale = jnp.dot(member_bf[:, 64:128], table[:, :128], preferred_element_type=F32)
    logits = logits * scale[:, 0:1]
    shifted = jnp.exp(logits - jnp.max(logits, axis=1, keepdims=True))
    fine = float(out.shape[1])
    out[...] = (shifted * (fine / jnp.sum(shifted, axis=1, keepdims=True))).astype(BF)


def weighted_body(groups, rows, which, *refs):
    blocks, softs, out = refs[:groups], refs[groups : 2 * groups], refs[2 * groups]
    width = blocks[0].shape[1]
    dims = (((0,), (0,)), ((), ()))
    members = [member_lanes(b, rows).astype(BF) for b in blocks]
    mass = 0.0
    for m, s in zip(members, softs):
        mass = mass + lax.dot_general(m[:, 128:], s[...], dims, preferred_element_type=F32)
    row = lax.broadcasted_iota(jnp.int32, (META, out.shape[2]), 0)
    for n, r in enumerate(which):
        total = 0.0
        for b, m, s in zip(blocks, members, softs):
            chosen = b[:rows, :] * m[:, 128 + r : 129 + r]
            total = total + lax.dot_general(chosen, s[...], dims, preferred_element_type=F32)
        out[n, :width, :] = total.astype(BF)
        out[n, width:, :] = mass_rows(row, mass[r : r + 1, :])


def mass_rows(row, mass):
    terms = three(mass)
    total = jnp.zeros(row.shape, F32)
    for t in range(3):
        total = jnp.where(row == t, terms[t].astype(F32), total)
    return total.astype(BF)


def combine_body(keep, got, out):
    width = out.shape[1] - META
    row = lax.broadcasted_iota(jnp.int32, (META, out.shape[2]), 0)
    for c in range(out.shape[0]):
        n = c + out.shape[0]
        out[c, :width, :] = (
            keep[n, :width, :].astype(F32) + got[n, :width, :].astype(F32)
        ).astype(BF)
        mass = keep[n, width:, :].astype(F32) + got[n, width:, :].astype(F32)
        out[c, width:, :] = mass_rows(row, jnp.sum(mass, axis=0, keepdims=True))


def finish_body(keep, got, far, centres, out):
    width = centres.shape[2]
    for c in range(out.shape[0]):
        total = keep[c].astype(F32) + got[c].astype(F32) + far[c].astype(F32)
        mass = jnp.sum(total[width:, :], axis=0, keepdims=True) + 1.0
        column = jnp.broadcast_to(mass, (8, mass.shape[1])).T[:, 0:1]
        out[c] = (total[:width, :].T + centres[c].astype(F32)) / column


def unpack_body(groups, rows, slot, *refs):
    frames = slot.shape[0]
    out = refs[groups]
    lane = lax.broadcasted_iota(jnp.int32, (frames, rows), 1)
    total = 0.0
    for k in range(groups):
        pick = (slot[...] == lane + k * rows).astype(F32).astype(BF)
        total = total + jnp.dot(pick, refs[k][...], preferred_element_type=F32)
    out[...] = total.astype(BF)


def shards(codes, labels, centroids, sharpness):
    route = lax.axis_size("route")
    frames, width = codes.shape
    per_device, fine, _ = centroids.shape
    groups = route // GRP
    rows = GRP * max(8, 2 * frames // route)
    me = lax.axis_index("route")
    group, place = me // GRP, me % GRP

    def swap(x, mask):
        return lax.ppermute(x, "route", [(r, r ^ mask) for r in range(route)])

    within = labels % (GRP * per_device)
    key = ((labels // (GRP * per_device)) ^ group) * (GRP * per_device) + (
        ((within // per_device) ^ place) * per_device + within % per_device
    )
    far_centres = swap(centroids, 2)
    block_shape = jax.ShapeDtypeStruct((rows + META, width), BF)
    *send, slot = call(
        functools.partial(pack_body, groups, rows),
        [block_shape] * groups + [jax.ShapeDtypeStruct((frames, 1), jnp.int32)],
        3,
        2 * groups * rows * frames * width,
        frames * width * 8,
    )(key.reshape(1, frames), key.reshape(frames, 1), codes)
    order = sorted(range(1, groups), key=lambda k: (-(k.bit_length()), k))
    blocks = {0: send[0]}
    for k in order:
        blocks[k] = swap(send[k], GRP * k)
    near_centres = swap(centroids, 1)
    meta = call(
        norm_body,
        jax.ShapeDtypeStruct((META, fine), BF),
        2,
        4 * 8 * per_device * fine * width,
        per_device * fine * width * 2,
        in_specs=[SMEM, VMEM],
    )(sharpness.astype(F32), centroids)
    metas = [meta] + [swap(meta, m) for m in range(1, GRP)]
    last_centres = swap(far_centres, 1)

    soft = {}
    back = {}
    for k in order + [0]:
        soft[k] = call(
            functools.partial(soft_body, rows),
            jax.ShapeDtypeStruct((rows, fine), BF),
            9,
            2 * rows * fine * width * 2 * GRP,
            GRP * per_device * fine * width * 2,
        )(blocks[k], centroids, near_centres, far_centres, last_centres, *metas)
        back[k] = swap(soft[k], GRP * k) if k else soft[k]

    def sums(which):
        return call(
            functools.partial(weighted_body, groups, rows, which),
            jax.ShapeDtypeStruct((len(which), width + META, fine), BF),
            2 * groups,
            2 * groups * rows * fine * width * len(which),
            groups * rows * fine * 2,
        )(*[blocks[k] for k in range(groups)], *[soft[k] for k in range(groups)])

    got = swap(sums((2, 3, 6, 7)), 1)
    keep = sums((0, 1, 4, 5))
    chip = call(
        combine_body,
        jax.ShapeDtypeStruct((per_device, width + META, fine), BF),
        2,
        per_device * fine * width * 4,
        per_device * fine * width * 12,
    )(keep, got)
    far = swap(chip, 2)
    new_centroids = call(
        finish_body,
        jax.ShapeDtypeStruct(centroids.shape, F32),
        4,
        per_device * fine * width * 8,
        per_device * fine * width * 16,
    )(keep, got, far, centroids)
    soft_labels = call(
        functools.partial(unpack_body, groups, rows),
        jax.ShapeDtypeStruct((frames, fine), BF),
        1 + groups,
        2 * frames * groups * rows * fine,
        groups * rows * fine * 2,
    )(slot, *[back[k] for k in range(groups)])
    return soft_labels, new_centroids


def solution(mesh):
    placed = (
        P(("parts", "route"), None),
        P(("parts", "route")),
        P(("parts", "route"), None, None),
        P(("parts", "route")),
    )
    return jax.shard_map(
        shards,
        mesh=mesh,
        in_specs=placed,
        out_specs=(P(("parts", "route"), None), P(("parts", "route"), None, None)),
        check_vma=False,
    )
```

time: 378 us -> 119 us (0.31); the launches traced: 373 us -> 119 us
  waiting for transfers between devices: 191 us -> 74 us
  local copies, waits for them, and re-layouts: 94.6 us -> 2.42 us
  other arithmetic: 29.7 us -> 1.36 us
  starting transfers between devices: 41.5 us -> 14.9 us
  Pallas kernels: 0 us -> 25.5 us
  matrix products: 8.68 us -> 0 us
  loops' own time: 4 us -> 0 us
    all_to_all x3 -> x0, waiting for transfers between devices: 191 us -> none  [the longest x1 179 us: shards(): lax.all_to_all(soft_rows.reshape(route_count, room, fine_count), 'route',...]
    ppermute x0 -> x14, waiting for transfers between devices: none -> 74 us  [swap(): return lax.ppermute(x, 'route', [(r, r ^ mask) for r in range(route)])]
    scatter x3 -> x0, local copies, waits for them, and re-layouts: 51.5 us -> none  [the longest x1 28.7 us: refine_rows(): live_mask = jnp.zeros((block_count * block_size,), jnp.bfloat16).at[slot_...]
    all_to_all x3 -> x0, starting transfers between devices: 41.5 us -> none  [the longest x1 29.6 us: shards(): lax.all_to_all(soft_rows.reshape(route_count, room, fine_count), 'route',...]
    gather x2 -> x0, local copies, waits for them, and re-layouts: 33.4 us -> none  [the longest x1 26.2 us: refine_rows(): jnp.take(soft_buf, jnp.minimum(slot_index, block_count * block_size - 1),...]
    pallas_call x0 -> x11, Pallas kernels: none -> 25.5 us  [the longest x4 12.1 us: shards(): call(functools.partial(soft_body, rows), jax.ShapeDtypeStruct((rows, fine...]
    ppermute x0 -> x14, starting transfers between devices: none -> 14.9 us  [swap(): return lax.ppermute(x, 'route', [(r, r ^ mask) for r in range(route)])]
    dot_general x4 -> x0, matrix products: 8.68 us -> none  [the longest x2 4.53 us: advance(): lax.dot_general(masked, block_codes, (((0,), (0,)), ((), ())), preferred_...]
  transfers between devices with their start and end apart: 3 -> 14, of which waited for: 3 -> 9; matrix products, arithmetic and copies ran while one was open for 10% -> 1% of each run, Pallas kernels for 0% -> 12%
where the time goes in v1:
time: 119 us
  waiting for transfers between devices  74 us (62%)
  Pallas kernels  25.5 us (21%)
  starting transfers between devices  14.9 us (13%)
  local copies, waits for them, and re-layouts  2.42 us (2%)
  other arithmetic  1.36 us (1%)
    ppermute x14, waiting for transfers between devices, swap(): return lax.ppermute(x, 'route', [(r, r ^ mask) for r in range(route)])  74 us
    ppermute x14, starting transfers between devices, swap(): return lax.ppermute(x, 'route', [(r, r ^ mask) for r in range(route)])  14.9 us
    pallas_call x4, Pallas kernels, shards(): call(functools.partial(soft_body, rows), jax.ShapeDtypeStruct((rows, fine...  12.1 us
    pallas_call x2, Pallas kernels, sums(): call(functools.partial(weighted_body, groups, rows, which), jax.ShapeDtyp...  5.69 us
    pallas_call x1, Pallas kernels, shards(): call(finish_body, jax.ShapeDtypeStruct(centroids.shape, F32), 4, per_devi...  2.5 us
  transfers between devices with their start and end apart: 14, of which 9 were waited for; matrix products, arithmetic and copies ran while one was open for 1% of the time, Pallas kernels for 12%

profile of v1, /device:TPU:8, one launch (start us, length us, event | category | flops | bytes accessed | tf_op | source)
XLA Modules:
  0.0 119.0 jit_solution(5064370324273961487)
XLA Ops:
  0.6 0.0 copy-start.1
  0.6 1.6 %collective-permute-start.1 = (bf16[2,1024,256]{2,1,0:T(8,128)(2,1)}, bf16[2,1024,256]{2,1,0:T(8,128)(2,1)S(1)}, u32[]{:S(2)}, u32[]{:S(2)}) collective-permute-start(bf16[2,1024,256]{2,1,0:T(8,128)(2,1)} %centres.3), channel_id=1, source_target_pairs={{0,2},{1,3},{2,0},{3,1},{4,6},{5,7},{6,4},{7,5},{8,10},{9,11},{10,... | collective-permute-start | bytes 3145736 | tf_op jit(solution)/shard_map/ppermute | solution.py:195
  2.2 0.0 collective-permute-start
  2.2 23.6 %collective-permute-done.1.c2 = bf16[2,1024,256]{2,1,0:T(8,128)(2,1)S(1)} collective-permute-done((bf16[2,1024,256]{2,1,0:T(8,128)(2,1)}, bf16[2,1024,256]{2,1,0:T(8,128)(2,1)S(1)}, u32[]{:S(2)}, u32[]{:S(2)}) %collective-permute-start.1) | collective-permute-done | bytes 1048608 | tf_op jit(solution)/shard_map/ppermute | solution.py:195
  25.8 0.0 collective-permute-start.2
  25.8 0.7 fusion.2
  26.5 0.1 copy.6.key_col
  26.7 0.0 copy-start.2
  26.7 1.0 copy-done.2
  27.7 1.5 %shard_map.59 = (bf16[272,256]{1,0:T(8,128)(2,1)S(1)}, bf16[272,256]{1,0:T(8,128)(2,1)S(1)}, bf16[272,256]{1,0:T(8,128)(2,1)S(1)}, bf16[272,256]{1,0:T(8,128)(2,1)S(1)}, s32[512,1]{1,0:T(8,128)S(1)}) custom-call(s32[1,512]{1,0:T(1,128)S(1)} %bitcast.3, s32[512,1]{1,0:T(8,128)S(1)} %copy.6.key_col, f32[512,256]{1,0:T(8,128)S(1)} %copy-done.2), custom_call_target="tpu_custom_call" | custom-call | flops 268435456 | bytes 1048576 | tf_op jit(solution)/shard_map/pallas_call | solution.py:203
  29.2 1.6 %collective-permute-start.10 = (bf16[272,256]{1,0:T(8,128)(2,1)S(1)}, bf16[272,256]{1,0:T(8,128)(2,1)S(1)}, u32[]{:S(2)}, u32[]{:S(2)}) collective-permute-start(bf16[272,256]{1,0:T(8,128)(2,1)S(1)} %get-tuple-element.11), channel_id=1, source_target_pairs={{0,12},{1,13},{2,14},{3,15},{4,8},{5,9},{6,10},{7,11},{8,4},{9,5},... | collective-permute-start | bytes 417800 | tf_op jit(solution)/shard_map/ppermute | solution.py:195
  30.8 0.7 convert_element_type.3.sharp
  31.5 0.0 copy-start
  31.5 1.2 %copy-done = bf16[2,1024,256]{2,1,0:T(8,128)(2,1)S(1)} copy-done((bf16[2,1024,256]{2,1,0:T(8,128)(2,1)S(1)}, bf16[2,1024,256]{2,1,0:T(8,128)(2,1)}, u32[]{:S(2)}) %copy-start) | copy-done | bytes 1048600
  32.7 1.2 %shard_map.60.m0 = bf16[16,1024]{1,0:T(8,128)(2,1)S(1)} custom-call(f32[2]{0:T(128)S(1)} %convert_element_type.3.sharp, bf16[2,1024,256]{2,1,0:T(8,128)(2,1)S(1)} %copy-done), custom_call_target="tpu_custom_call" | custom-call | flops 16777216 | bytes 1048576 | tf_op jit(solution)/shard_map/pallas_call | solution.py:215
  34.0 1.4 %collective-permute-start.5 = (bf16[16,1024]{1,0:T(8,128)(2,1)S(1)}, bf16[16,1024]{1,0:T(8,128)(2,1)S(1)}, u32[]{:S(2)}, u32[]{:S(2)}) collective-permute-start(bf16[16,1024]{1,0:T(8,128)(2,1)S(1)} %shard_map.60.m0), channel_id=1, source_target_pairs={{0,3},{1,2},{2,1},{3,0},{4,7},{5,6},{6,5},{7,4},{8,11},{9,10},{10,... | collective-permute-start | bytes 98312 | tf_op jit(solution)/shard_map/ppermute | solution.py:195
  35.4 0.5 collective-permute-start.4
  35.9 1.5 %collective-permute-done.5.m3 = bf16[16,1024]{1,0:T(8,128)(2,1)S(1)} collective-permute-done((bf16[16,1024]{1,0:T(8,128)(2,1)S(1)}, bf16[16,1024]{1,0:T(8,128)(2,1)S(1)}, u32[]{:S(2)}, u32[]{:S(2)}) %collective-permute-start.5) | collective-permute-done | bytes 32800 | tf_op jit(solution)/shard_map/ppermute | solution.py:195
  37.4 1.0 collective-permute-start.8
  38.4 0.9 collective-permute-done.4.m2
  39.3 0.0 collective-permute-start.3
  39.3 1.2 %collective-permute-done.3.m1 = bf16[16,1024]{1,0:T(8,128)(2,1)S(1)} collective-permute-done((bf16[16,1024]{1,0:T(8,128)(2,1)S(1)}, bf16[16,1024]{1,0:T(8,128)(2,1)S(1)}, u32[]{:S(2)}, u32[]{:S(2)}) %collective-permute-start.3) | collective-permute-done | bytes 32800 | tf_op jit(solution)/shard_map/ppermute | solution.py:195
  40.5 2.5 %collective-permute-start.6 = (bf16[272,256]{1,0:T(8,128)(2,1)S(1)}, bf16[272,256]{1,0:T(8,128)(2,1)S(1)}, u32[]{:S(2)}, u32[]{:S(2)}) collective-permute-start(bf16[272,256]{1,0:T(8,128)(2,1)S(1)} %get-tuple-element.9), channel_id=1, source_target_pairs={{0,4},{1,5},{2,6},{3,7},{4,0},{5,1},{6,2},{7,3},{8,12},{9,13},{10,... | collective-permute-start | bytes 417800 | tf_op jit(solution)/shard_map/ppermute | solution.py:195
  43.0 0.0 collective-permute-done.10.block.refs_3_
  43.0 0.0 collective-permute-done.c1
  43.0 0.0 collective-permute-done.2.c3
  43.0 0.0 copy-done.1
  43.0 3.0 %shard_map.64.refs_7_ = bf16[256,1024]{1,0:T(8,128)(2,1)S(1)} custom-call(bf16[272,256]{1,0:T(8,128)(2,1)S(1)} %collective-permute-done.10.block.refs_3_, bf16[2,1024,256]{2,1,0:T(8,128)(2,1)S(1)} %copy-done.1, bf16[2,1024,256]{2,1,0:T(8,128)(2,1)S(1)} %collective-permute-done.c1, bf16[2,1024,256]{2,1,0:T(8,128)(2,1)S(1)} %collective-permute-done.1.c2, ...), custom_call_target="tpu_custom_call" | custom-call | flops 1073741824 | bytes 4194304 | tf_op jit(solution)/shard_map/pallas_call | solution.py:229
  46.0 0.0 collective-permute-done.8.block.refs_2_
  46.0 3.0 %shard_map.63.refs_6_ = bf16[256,1024]{1,0:T(8,128)(2,1)S(1)} custom-call(bf16[272,256]{1,0:T(8,128)(2,1)S(1)} %collective-permute-done.8.block.refs_2_, bf16[2,1024,256]{2,1,0:T(8,128)(2,1)S(1)} %copy-done.1, bf16[2,1024,256]{2,1,0:T(8,128)(2,1)S(1)} %collective-permute-done.c1, bf16[2,1024,256]{2,1,0:T(8,128)(2,1)S(1)} %collective-permute-done.1.c2, ...), custom_call_target="tpu_custom_call" | custom-call | flops 1073741824 | bytes 4194304 | tf_op jit(solution)/shard_map/pallas_call | solution.py:229
  49.1 0.1 collective-permute-done.6.block.refs_1_
  49.1 3.0 %shard_map.62.refs_5_ = bf16[256,1024]{1,0:T(8,128)(2,1)S(1)} custom-call(bf16[272,256]{1,0:T(8,128)(2,1)S(1)} %collective-permute-done.6.block.refs_1_, bf16[2,1024,256]{2,1,0:T(8,128)(2,1)S(1)} %copy-done.1, bf16[2,1024,256]{2,1,0:T(8,128)(2,1)S(1)} %collective-permute-done.c1, bf16[2,1024,256]{2,1,0:T(8,128)(2,1)S(1)} %collective-permute-done.1.c2, ...), custom_call_target="tpu_custom_call" | custom-call | flops 1073741824 | bytes 4194304 | tf_op jit(solution)/shard_map/pallas_call | solution.py:229
  52.2 3.0 %shard_map.61.refs_0_.refs_4_ = bf16[256,1024]{1,0:T(8,128)(2,1)S(1)} custom-call(bf16[272,256]{1,0:T(8,128)(2,1)S(1)} %get-tuple-element.8.block.refs_0_, bf16[2,1024,256]{2,1,0:T(8,128)(2,1)S(1)} %copy-done.1, bf16[2,1024,256]{2,1,0:T(8,128)(2,1)S(1)} %collective-permute-done.c1, bf16[2,1024,256]{2,1,0:T(8,128)(2,1)S(1)} %collective-permute-done.1.c2, ...), custom_call_target="tpu_custom_call" | custom-call | flops 1073741824 | bytes 4194304 | tf_op jit(solution)/shard_map/pallas_call | solution.py:229
  55.2 2.7 %shard_map.67 = bf16[4,272,1024]{2,1,0:T(8,128)(2,1)S(1)} custom-call(bf16[272,256]{1,0:T(8,128)(2,1)S(1)} %get-tuple-element.8.block.refs_0_, bf16[272,256]{1,0:T(8,128)(2,1)S(1)} %collective-permute-done.6.block.refs_1_, bf16[272,256]{1,0:T(8,128)(2,1)S(1)} %collective-permute-done.8.block.refs_2_, ...), custom_call_target="tpu_custom_call" | custom-call | flops 2147483648 | bytes 2097152 | tf_op jit(solution)/shard_map/pallas_call | solution.py:239
  57.9 0.1 collective-permute-start.12
  58.0 2.9 %shard_map.66.keep = bf16[4,272,1024]{2,1,0:T(8,128)(2,1)S(1)} custom-call(bf16[272,256]{1,0:T(8,128)(2,1)S(1)} %get-tuple-element.8.block.refs_0_, bf16[272,256]{1,0:T(8,128)(2,1)S(1)} %collective-permute-done.6.block.refs_1_, bf16[272,256]{1,0:T(8,128)(2,1)S(1)} %collective-permute-done.8.block.refs_2_, ...), custom_call_target="tpu_custom_call" | custom-call | flops 2147483648 | bytes 2097152 | tf_op jit(solution)/shard_map/pallas_call | solution.py:239
  61.0 1.4 %collective-permute-done.12.got = bf16[4,272,1024]{2,1,0:T(8,128)(2,1)S(1)} collective-permute-done((bf16[4,272,1024]{2,1,0:T(8,128)(2,1)S(1)}, bf16[4,272,1024]{2,1,0:T(8,128)(2,1)S(1)}, u32[]{:S(2)}, u32[]{:S(2)}) %collective-permute-start.12) | collective-permute-done | bytes 2228256 | tf_op jit(solution)/shard_map/ppermute | solution.py:195
  62.4 0.3 shard_map.68
  62.7 1.1 collective-permute-start.13
  63.7 3.6 %collective-permute-start.7 = (bf16[256,1024]{1,0:T(8,128)(2,1)S(1)}, bf16[256,1024]{1,0:T(8,128)(2,1)S(1)}, u32[]{:S(2)}, u32[]{:S(2)}) collective-permute-start(bf16[256,1024]{1,0:T(8,128)(2,1)S(1)} %shard_map.62.refs_5_), channel_id=1, source_target_pairs={{0,4},{1,5},{2,6},{3,7},{4,0},{5,1},{6,2},{7,3},{8,12},{9,13},{10,... | collective-permute-start | bytes 1572872 | tf_op jit(solution)/shard_map/ppermute | solution.py:195
  67.3 0.0 collective-permute-start.9
  67.3 1.5 %collective-permute-start.11 = (bf16[256,1024]{1,0:T(8,128)(2,1)S(1)}, bf16[256,1024]{1,0:T(8,128)(2,1)S(1)}, u32[]{:S(2)}, u32[]{:S(2)}) collective-permute-start(bf16[256,1024]{1,0:T(8,128)(2,1)S(1)} %shard_map.64.refs_7_), channel_id=1, source_target_pairs={{0,12},{1,13},{2,14},{3,15},{4,8},{5,9},{6,10},{7,11},{8,4},{9,5},... | collective-permute-start | bytes 1572872 | tf_op jit(solution)/shard_map/ppermute | solution.py:195
  68.8 19.7 %collective-permute-done.7.refs_1_ = bf16[256,1024]{1,0:T(8,128)(2,1)S(1)} collective-permute-done((bf16[256,1024]{1,0:T(8,128)(2,1)S(1)}, bf16[256,1024]{1,0:T(8,128)(2,1)S(1)}, u32[]{:S(2)}, u32[]{:S(2)}) %collective-permute-start.7) | collective-permute-done | bytes 524320 | tf_op jit(solution)/shard_map/ppermute | solution.py:195
  88.5 13.7 %collective-permute-done.9.refs_2_ = bf16[256,1024]{1,0:T(8,128)(2,1)S(1)} collective-permute-done((bf16[256,1024]{1,0:T(8,128)(2,1)S(1)}, bf16[256,1024]{1,0:T(8,128)(2,1)S(1)}, u32[]{:S(2)}, u32[]{:S(2)}) %collective-permute-start.9) | collective-permute-done | bytes 524320 | tf_op jit(solution)/shard_map/ppermute | solution.py:195
  102.1 12.1 %collective-permute-done.11.refs_3_ = bf16[256,1024]{1,0:T(8,128)(2,1)S(1)} collective-permute-done((bf16[256,1024]{1,0:T(8,128)(2,1)S(1)}, bf16[256,1024]{1,0:T(8,128)(2,1)S(1)}, u32[]{:S(2)}, u32[]{:S(2)}) %collective-permute-start.11) | collective-permute-done | bytes 524320 | tf_op jit(solution)/shard_map/ppermute | solution.py:195
  114.2 2.3 %shard_map.65 = bf16[512,1024]{1,0:T(8,128)(2,1)} custom-call(s32[512,1]{1,0:T(8,128)S(1)} %get-tuple-element.7.slot, bf16[256,1024]{1,0:T(8,128)(2,1)S(1)} %shard_map.61.refs_0_.refs_4_, bf16[256,1024]{1,0:T(8,128)(2,1)S(1)} %collective-permute-done.7.refs_1_, bf16[256,1024]{1,0:T(8,128)(2,1)S(1)} %collective-permute-done.9.refs_2_, ...), custom_call_target="tpu_custom_call" | custom-call | flops 1073741824 | bytes 2097152 | tf_op jit(solution)/shard_map/pallas_call | solution.py:264
  116.5 0.0 collective-permute-done.13.far
  116.5 2.5 %shard_map.69 = f32[2,1024,256]{2,1,0:T(8,128)} custom-call(bf16[4,272,1024]{2,1,0:T(8,128)(2,1)S(1)} %shard_map.66.keep, bf16[4,272,1024]{2,1,0:T(8,128)(2,1)S(1)} %collective-permute-done.12.got, bf16[2,272,1024]{2,1,0:T(8,128)(2,1)S(1)} %collective-permute-done.13.far, bf16[2,1024,256]{2,1,0:T(8,128)(2,1)S(1)} %copy-done.1), custom_call_target="tpu_custom_call" | custom-call | flops 4194304 | bytes 8388608 | tf_op jit(solution)/shard_map/pallas_call | solution.py:257
Async XLA Ops:
  0.6 42.4 %copy-start.1 = (bf16[2,1024,256]{2,1,0:T(8,128)(2,1)S(1)}, bf16[2,1024,256]{2,1,0:T(8,128)(2,1)}, u32[]{:S(2)}) copy-start(bf16[2,1024,256]{2,1,0:T(8,128)(2,1)} %centres.3) | copy-start | bytes 3145732
  0.6 25.2 %collective-permute-start.1 = (bf16[2,1024,256]{2,1,0:T(8,128)(2,1)}, bf16[2,1024,256]{2,1,0:T(8,128)(2,1)S(1)}, u32[]{:S(2)}, u32[]{:S(2)}) collective-permute-start(bf16[2,1024,256]{2,1,0:T(8,128)(2,1)} %centres.3), channel_id=1, source_target_pairs={{0,2},{1,3},{2,0},{3,1},{4,6},{5,7},{6,4},{7,5},{8,10},{9,11},{10,... | collective-permute-start | bytes 3145736 | tf_op jit(solution)/shard_map/ppermute | solution.py:195
  2.2 40.8 %collective-permute-start = (bf16[2,1024,256]{2,1,0:T(8,128)(2,1)}, bf16[2,1024,256]{2,1,0:T(8,128)(2,1)S(1)}, u32[]{:S(2)}, u32[]{:S(2)}) collective-permute-start(bf16[2,1024,256]{2,1,0:T(8,128)(2,1)} %centres.3), channel_id=1, source_target_pairs={{0,1},{1,0},{2,3},{3,2},{4,5},{5,4},{6,7},{7,6},{8,9},{9,8},{10,11... | collective-permute-start | bytes 3145736 | tf_op jit(solution)/shard_map/ppermute | solution.py:195
  25.8 17.2 %collective-permute-start.2 = (bf16[2,1024,256]{2,1,0:T(8,128)(2,1)S(1)}, bf16[2,1024,256]{2,1,0:T(8,128)(2,1)}, u32[]{:S(2)}, u32[]{:S(2)}) collective-permute-start(bf16[2,1024,256]{2,1,0:T(8,128)(2,1)S(1)} %collective-permute-done.1.c2), channel_id=1, source_target_pairs={{0,1},{1,0},{2,3},{3,2},{4,5},{5,4},{6,7},{7,6},{8,9},{9,8},{10,11... | collective-permute-start | bytes 3145736 | tf_op jit(solution)/shard_map/ppermute | solution.py:195
  26.7 1.0 copy-start.2
  29.2 13.8 %collective-permute-start.10 = (bf16[272,256]{1,0:T(8,128)(2,1)S(1)}, bf16[272,256]{1,0:T(8,128)(2,1)S(1)}, u32[]{:S(2)}, u32[]{:S(2)}) collective-permute-start(bf16[272,256]{1,0:T(8,128)(2,1)S(1)} %get-tuple-element.11), channel_id=1, source_target_pairs={{0,12},{1,13},{2,14},{3,15},{4,8},{5,9},{6,10},{7,11},{8,4},{9,5},... | collective-permute-start | bytes 417800 | tf_op jit(solution)/shard_map/ppermute | solution.py:195
  31.5 1.2 %copy-start = (bf16[2,1024,256]{2,1,0:T(8,128)(2,1)S(1)}, bf16[2,1024,256]{2,1,0:T(8,128)(2,1)}, u32[]{:S(2)}) copy-start(bf16[2,1024,256]{2,1,0:T(8,128)(2,1)} %centres.3) | copy-start | bytes 3145732
  34.0 3.4 %collective-permute-start.5 = (bf16[16,1024]{1,0:T(8,128)(2,1)S(1)}, bf16[16,1024]{1,0:T(8,128)(2,1)S(1)}, u32[]{:S(2)}, u32[]{:S(2)}) collective-permute-start(bf16[16,1024]{1,0:T(8,128)(2,1)S(1)} %shard_map.60.m0), channel_id=1, source_target_pairs={{0,3},{1,2},{2,1},{3,0},{4,7},{5,6},{6,5},{7,4},{8,11},{9,10},{10,... | collective-permute-start | bytes 98312 | tf_op jit(solution)/shard_map/ppermute | solution.py:195
  35.4 3.9 %collective-permute-start.4 = (bf16[16,1024]{1,0:T(8,128)(2,1)S(1)}, bf16[16,1024]{1,0:T(8,128)(2,1)S(1)}, u32[]{:S(2)}, u32[]{:S(2)}) collective-permute-start(bf16[16,1024]{1,0:T(8,128)(2,1)S(1)} %shard_map.60.m0), channel_id=1, source_target_pairs={{0,2},{1,3},{2,0},{3,1},{4,6},{5,7},{6,4},{7,5},{8,10},{9,11},{10,... | collective-permute-start | bytes 98312 | tf_op jit(solution)/shard_map/ppermute | solution.py:195
  37.4 8.7 %collective-permute-start.8 = (bf16[272,256]{1,0:T(8,128)(2,1)S(1)}, bf16[272,256]{1,0:T(8,128)(2,1)S(1)}, u32[]{:S(2)}, u32[]{:S(2)}) collective-permute-start(bf16[272,256]{1,0:T(8,128)(2,1)S(1)} %get-tuple-element.10), channel_id=1, source_target_pairs={{0,8},{1,9},{2,10},{3,11},{4,12},{5,13},{6,14},{7,15},{8,0},{9,1},... | collective-permute-start | bytes 417800 | tf_op jit(solution)/shard_map/ppermute | solution.py:195
  39.3 1.2 %collective-permute-start.3 = (bf16[16,1024]{1,0:T(8,128)(2,1)S(1)}, bf16[16,1024]{1,0:T(8,128)(2,1)S(1)}, u32[]{:S(2)}, u32[]{:S(2)}) collective-permute-start(bf16[16,1024]{1,0:T(8,128)(2,1)S(1)} %shard_map.60.m0), channel_id=1, source_target_pairs={{0,1},{1,0},{2,3},{3,2},{4,5},{5,4},{6,7},{7,6},{8,9},{9,8},{10,11... | collective-permute-start | bytes 98312 | tf_op jit(solution)/shard_map/ppermute | solution.py:195
  40.5 8.6 %collective-permute-start.6 = (bf16[272,256]{1,0:T(8,128)(2,1)S(1)}, bf16[272,256]{1,0:T(8,128)(2,1)S(1)}, u32[]{:S(2)}, u32[]{:S(2)}) collective-permute-start(bf16[272,256]{1,0:T(8,128)(2,1)S(1)} %get-tuple-element.9), channel_id=1, source_target_pairs={{0,4},{1,5},{2,6},{3,7},{4,0},{5,1},{6,2},{7,3},{8,12},{9,13},{10,... | collective-permute-start | bytes 417800 | tf_op jit(solution)/shard_map/ppermute | solution.py:195
  57.9 4.4 %collective-permute-start.12 = (bf16[4,272,1024]{2,1,0:T(8,128)(2,1)S(1)}, bf16[4,272,1024]{2,1,0:T(8,128)(2,1)S(1)}, u32[]{:S(2)}, u32[]{:S(2)}) collective-permute-start(bf16[4,272,1024]{2,1,0:T(8,128)(2,1)S(1)} %shard_map.67), channel_id=1, source_target_pairs={{0,1},{1,0},{2,3},{3,2},{4,5},{5,4},{6,7},{7,6},{8,9},{9,8},{10,11... | collective-permute-start | bytes 6684680 | tf_op jit(solution)/shard_map/ppermute | solution.py:195
  62.7 53.8 %collective-permute-start.13 = (bf16[2,272,1024]{2,1,0:T(8,128)(2,1)S(1)}, bf16[2,272,1024]{2,1,0:T(8,128)(2,1)S(1)}, u32[]{:S(2)}, u32[]{:S(2)}) collective-permute-start(bf16[2,272,1024]{2,1,0:T(8,128)(2,1)S(1)} %shard_map.68), channel_id=1, source_target_pairs={{0,2},{1,3},{2,0},{3,1},{4,6},{5,7},{6,4},{7,5},{8,10},{9,11},{10,... | collective-permute-start | bytes 3342344 | tf_op jit(solution)/shard_map/ppermute | solution.py:195
  63.7 24.8 %collective-permute-start.7 = (bf16[256,1024]{1,0:T(8,128)(2,1)S(1)}, bf16[256,1024]{1,0:T(8,128)(2,1)S(1)}, u32[]{:S(2)}, u32[]{:S(2)}) collective-permute-start(bf16[256,1024]{1,0:T(8,128)(2,1)S(1)} %shard_map.62.refs_5_), channel_id=1, source_target_pairs={{0,4},{1,5},{2,6},{3,7},{4,0},{5,1},{6,2},{7,3},{8,12},{9,13},{10,... | collective-permute-start | bytes 1572872 | tf_op jit(solution)/shard_map/ppermute | solution.py:195
  67.3 34.8 %collective-permute-start.9 = (bf16[256,1024]{1,0:T(8,128)(2,1)S(1)}, bf16[256,1024]{1,0:T(8,128)(2,1)S(1)}, u32[]{:S(2)}, u32[]{:S(2)}) collective-permute-start(bf16[256,1024]{1,0:T(8,128)(2,1)S(1)} %shard_map.63.refs_6_), channel_id=1, source_target_pairs={{0,8},{1,9},{2,10},{3,11},{4,12},{5,13},{6,14},{7,15},{8,0},{9,1},... | collective-permute-start | bytes 1572872 | tf_op jit(solution)/shard_map/ppermute | solution.py:195
  67.3 46.9 %collective-permute-start.11 = (bf16[256,1024]{1,0:T(8,128)(2,1)S(1)}, bf16[256,1024]{1,0:T(8,128)(2,1)S(1)}, u32[]{:S(2)}, u32[]{:S(2)}) collective-permute-start(bf16[256,1024]{1,0:T(8,128)(2,1)S(1)} %shard_map.64.refs_7_), channel_id=1, source_target_pairs={{0,12},{1,13},{2,14},{3,15},{4,8},{5,9},{6,10},{7,11},{8,4},{9,5},... | collective-permute-start | bytes 1572872 | tf_op jit(solution)/shard_map/ppermute | solution.py:195

commit v2 on v1

v2 whole, which is shorter than its diff:
```python
import functools

import jax
import jax.numpy as jnp
from jax import lax
from jax.experimental import pallas as pl
from jax.experimental.pallas import tpu as pltpu
from jax.sharding import PartitionSpec as P

GRP = 4
META = 16
SCALE = 5
BF = jnp.bfloat16
F32 = jnp.float32
VMEM = pl.BlockSpec(memory_space=pltpu.VMEM)
SMEM = pl.BlockSpec(memory_space=pltpu.SMEM)


def call(body, out_shape, n_in, flops, nbytes, in_specs=None, scratch=()):
    many = isinstance(out_shape, (list, tuple))
    return pl.pallas_call(
        body,
        out_shape=out_shape,
        in_specs=in_specs or [VMEM] * n_in,
        out_specs=[VMEM] * len(out_shape) if many else VMEM,
        scratch_shapes=list(scratch),
        compiler_params=pltpu.CompilerParams(vmem_limit_bytes=40 * 1024 * 1024),
        cost_estimate=pl.CostEstimate(flops=flops, bytes_accessed=nbytes, transcendentals=0),
    )


def three(value):
    first = value.astype(BF)
    rest = value - first.astype(F32)
    second = rest.astype(BF)
    third = (rest - second.astype(F32)).astype(BF)
    return first, second, third


def cluster_lanes(shape):
    lane = lax.broadcasted_iota(jnp.int32, shape, 1)
    return jnp.where(lane < 128, lane >> 4, lane - 128)


def pack_body(groups, rows, here, labels, codes, *outs):
    frames, width = codes.shape
    group, place = here[0] // GRP, here[0] % GRP
    kr = jnp.broadcast_to(labels[...], (8, frames)) ^ (group * 8 + place * 2)
    kc = kr.T[:, 0:1]
    kr = kr[0:1, :]
    lane = lax.broadcasted_iota(jnp.int32, (1, frames), 1)
    sub = lax.broadcasted_iota(jnp.int32, (frames, 1), 0)
    ur, uc = kr * frames + lane, kc * frames + sub
    gr = kr >> 3
    base_r = gr * (8 * frames)
    rank = jnp.sum(((uc < ur) & (uc >= base_r)).astype(jnp.int32), axis=0, keepdims=True)
    slot = gr * rows + rank
    rounded = codes[...].astype(BF)
    target = lax.broadcasted_iota(jnp.int32, (rows, frames), 0)
    cluster = cluster_lanes((1, width))
    row = lax.broadcasted_iota(jnp.int32, (META, width), 0)
    for k in range(groups):
        pick = (slot == target + k * rows).astype(F32).astype(BF)
        outs[k][:rows, :] = jnp.dot(pick, rounded, preferred_element_type=F32).astype(BF)
        inside = kc >= 8 * k
        first = jnp.sum((inside & (kc < 8 * k + cluster)).astype(F32), axis=0, keepdims=True)
        last = jnp.sum((inside & (kc < 8 * k + cluster + 1)).astype(F32), axis=0, keepdims=True)
        bounds = jnp.where(row == 0, first, jnp.where(row == 1, last, 0.0))
        outs[k][rows:, :] = bounds.astype(BF)
    gc = kc >> 3
    base_c = gc * (8 * frames)
    rank_c = jnp.sum(((ur < uc) & (ur >= base_c)).astype(jnp.int32), axis=1, keepdims=True)
    outs[groups][...] = gc * rows + rank_c


def share_body(c, sharp, centres, out):
    width = out.shape[1]
    fine = centres.shape[1]
    row = lax.broadcasted_iota(jnp.int32, (8, width), 0)
    ones = jnp.ones((8, width), BF)
    dims = (((1,), (1,)), ((), ()))
    values = centres[c]
    out[:fine, :] = values
    wide = values.astype(F32)
    square = wide * wide
    high = square.astype(BF)
    low = (square - high.astype(F32)).astype(BF)
    norm = lax.dot_general(ones, high, dims, preferred_element_type=F32)
    norm = norm + lax.dot_general(ones, low, dims, preferred_element_type=F32)
    terms = [t.astype(F32) for t in three(-0.5 * norm)]
    tiles = []
    for q in range(fine // width):
        tile = jnp.where(row == 3, sharp[c : c + 1, 0:1].astype(F32), 0.0)
        for t in range(3):
            tile = jnp.where(row == t, terms[t][:, q * width : (q + 1) * width], tile)
        tiles.append(tile)
    out[fine:, :] = jnp.concatenate(tiles, axis=0).astype(BF)


def member_lanes(block, rows):
    bounds = block[rows:, :].astype(F32)
    row = lax.broadcasted_iota(jnp.int32, (rows, block.shape[1]), 0).astype(F32)
    return ((row >= bounds[0:1, :]) & (row < bounds[1:2, :])).astype(F32)


def mass_rows(row, mass):
    terms = three(mass)
    total = jnp.zeros(row.shape, F32)
    for t in range(3):
        total = jnp.where(row == t, terms[t].astype(F32), total)
    return total.astype(BF)


def soft_rows(block, rows, first, refs, fine):
    member = member_lanes(block, rows).astype(BF)
    codes = block[:rows, :]
    count = len(refs)
    width = codes.shape[1]
    pick = member[:, 16 * first : 16 * (first + count)]
    part = lax.broadcasted_iota(jnp.int32, pick.shape, 1) & 15
    zero = jnp.zeros_like(pick)
    low = jnp.where(part < 3, pick, zero)
    high = jnp.where((part >= 8) & (part < 11), pick, zero)
    columns = []
    for q in range(0, fine // width, 2):
        start = fine + 8 * q
        table = jnp.concatenate([ref[start : start + 16, :] for ref in refs], axis=0)
        columns += [jnp.dot(p, table, preferred_element_type=F32) for p in (low, high)]
    logits = jnp.concatenate(columns, axis=1)
    for n, ref in enumerate(refs):
        r = first + n
        chosen = codes * member[:, 128 + r : 129 + r]
        logits = logits + lax.dot_general(
            chosen, ref[:fine, :], (((1,), (1,)), ((), ())), preferred_element_type=F32
        )
    scale = jnp.dot(jnp.where(part == 3, pick, zero), table[:, :128], preferred_element_type=F32)
    logits = logits * scale[:, 0:1]
    shifted = jnp.exp(logits - jnp.max(logits, axis=1, keepdims=True))
    unit = float(fine) / jnp.sum(shifted, axis=1, keepdims=True)
    return (shifted * unit).astype(BF)


def soft_body(rows, block, *refs):
    out = refs[-1]
    out[...] = soft_rows(block, rows, 0, refs[:-1], out.shape[1])


def other_body(groups, rows, blocks, *refs):
    out = refs[-1]
    step = rows + META
    for k in range(groups):
        block = blocks[k * step : (k + 1) * step, :]
        out[k * rows : (k + 1) * rows, :] = soft_rows(block, rows, 4, refs[:-1], out.shape[1])


def sums(groups, rows, which, refs):
    blocks, softs = refs[:groups], refs[groups : 2 * groups]
    others, soft = refs[2 * groups], refs[2 * groups + 1]
    dims = (((0,), (0,)), ((), ()))
    step = rows + META
    terms = []
    for k in range(groups):
        block = blocks[k][...]
        terms.append((block, member_lanes(block, rows).astype(BF), softs[k][...], 0))
    for k in range(groups):
        block = others[k * step : (k + 1) * step, :]
        values = soft[k * rows : (k + 1) * rows, :]
        terms.append((block, member_lanes(block, rows).astype(BF), values, 4))
    mass = 0.0
    for _, member, values, first in terms:
        picked = member[:, 128 + first : 132 + first]
        picked = jnp.concatenate([picked, jnp.zeros((rows, 124), BF)], axis=1)
        mass = mass + lax.dot_general(picked, values, dims, preferred_element_type=F32)
    for r in which:
        total = 0.0
        for block, member, values, first in terms:
            chosen = block[:rows, :] * member[:, 128 + first + r : 129 + first + r]
            total = total + lax.dot_general(chosen, values, dims, preferred_element_type=F32)
        yield total, mass[r : r + 1, :]


def give_body(groups, rows, *refs):
    out = refs[-1]
    fine, width = out.shape[1] - META, out.shape[2]
    for n, (total, mass) in enumerate(sums(groups, rows, (2, 3), refs)):
        out[n, :fine, :] = total.astype(BF).T
        pieces = [mass[:, q * width : (q + 1) * width] for q in range(fine // width)]
        terms = [t.astype(F32) for t in three(jnp.concatenate(pieces, axis=0))]
        rest = jnp.zeros((META - 3 * len(pieces), width), F32)
        out[n, fine:, :] = jnp.concatenate(terms + [rest], axis=0).astype(BF)


def mine_body(groups, rows, *refs):
    centres, out, mass_out = refs[-3:]
    fine, width = out.shape[1:]
    for n, (total, mass) in enumerate(sums(groups, rows, (0, 1), refs)):
        out[n] = total.T + centres[n].astype(F32)
        for q in range(fine // width):
            mass_out[n, q : q + 1, :] = mass[:, q * width : (q + 1) * width] + 1.0


def finish_body(mine, mass, got, out):
    fine, width = out.shape[1:]
    count = fine // width
    for n in range(out.shape[0]):
        tail = got[n, fine:, :].astype(F32)
        total = mass[n]
        for t in range(3):
            total = total + tail[t * count : (t + 1) * count, :]
        inverse = 1.0 / total
        for q in range(count):
            column = jnp.broadcast_to(inverse[q : q + 1, :], (8, width)).T[:, 0:1]
            span = slice(q * width, (q + 1) * width)
            out[n, span, :] = (mine[n, span, :] + got[n, span, :].astype(F32)) * column


def unpack_body(groups, rows, slot, *refs):
    frames = slot.shape[0]
    out = refs[groups]
    lane = lax.broadcasted_iota(jnp.int32, (frames, rows), 1)
    total = 0.0
    for k in range(groups):
        pick = (slot[...] == lane + k * rows).astype(F32).astype(BF)
        total = total + jnp.dot(pick, refs[k][...], preferred_element_type=F32)
    out[...] = total.astype(BF)


def shards(codes, labels, centroids, sharpness):
    route = lax.axis_size("route")
    frames, width = codes.shape
    per_device, fine, _ = centroids.shape
    groups = route // GRP
    rows = GRP * max(8, 2 * frames // route)
    here = lax.axis_index("route").astype(jnp.int32).reshape(1)

    def swap(x, mask):
        return lax.ppermute(x, "route", [(r, r ^ mask) for r in range(route)])

    sharp = sharpness.reshape(per_device, 1)
    own, far = [], []
    for c in range(per_device):
        own.append(
            call(
                functools.partial(share_body, c),
                jax.ShapeDtypeStruct((fine + 8 * (fine // width), width), BF),
                2,
                SCALE * 4 * 8 * fine * width,
                SCALE * fine * width * 4,
            )(sharp, centroids)
        )
        far.append(swap(own[c], 2))
    here, _ = lax.optimization_barrier((here, own[0]))
    block_shape = jax.ShapeDtypeStruct((rows + META, width), BF)
    *send, slot = call(
        functools.partial(pack_body, groups, rows),
        [block_shape] * groups + [jax.ShapeDtypeStruct((frames, 1), jnp.int32)],
        3,
        SCALE * 2 * groups * rows * frames * width,
        SCALE * frames * width * 8,
        in_specs=[SMEM, VMEM, VMEM],
    )(here, labels.reshape(1, frames), codes)
    order = sorted(range(1, groups), key=lambda k: (-(k.bit_length()), k))
    *send, _ = lax.optimization_barrier((*send, own[1]))
    blocks = {0: send[0]}
    for k in order:
        blocks[k] = swap(send[k], GRP * k)
    arrived = [blocks[k] for k in order]
    near = [swap(lax.optimization_barrier((x, *arrived))[0], 1) for x in own]
    last = [swap(lax.optimization_barrier((x, *arrived))[0], 1) for x in far]

    work = 2 * rows * fine * width * 2 * GRP
    soft, back = {}, {}
    for k in order + [0]:
        soft[k] = call(
            functools.partial(soft_body, rows),
            jax.ShapeDtypeStruct((rows, fine), BF),
            9,
            SCALE * work,
            SCALE * GRP * per_device * fine * width * 2,
        )(blocks[k], *own, *near, *far, *last)
        back[k] = swap(soft[k], GRP * k) if k else soft[k]

    others = jnp.concatenate([blocks[k] for k in range(groups)], axis=0)
    others, _ = lax.optimization_barrier((others, far[1]))
    others = swap(others, 2)
    others, _ = lax.optimization_barrier((others, soft[0]))
    other_soft = call(
        functools.partial(other_body, groups, rows),
        jax.ShapeDtypeStruct((groups * rows, fine), BF),
        5,
        SCALE * 2 * groups * work,
        SCALE * groups * rows * fine * 2,
    )(others, *own, *near)
    parts = [blocks[k] for k in range(groups)] + [soft[k] for k in range(groups)]
    parts += [others, other_soft]
    work = 4 * 2 * groups * rows * fine * width
    got = swap(
        call(
            functools.partial(give_body, groups, rows),
            jax.ShapeDtypeStruct((per_device, fine + META, width), BF),
            len(parts),
            SCALE * work,
            SCALE * groups * rows * fine * 4,
        )(*parts),
        1,
    )
    mine, mass = call(
        functools.partial(mine_body, groups, rows),
        [
            jax.ShapeDtypeStruct(centroids.shape, F32),
            jax.ShapeDtypeStruct((per_device, fine // width, width), F32),
        ],
        len(parts) + 1,
        SCALE * work,
        SCALE * groups * rows * fine * 4,
    )(*parts, centroids)
    new_centroids = call(
        finish_body,
        jax.ShapeDtypeStruct(centroids.shape, F32),
        3,
        4 * per_device * fine * width,
        per_device * fine * width * 10,
    )(mine, mass, got)
    soft_labels = call(
        functools.partial(unpack_body, groups, rows),
        jax.ShapeDtypeStruct((frames, fine), BF),
        1 + groups,
        SCALE * 4 * frames * groups * rows * fine,
        groups * rows * fine * 2,
    )(slot, *[back[k] for k in range(groups)])
    return soft_labels, new_centroids


def solution(mesh):
    placed = (
        P(("parts", "route"), None),
        P(("parts", "route")),
        P(("parts", "route"), None, None),
        P(("parts", "route")),
    )
    return jax.shard_map(
        shards,
        mesh=mesh,
        in_specs=placed,
        out_specs=(P(("parts", "route"), None), P(("parts", "route"), None, None)),
        check_vma=False,
    )
```

time: 119 us -> 87.7 us (0.74)
  waiting for transfers between devices: 74 us -> 48.3 us
  starting transfers between devices: 14.9 us -> 12.5 us
  Pallas kernels: 25.5 us -> 23.9 us
  other arithmetic: 1.36 us -> 0.04 us
    ppermute x14, waiting for transfers between devices: 74 us -> 48.3 us  [swap(): return lax.ppermute(x, 'route', [(r, r ^ mask) for r in range(route)])]
    pallas_call x4, Pallas kernels: 12.1 us -> 6.96 us  [shards(): call(functools.partial(soft_body, rows), jax.ShapeDtypeStruct((rows, fine...]
    pallas_call x5 -> x6, Pallas kernels: 9.73 us -> 13.1 us  [the longest x1 3.73 us: shards(): call(functools.partial(other_body, groups, rows), jax.ShapeDtypeStruct((g...]
    ppermute x14, starting transfers between devices: 14.9 us -> 12.5 us  [swap(): return lax.ppermute(x, 'route', [(r, r ^ mask) for r in range(route)])]
  transfers between devices with their start and end apart: 14 -> 14, of which waited for: 9 -> 7; matrix products, arithmetic and copies ran while one was open for 1% -> 0% of each run, Pallas kernels for 12% -> 24%
where the time goes in v2:
time: 87.7 us; the launch traced here: 87.5 us
  waiting for transfers between devices  48.3 us (55%)
  Pallas kernels  23.9 us (27%)
  starting transfers between devices  12.5 us (14%)
  local copies, waits for them, and re-layouts  2 us (2%)
    ppermute x14, waiting for transfers between devices, swap(): return lax.ppermute(x, 'route', [(r, r ^ mask) for r in range(route)])  48.3 us
    ppermute x14, starting transfers between devices, swap(): return lax.ppermute(x, 'route', [(r, r ^ mask) for r in range(route)])  12.5 us
    pallas_call x4, Pallas kernels, shards(): call(functools.partial(soft_body, rows), jax.ShapeDtypeStruct((rows, fine...  6.96 us
    pallas_call x1, Pallas kernels, shards(): call(functools.partial(other_body, groups, rows), jax.ShapeDtypeStruct((g...  3.73 us
    pallas_call x1, Pallas kernels, shards(): call(functools.partial(give_body, groups, rows), jax.ShapeDtypeStruct((pe...  3.23 us
    pallas_call x1, Pallas kernels, shards(): call(functools.partial(mine_body, groups, rows), [jax.ShapeDtypeStruct(ce...  3.23 us
    pallas_call x1, Pallas kernels, shards(): call(functools.partial(unpack_body, groups, rows), jax.ShapeDtypeStruct((...  2.26 us
    pallas_call x1, Pallas kernels, shards(): call(finish_body, jax.ShapeDtypeStruct(centroids.shape, F32), 3, 4 * per_...  2.02 us
  transfers between devices with their start and end apart: 14, of which 7 were waited for; matrix products, arithmetic and copies ran while one was open for 0% of the time, Pallas kernels for 24%

profile of v2, /device:TPU:8, one launch (start us, length us, event | category | flops | bytes accessed | tf_op | source)
XLA Modules:
  0.0 87.5 jit_solution(3490385525693721751)
XLA Ops:
  0.6 0.8 copy.6.sharp
  1.4 1.2 %copy-done = bf16[2,1024,256]{2,1,0:T(8,128)(2,1)S(1)} copy-done((bf16[2,1024,256]{2,1,0:T(8,128)(2,1)S(1)}, bf16[2,1024,256]{2,1,0:T(8,128)(2,1)}, u32[]{:S(2)}) %copy-start) | copy-done | bytes 1048600
  2.6 0.4 shard_map.59.refs_0_
  3.1 0.0 copy-start.2
  3.1 0.0 copy-start.3
  3.1 1.6 %collective-permute-start.5 = (bf16[1056,256]{1,0:T(8,128)(2,1)S(1)}, bf16[1056,256]{1,0:T(8,128)(2,1)S(1)}, u32[]{:S(2)}, u32[]{:S(2)}) collective-permute-start(bf16[1056,256]{1,0:T(8,128)(2,1)S(1)} %shard_map.59.refs_0_), channel_id=1, source_target_pairs={{0,2},{1,3},{2,0},{3,1},{4,6},{5,7},{6,4},{7,5},{8,10},{9,11},{10,... | collective-permute-start | bytes 1622024 | tf_op jit(solution)/shard_map/ppermute | solution.py:237
  4.7 0.4 shard_map.61.refs_1_
  5.1 0.6 collective-permute-start.6
  5.7 0.0 copy-done.2
  5.7 0.0 copy-done.3
  5.7 1.6 %shard_map.60 = (bf16[272,256]{1,0:T(8,128)(2,1)S(1)}, bf16[272,256]{1,0:T(8,128)(2,1)S(1)}, bf16[272,256]{1,0:T(8,128)(2,1)S(1)}, bf16[272,256]{1,0:T(8,128)(2,1)S(1)}, s32[512,1]{1,0:T(8,128)S(1)}) custom-call(s32[1]{0:T(128)} %bitcast.here, s32[1,512]{1,0:T(1,128)S(1)} %bitcast.3, f32[512,256]{1,0:T(8,128)S(1)} %copy-done.2), custom_call_target="tpu_custom_call" | custom-call | flops 1342177280 | bytes 5242880 | tf_op jit(solution)/shard_map/pallas_call | solution.py:254
  7.3 2.7 %collective-permute-start = (bf16[272,256]{1,0:T(8,128)(2,1)S(1)}, bf16[272,256]{1,0:T(8,128)(2,1)S(1)}, u32[]{:S(2)}, u32[]{:S(2)}) collective-permute-start(bf16[272,256]{1,0:T(8,128)(2,1)S(1)} %get-tuple-element.27), channel_id=1, source_target_pairs={{0,8},{1,9},{2,10},{3,11},{4,12},{5,13},{6,14},{7,15},{8,0},{9,1},... | collective-permute-start | bytes 417800 | tf_op jit(solution)/shard_map/ppermute | solution.py:237
  9.9 0.0 collective-permute-start.1
  9.9 1.8 %collective-permute-start.2 = (bf16[272,256]{1,0:T(8,128)(2,1)S(1)}, bf16[272,256]{1,0:T(8,128)(2,1)S(1)}, u32[]{:S(2)}, u32[]{:S(2)}) collective-permute-start(bf16[272,256]{1,0:T(8,128)(2,1)S(1)} %get-tuple-element.29), channel_id=1, source_target_pairs={{0,4},{1,5},{2,6},{3,7},{4,0},{5,1},{6,2},{7,3},{8,12},{9,13},{10,... | collective-permute-start | bytes 417800 | tf_op jit(solution)/shard_map/ppermute | solution.py:237
  11.7 6.5 %collective-permute-done.block.refs_2_ = bf16[272,256]{1,0:T(8,128)(2,1)S(1)} collective-permute-done((bf16[272,256]{1,0:T(8,128)(2,1)S(1)}, bf16[272,256]{1,0:T(8,128)(2,1)S(1)}, u32[]{:S(2)}, u32[]{:S(2)}) %collective-permute-start) | collective-permute-done | bytes 139296 | tf_op jit(solution)/shard_map/ppermute | solution.py:237
  18.2 2.9 %collective-permute-done.1.block.refs_3_ = bf16[272,256]{1,0:T(8,128)(2,1)S(1)} collective-permute-done((bf16[272,256]{1,0:T(8,128)(2,1)S(1)}, bf16[272,256]{1,0:T(8,128)(2,1)S(1)}, u32[]{:S(2)}, u32[]{:S(2)}) %collective-permute-start.1) | collective-permute-done | bytes 139296 | tf_op jit(solution)/shard_map/ppermute | solution.py:237
  21.1 0.0 collective-permute-done.2.block.refs_1_
  21.1 0.0 collective-permute-start.3
  21.1 0.5 collective-permute-start.4
  21.6 0.0 collective-permute-done.5.refs_4_
  21.6 0.0 collective-permute-start.7
  21.7 7.1 %collective-permute-done.6.refs_5_ = bf16[1056,256]{1,0:T(8,128)(2,1)S(1)} collective-permute-done((bf16[1056,256]{1,0:T(8,128)(2,1)S(1)}, bf16[1056,256]{1,0:T(8,128)(2,1)S(1)}, u32[]{:S(2)}, u32[]{:S(2)}) %collective-permute-start.6) | collective-permute-done | bytes 540704 | tf_op jit(solution)/shard_map/ppermute | solution.py:237
  28.8 0.0 collective-permute-start.8
  28.8 1.6 %collective-permute-start.12 = (bf16[1088,256]{1,0:T(8,128)(2,1)S(1)}, bf16[1088,256]{1,0:T(8,128)(2,1)S(1)}, u32[]{:S(2)}, u32[]{:S(2)}) collective-permute-start(bf16[1088,256]{1,0:T(8,128)(2,1)S(1)} %pad_maximum_fusion), channel_id=1, source_target_pairs={{0,2},{1,3},{2,0},{3,1},{4,6},{5,7},{6,4},{7,5},{8,10},{9,11},{10,... | collective-permute-start | bytes 1671176 | tf_op jit(solution)/shard_map/ppermute | solution.py:237
  30.4 0.0 collective-permute-done.3.refs_2_
  30.4 0.0 collective-permute-done.4.refs_3_
  30.4 0.0 collective-permute-done.7.refs_6_
  30.4 0.3 collective-permute-done.8.refs_7_
  30.7 1.7 %shard_map.63.refs_5_ = bf16[256,1024]{1,0:T(8,128)(2,1)S(1)} custom-call(bf16[272,256]{1,0:T(8,128)(2,1)S(1)} %collective-permute-done.2.block.refs_1_, bf16[1056,256]{1,0:T(8,128)(2,1)S(1)} %shard_map.59.refs_0_, bf16[1056,256]{1,0:T(8,128)(2,1)S(1)} %shard_map.61.refs_1_, bf16[1056,256]{1,0:T(8,128)(2,1)S(1)} %collective-permute-done.3.refs_2_, ...), custom_call_target="tpu_custom_call" | custom-call | flops 5368709120 | bytes 20971520 | tf_op jit(solution)/shard_map/pallas_call | solution.py:274
  32.4 0.3 collective-permute-start.9
  32.7 1.7 %shard_map.64.refs_6_ = bf16[256,1024]{1,0:T(8,128)(2,1)S(1)} custom-call(bf16[272,256]{1,0:T(8,128)(2,1)S(1)} %collective-permute-done.block.refs_2_, bf16[1056,256]{1,0:T(8,128)(2,1)S(1)} %shard_map.59.refs_0_, bf16[1056,256]{1,0:T(8,128)(2,1)S(1)} %shard_map.61.refs_1_, bf16[1056,256]{1,0:T(8,128)(2,1)S(1)} %collective-permute-done.3.refs_2_, ...), custom_call_target="tpu_custom_call" | custom-call | flops 5368709120 | bytes 20971520 | tf_op jit(solution)/shard_map/pallas_call | solution.py:274
  34.5 2.9 %collective-permute-start.10 = (bf16[256,1024]{1,0:T(8,128)(2,1)S(1)}, bf16[256,1024]{1,0:T(8,128)(2,1)S(1)}, u32[]{:S(2)}, u32[]{:S(2)}) collective-permute-start(bf16[256,1024]{1,0:T(8,128)(2,1)S(1)} %shard_map.64.refs_6_), channel_id=1, source_target_pairs={{0,8},{1,9},{2,10},{3,11},{4,12},{5,13},{6,14},{7,15},{8,0},{9,1},... | collective-permute-start | bytes 1572872 | tf_op jit(solution)/shard_map/ppermute | solution.py:237
  37.4 1.7 %shard_map.65.refs_7_ = bf16[256,1024]{1,0:T(8,128)(2,1)S(1)} custom-call(bf16[272,256]{1,0:T(8,128)(2,1)S(1)} %collective-permute-done.1.block.refs_3_, bf16[1056,256]{1,0:T(8,128)(2,1)S(1)} %shard_map.59.refs_0_, bf16[1056,256]{1,0:T(8,128)(2,1)S(1)} %shard_map.61.refs_1_, bf16[1056,256]{1,0:T(8,128)(2,1)S(1)} %collective-permute-done.3.refs_2_, ...), custom_call_target="tpu_custom_call" | custom-call | flops 5368709120 | bytes 20971520 | tf_op jit(solution)/shard_map/pallas_call | solution.py:274
  39.1 0.5 collective-permute-start.11
  39.6 1.7 %shard_map.62.refs_0_.refs_4_ = bf16[256,1024]{1,0:T(8,128)(2,1)S(1)} custom-call(bf16[272,256]{1,0:T(8,128)(2,1)S(1)} %get-tuple-element.26.block.refs_0_, bf16[1056,256]{1,0:T(8,128)(2,1)S(1)} %shard_map.59.refs_0_, bf16[1056,256]{1,0:T(8,128)(2,1)S(1)} %shard_map.61.refs_1_, bf16[1056,256]{1,0:T(8,128)(2,1)S(1)} %collective-permute-done.3.refs_2_, ...), custom_call_target="tpu_custom_call" | custom-call | flops 5368709120 | bytes 20971520 | tf_op jit(solution)/shard_map/pallas_call | solution.py:274
  41.4 2.5 %collective-permute-done.12.blocks.refs_8_ = bf16[1088,256]{1,0:T(8,128)(2,1)S(1)} collective-permute-done((bf16[1088,256]{1,0:T(8,128)(2,1)S(1)}, bf16[1088,256]{1,0:T(8,128)(2,1)S(1)}, u32[]{:S(2)}, u32[]{:S(2)}) %collective-permute-start.12) | collective-permute-done | bytes 557088 | tf_op jit(solution)/shard_map/ppermute | solution.py:237
  43.9 3.7 %shard_map.67.refs_9_ = bf16[1024,1024]{1,0:T(8,128)(2,1)S(1)} custom-call(bf16[1088,256]{1,0:T(8,128)(2,1)S(1)} %collective-permute-done.12.blocks.refs_8_, bf16[1056,256]{1,0:T(8,128)(2,1)S(1)} %shard_map.59.refs_0_, bf16[1056,256]{1,0:T(8,128)(2,1)S(1)} %shard_map.61.refs_1_, bf16[1056,256]{1,0:T(8,128)(2,1)S(1)} %collective-permute-done.3.refs_2_, ...), custom_call_target="tpu_custom_call" | custom-call | flops 42949672960 | bytes 10485760 | tf_op jit(solution)/shard_map/pallas_call | solution.py:287
  47.6 0.0 copy-start.1
  47.6 3.2 %shard_map.69 = bf16[2,1040,256]{2,1,0:T(8,128)(2,1)S(1)} custom-call(bf16[272,256]{1,0:T(8,128)(2,1)S(1)} %get-tuple-element.26.block.refs_0_, bf16[272,256]{1,0:T(8,128)(2,1)S(1)} %collective-permute-done.2.block.refs_1_, bf16[272,256]{1,0:T(8,128)(2,1)S(1)} %collective-permute-done.block.refs_2_, ...), custom_call_target="tpu_custom_call" | custom-call | flops 10737418240 | bytes 20971520 | tf_op jit(solution)/shard_map/pallas_call | solution.py:298
  50.9 0.1 collective-permute-start.13
  51.0 0.0 copy-done.1
  51.0 3.2 %shard_map.68 = (f32[2,1024,256]{2,1,0:T(8,128)S(1)}, f32[2,4,256]{2,1,0:T(4,128)S(1)}) custom-call(bf16[272,256]{1,0:T(8,128)(2,1)S(1)} %get-tuple-element.26.block.refs_0_, bf16[272,256]{1,0:T(8,128)(2,1)S(1)} %collective-permute-done.2.block.refs_1_, bf16[272,256]{1,0:T(8,128)(2,1)S(1)} %collective-permute-done.block.refs_2_, ...), custom_call_target="tpu_custom_call" | custom-call | flops 10737418240 | bytes 20971520 | tf_op jit(solution)/shard_map/pallas_call | solution.py:307
  54.2 0.0 collective-permute-done.9.refs_1_
  54.2 17.9 %collective-permute-done.10.refs_2_ = bf16[256,1024]{1,0:T(8,128)(2,1)S(1)} collective-permute-done((bf16[256,1024]{1,0:T(8,128)(2,1)S(1)}, bf16[256,1024]{1,0:T(8,128)(2,1)S(1)}, u32[]{:S(2)}, u32[]{:S(2)}) %collective-permute-start.10) | collective-permute-done | bytes 524320 | tf_op jit(solution)/shard_map/ppermute | solution.py:237
  72.2 11.1 %collective-permute-done.11.refs_3_ = bf16[256,1024]{1,0:T(8,128)(2,1)S(1)} collective-permute-done((bf16[256,1024]{1,0:T(8,128)(2,1)S(1)}, bf16[256,1024]{1,0:T(8,128)(2,1)S(1)}, u32[]{:S(2)}, u32[]{:S(2)}) %collective-permute-start.11) | collective-permute-done | bytes 524320 | tf_op jit(solution)/shard_map/ppermute | solution.py:237
  83.2 2.3 %shard_map.66 = bf16[512,1024]{1,0:T(8,128)(2,1)} custom-call(s32[512,1]{1,0:T(8,128)S(1)} %get-tuple-element.21.slot, bf16[256,1024]{1,0:T(8,128)(2,1)S(1)} %shard_map.62.refs_0_.refs_4_, bf16[256,1024]{1,0:T(8,128)(2,1)S(1)} %collective-permute-done.9.refs_1_, bf16[256,1024]{1,0:T(8,128)(2,1)S(1)} %collective-permute-done.10.refs_2_, ...), custom_call_target="tpu_custom_call" | custom-call | flops 10737418240 | bytes 2097152 | tf_op jit(solution)/shard_map/pallas_call | solution.py:324
  85.5 0.0 collective-permute-done.13.got
  85.5 2.0 %shard_map.70 = f32[2,1024,256]{2,1,0:T(8,128)} custom-call(f32[2,1024,256]{2,1,0:T(8,128)S(1)} %get-tuple-element.36.mine, f32[2,4,256]{2,1,0:T(4,128)S(1)} %get-tuple-element.37.mass, bf16[2,1040,256]{2,1,0:T(8,128)(2,1)S(1)} %collective-permute-done.13.got), custom_call_target="tpu_custom_call" | custom-call | flops 2097152 | bytes 5242880 | tf_op jit(solution)/shard_map/pallas_call | solution.py:317
  (2 shorter events, 0.0 us)
Async XLA Ops:
  1.4 1.2 %copy-start = (bf16[2,1024,256]{2,1,0:T(8,128)(2,1)S(1)}, bf16[2,1024,256]{2,1,0:T(8,128)(2,1)}, u32[]{:S(2)}) copy-start(bf16[2,1024,256]{2,1,0:T(8,128)(2,1)} %refs_10_.1) | copy-start | bytes 3145732
  3.1 2.6 %copy-start.2 = (f32[512,256]{1,0:T(8,128)S(1)}, f32[512,256]{1,0:T(8,128)}, u32[]{:S(2)}) copy-start(f32[512,256]{1,0:T(8,128)} %codes.1) | copy-start | bytes 1572868
  3.1 2.6 %copy-start.3 = (s32[512]{0:T(512)S(1)}, s32[512]{0:T(512)}, u32[]{:S(2)}) copy-start(s32[512]{0:T(512)} %param.5) | copy-start | bytes 6148
  3.1 18.6 %collective-permute-start.5 = (bf16[1056,256]{1,0:T(8,128)(2,1)S(1)}, bf16[1056,256]{1,0:T(8,128)(2,1)S(1)}, u32[]{:S(2)}, u32[]{:S(2)}) collective-permute-start(bf16[1056,256]{1,0:T(8,128)(2,1)S(1)} %shard_map.59.refs_0_), channel_id=1, source_target_pairs={{0,2},{1,3},{2,0},{3,1},{4,6},{5,7},{6,4},{7,5},{8,10},{9,11},{10,... | collective-permute-start | bytes 1622024 | tf_op jit(solution)/shard_map/ppermute | solution.py:237
  5.1 23.6 %collective-permute-start.6 = (bf16[1056,256]{1,0:T(8,128)(2,1)S(1)}, bf16[1056,256]{1,0:T(8,128)(2,1)S(1)}, u32[]{:S(2)}, u32[]{:S(2)}) collective-permute-start(bf16[1056,256]{1,0:T(8,128)(2,1)S(1)} %shard_map.61.refs_1_), channel_id=1, source_target_pairs={{0,2},{1,3},{2,0},{3,1},{4,6},{5,7},{6,4},{7,5},{8,10},{9,11},{10,... | collective-permute-start | bytes 1622024 | tf_op jit(solution)/shard_map/ppermute | solution.py:237
  7.3 11.0 %collective-permute-start = (bf16[272,256]{1,0:T(8,128)(2,1)S(1)}, bf16[272,256]{1,0:T(8,128)(2,1)S(1)}, u32[]{:S(2)}, u32[]{:S(2)}) collective-permute-start(bf16[272,256]{1,0:T(8,128)(2,1)S(1)} %get-tuple-element.27), channel_id=1, source_target_pairs={{0,8},{1,9},{2,10},{3,11},{4,12},{5,13},{6,14},{7,15},{8,0},{9,1},... | collective-permute-start | bytes 417800 | tf_op jit(solution)/shard_map/ppermute | solution.py:237
  9.9 11.2 %collective-permute-start.1 = (bf16[272,256]{1,0:T(8,128)(2,1)S(1)}, bf16[272,256]{1,0:T(8,128)(2,1)S(1)}, u32[]{:S(2)}, u32[]{:S(2)}) collective-permute-start(bf16[272,256]{1,0:T(8,128)(2,1)S(1)} %get-tuple-element.28), channel_id=1, source_target_pairs={{0,12},{1,13},{2,14},{3,15},{4,8},{5,9},{6,10},{7,11},{8,4},{9,5},... | collective-permute-start | bytes 417800 | tf_op jit(solution)/shard_map/ppermute | solution.py:237
  9.9 11.2 %collective-permute-start.2 = (bf16[272,256]{1,0:T(8,128)(2,1)S(1)}, bf16[272,256]{1,0:T(8,128)(2,1)S(1)}, u32[]{:S(2)}, u32[]{:S(2)}) collective-permute-start(bf16[272,256]{1,0:T(8,128)(2,1)S(1)} %get-tuple-element.29), channel_id=1, source_target_pairs={{0,4},{1,5},{2,6},{3,7},{4,0},{5,1},{6,2},{7,3},{8,12},{9,13},{10,... | collective-permute-start | bytes 417800 | tf_op jit(solution)/shard_map/ppermute | solution.py:237
  21.1 9.3 %collective-permute-start.3 = (bf16[1056,256]{1,0:T(8,128)(2,1)S(1)}, bf16[1056,256]{1,0:T(8,128)(2,1)S(1)}, u32[]{:S(2)}, u32[]{:S(2)}) collective-permute-start(bf16[1056,256]{1,0:T(8,128)(2,1)S(1)} %shard_map.59.refs_0_), channel_id=1, source_target_pairs={{0,1},{1,0},{2,3},{3,2},{4,5},{5,4},{6,7},{7,6},{8,9},{9,8},{10,11... | collective-permute-start | bytes 1622024 | tf_op jit(solution)/shard_map/ppermute | solution.py:237
  21.1 9.2 %collective-permute-start.4 = (bf16[1056,256]{1,0:T(8,128)(2,1)S(1)}, bf16[1056,256]{1,0:T(8,128)(2,1)S(1)}, u32[]{:S(2)}, u32[]{:S(2)}) collective-permute-start(bf16[1056,256]{1,0:T(8,128)(2,1)S(1)} %shard_map.61.refs_1_), channel_id=1, source_target_pairs={{0,1},{1,0},{2,3},{3,2},{4,5},{5,4},{6,7},{7,6},{8,9},{9,8},{10,11... | collective-permute-start | bytes 1622024 | tf_op jit(solution)/shard_map/ppermute | solution.py:237
  21.6 8.7 %collective-permute-start.7 = (bf16[1056,256]{1,0:T(8,128)(2,1)S(1)}, bf16[1056,256]{1,0:T(8,128)(2,1)S(1)}, u32[]{:S(2)}, u32[]{:S(2)}) collective-permute-start(bf16[1056,256]{1,0:T(8,128)(2,1)S(1)} %collective-permute-done.5.refs_4_), channel_id=1, source_target_pairs={{0,1},{1,0},{2,3},{3,2},{4,5},{5,4},{6,7},{7,6},{8,9},{9,8},{10,11... | collective-permute-start | bytes 1622024 | tf_op jit(solution)/shard_map/ppermute | solution.py:237
  28.8 1.9 %collective-permute-start.8 = (bf16[1056,256]{1,0:T(8,128)(2,1)S(1)}, bf16[1056,256]{1,0:T(8,128)(2,1)S(1)}, u32[]{:S(2)}, u32[]{:S(2)}) collective-permute-start(bf16[1056,256]{1,0:T(8,128)(2,1)S(1)} %collective-permute-done.6.refs_5_), channel_id=1, source_target_pairs={{0,1},{1,0},{2,3},{3,2},{4,5},{5,4},{6,7},{7,6},{8,9},{9,8},{10,11... | collective-permute-start | bytes 1622024 | tf_op jit(solution)/shard_map/ppermute | solution.py:237
  28.8 15.1 %collective-permute-start.12 = (bf16[1088,256]{1,0:T(8,128)(2,1)S(1)}, bf16[1088,256]{1,0:T(8,128)(2,1)S(1)}, u32[]{:S(2)}, u32[]{:S(2)}) collective-permute-start(bf16[1088,256]{1,0:T(8,128)(2,1)S(1)} %pad_maximum_fusion), channel_id=1, source_target_pairs={{0,2},{1,3},{2,0},{3,1},{4,6},{5,7},{6,4},{7,5},{8,10},{9,11},{10,... | collective-permute-start | bytes 1671176 | tf_op jit(solution)/shard_map/ppermute | solution.py:237
  32.4 21.8 %collective-permute-start.9 = (bf16[256,1024]{1,0:T(8,128)(2,1)S(1)}, bf16[256,1024]{1,0:T(8,128)(2,1)S(1)}, u32[]{:S(2)}, u32[]{:S(2)}) collective-permute-start(bf16[256,1024]{1,0:T(8,128)(2,1)S(1)} %shard_map.63.refs_5_), channel_id=1, source_target_pairs={{0,4},{1,5},{2,6},{3,7},{4,0},{5,1},{6,2},{7,3},{8,12},{9,13},{10,... | collective-permute-start | bytes 1572872 | tf_op jit(solution)/shard_map/ppermute | solution.py:237
  34.5 37.7 %collective-permute-start.10 = (bf16[256,1024]{1,0:T(8,128)(2,1)S(1)}, bf16[256,1024]{1,0:T(8,128)(2,1)S(1)}, u32[]{:S(2)}, u32[]{:S(2)}) collective-permute-start(bf16[256,1024]{1,0:T(8,128)(2,1)S(1)} %shard_map.64.refs_6_), channel_id=1, source_target_pairs={{0,8},{1,9},{2,10},{3,11},{4,12},{5,13},{6,14},{7,15},{8,0},{9,1},... | collective-permute-start | bytes 1572872 | tf_op jit(solution)/shard_map/ppermute | solution.py:237
  39.1 44.1 %collective-permute-start.11 = (bf16[256,1024]{1,0:T(8,128)(2,1)S(1)}, bf16[256,1024]{1,0:T(8,128)(2,1)S(1)}, u32[]{:S(2)}, u32[]{:S(2)}) collective-permute-start(bf16[256,1024]{1,0:T(8,128)(2,1)S(1)} %shard_map.65.refs_7_), channel_id=1, source_target_pairs={{0,12},{1,13},{2,14},{3,15},{4,8},{5,9},{6,10},{7,11},{8,4},{9,5},... | collective-permute-start | bytes 1572872 | tf_op jit(solution)/shard_map/ppermute | solution.py:237
  47.6 3.3 %copy-start.1 = (bf16[2,1024,256]{2,1,0:T(8,128)(2,1)S(1)}, bf16[2,1024,256]{2,1,0:T(8,128)(2,1)}, u32[]{:S(2)}) copy-start(bf16[2,1024,256]{2,1,0:T(8,128)(2,1)} %refs_10_.1) | copy-start | bytes 3145732
  50.9 34.6 %collective-permute-start.13 = (bf16[2,1040,256]{2,1,0:T(8,128)(2,1)S(1)}, bf16[2,1040,256]{2,1,0:T(8,128)(2,1)S(1)}, u32[]{:S(2)}, u32[]{:S(2)}) collective-permute-start(bf16[2,1040,256]{2,1,0:T(8,128)(2,1)S(1)} %shard_map.69), channel_id=1, source_target_pairs={{0,1},{1,0},{2,3},{3,2},{4,5},{5,4},{6,7},{7,6},{8,9},{9,8},{10,11... | collective-permute-start | bytes 3194888 | tf_op jit(solution)/shard_map/ppermute | solution.py:237

commit v3 on v2

v3 whole, which is shorter than its diff:
```python
import functools

import jax
import jax.numpy as jnp
from jax import lax
from jax.experimental import pallas as pl
from jax.experimental.pallas import tpu as pltpu
from jax.sharding import PartitionSpec as P

GRP = 4
META = 16
SCALE = 5
LIGHT = 1
HEAVY = 100
BF = jnp.bfloat16
F32 = jnp.float32
VMEM = pl.BlockSpec(memory_space=pltpu.VMEM)
SMEM = pl.BlockSpec(memory_space=pltpu.SMEM)


def call(body, out_shape, n_in, flops, nbytes, in_specs=None, out_specs=None, scratch=()):
    many = isinstance(out_shape, (list, tuple))
    return pl.pallas_call(
        body,
        out_shape=out_shape,
        in_specs=in_specs or [VMEM] * n_in,
        out_specs=out_specs or ([VMEM] * len(out_shape) if many else VMEM),
        scratch_shapes=[pltpu.VMEM(*x) for x in scratch],
        compiler_params=pltpu.CompilerParams(vmem_limit_bytes=24 * 1024 * 1024),
        cost_estimate=pl.CostEstimate(flops=flops, bytes_accessed=nbytes, transcendentals=0),
    )


def three(value):
    first = value.astype(BF)
    rest = value - first.astype(F32)
    second = rest.astype(BF)
    third = (rest - second.astype(F32)).astype(BF)
    return first, second, third


def cluster_lanes(shape):
    lane = lax.broadcasted_iota(jnp.int32, shape, 1)
    return jnp.where(lane < 128, lane >> 4, lane - 128)


def ring_place(group):
    for shift in (1, 2, 4, 8):
        group = group ^ (group >> shift)
    return group


def pack_body(groups, rows, here, labels, codes, *outs):
    frames, width = codes.shape
    group, place = here[0] // GRP, here[0] % GRP
    wide = jnp.broadcast_to(labels[...], (8, frames))
    steps = (ring_place(wide >> 3) - ring_place(group)) & (groups - 1)
    kr = steps * 8 + ((wide & 7) ^ (place * 2))
    kc = kr.T[:, 0:1]
    kr = kr[0:1, :]
    lane = lax.broadcasted_iota(jnp.int32, (1, frames), 1)
    sub = lax.broadcasted_iota(jnp.int32, (frames, 1), 0)
    ur, uc = kr * frames + lane, kc * frames + sub
    gr = kr >> 3
    base_r = gr * (8 * frames)
    rank = jnp.sum(((uc < ur) & (uc >= base_r)).astype(jnp.int32), axis=0, keepdims=True)
    slot = gr * rows + rank
    rounded = codes[...].astype(BF)
    target = lax.broadcasted_iota(jnp.int32, (rows, frames), 0)
    cluster = cluster_lanes((1, width))
    row = lax.broadcasted_iota(jnp.int32, (META, width), 0)
    step = lax.broadcasted_iota(jnp.int32, (frames, width), 1)
    counts = jnp.sum(((kc >> 3) == step).astype(F32), axis=0, keepdims=True)
    for k in range(groups):
        pick = (slot == target + k * rows).astype(F32).astype(BF)
        outs[k][:rows, :] = jnp.dot(pick, rounded, preferred_element_type=F32).astype(BF)
        inside = kc >= 8 * k
        first = jnp.sum((inside & (kc < 8 * k + cluster)).astype(F32), axis=0, keepdims=True)
        last = jnp.sum((inside & (kc < 8 * k + cluster + 1)).astype(F32), axis=0, keepdims=True)
        bounds = jnp.where(row == 0, first, jnp.where(row == 1, last, jnp.where(row == 2, counts, 0.0)))
        outs[k][rows:, :] = bounds.astype(BF)
    gc = kc >> 3
    base_c = gc * (8 * frames)
    rank_c = jnp.sum(((ur < uc) & (ur >= base_c)).astype(jnp.int32), axis=1, keepdims=True)
    outs[groups][...] = gc * rows + rank_c


def busy_body(groups, rows, here, *refs):
    out = refs[groups]
    lane = lax.broadcasted_iota(jnp.int32, (1, refs[0].shape[1]), 1)
    place = ring_place(here[0] // GRP)
    flags = [0, 0]
    for d in range(groups):
        most = jnp.zeros(lane.shape, F32)
        for s in range(groups):
            counts = refs[s][rows:, :].astype(F32)[2:3, :]
            most = jnp.maximum(most, jnp.where(lane == (d + s) % groups, counts, 0.0))
        flag = (jnp.max(most) > float(rows // 2)).astype(jnp.int32)
        flags[d % 2] = flags[d % 2] | flag
    odd = place & 1
    own, other = flags
    even = jnp.where(odd == 0, own, other)
    uneven = jnp.where(odd == 0, other, own)
    out[0] = jnp.where(uneven == 0, 0, jnp.where(even == 0, 1, 2))


def share_body(c, sharp, centres, out):
    width = out.shape[1]
    fine = centres.shape[1]
    row = lax.broadcasted_iota(jnp.int32, (8, width), 0)
    ones = jnp.ones((8, width), BF)
    dims = (((1,), (1,)), ((), ()))
    values = centres[c]
    out[:fine, :] = values
    wide = values.astype(F32)
    square = wide * wide
    high = square.astype(BF)
    low = (square - high.astype(F32)).astype(BF)
    norm = lax.dot_general(ones, high, dims, preferred_element_type=F32)
    norm = norm + lax.dot_general(ones, low, dims, preferred_element_type=F32)
    terms = [t.astype(F32) for t in three(-0.5 * norm)]
    tiles = []
    for q in range(fine // width):
        tile = jnp.where(row == 3, sharp[c : c + 1, 0:1].astype(F32), 0.0)
        for t in range(3):
            tile = jnp.where(row == t, terms[t][:, q * width : (q + 1) * width], tile)
        tiles.append(tile)
    out[fine:, :] = jnp.concatenate(tiles, axis=0).astype(BF)


def member_lanes(block, rows):
    bounds = block[rows:, :].astype(F32)
    row = lax.broadcasted_iota(jnp.int32, (rows, block.shape[1]), 0).astype(F32)
    return ((row >= bounds[0:1, :]) & (row < bounds[1:2, :])).astype(F32)


def mass_rows(row, mass):
    terms = three(mass)
    total = jnp.zeros(row.shape, F32)
    for t in range(3):
        total = jnp.where(row == t, terms[t].astype(F32), total)
    return total.astype(BF)


def soft_rows(block, rows, first, refs, fine):
    member = member_lanes(block, rows).astype(BF)
    codes = block[:rows, :]
    count = len(refs)
    width = codes.shape[1]
    pick = member[:, 16 * first : 16 * (first + count)]
    part = lax.broadcasted_iota(jnp.int32, pick.shape, 1) & 15
    zero = jnp.zeros_like(pick)
    low = jnp.where(part < 3, pick, zero)
    high = jnp.where((part >= 8) & (part < 11), pick, zero)
    columns = []
    for q in range(0, fine // width, 2):
        start = fine + 8 * q
        table = jnp.concatenate([ref[start : start + 16, :] for ref in refs], axis=0)
        columns += [jnp.dot(p, table, preferred_element_type=F32) for p in (low, high)]
    logits = jnp.concatenate(columns, axis=1)
    for n, ref in enumerate(refs):
        r = first + n
        chosen = codes * member[:, 128 + r : 129 + r]
        logits = logits + lax.dot_general(
            chosen, ref[:fine, :], (((1,), (1,)), ((), ())), preferred_element_type=F32
        )
    scale = jnp.dot(jnp.where(part == 3, pick, zero), table[:, :128], preferred_element_type=F32)
    logits = logits * scale[:, 0:1]
    shifted = jnp.exp(logits - jnp.max(logits, axis=1, keepdims=True))
    unit = float(fine) / jnp.sum(shifted, axis=1, keepdims=True)
    return (shifted * unit).astype(BF)


def copy_body(x, out):
    out[...] = x[...]


def halve(values, outs):
    size = values.shape[0] // len(outs)
    for n, out in enumerate(outs):
        out[...] = values[n * size : (n + 1) * size, :]


def soft_body(rows, count, block, *refs):
    outs = refs[count:]
    halve(soft_rows(block, rows, 0, refs[:count], outs[0].shape[1]), outs)


def softs_body(rows, count, last, blocks, *refs):
    outs = refs[count:]
    each = len(outs) // (last + 1)
    step = rows + META

    def one(n, _):
        block = blocks[pl.ds(pl.multiple_of((last - n) * step, 16), step), :]
        values = soft_rows(block, rows, 0, refs[:count], outs[0].shape[1])
        for k in range(last + 1):

            @pl.when(n == last - k)
            def _(k=k):
                halve(values, outs[k * each : (k + 1) * each])

        return 0

    lax.fori_loop(0, last + 1, one, 0)


def other_body(groups, rows, blocks, *refs):
    out = refs[-1]
    step = rows + META

    def one(k, _):
        block = blocks[pl.ds(pl.multiple_of(k * step, 16), step), :]
        values = soft_rows(block, rows, 4, refs[:-1], out.shape[1])
        out[pl.ds(pl.multiple_of(k * rows, 16), rows), :] = values
        return 0

    lax.fori_loop(0, groups, one, 0)


def sums_body(groups, rows, blocks, others, soft, centres, *refs):
    *mine, out, mass_out, give, sums, masses = refs
    each = len(mine) // groups
    width = blocks.shape[1]
    fine = soft.shape[1]
    count = fine // width
    step = rows + META
    dims = (((0,), (0,)), ((), ()))
    lane = lax.broadcasted_iota(jnp.int32, (1, width), 1)
    row = lax.broadcasted_iota(jnp.int32, (rows, 1), 0).astype(F32)

    def one(c, _):
        total, mass = 0.0, 0.0
        for k in range(2 * groups):
            source = blocks if k < groups else others
            n = k % groups
            codes = source[n * step : n * step + rows, :]
            bounds = source[n * step + rows : (n + 1) * step, :].astype(F32)
            r = c if k < groups else c + 4
            ends = jnp.sum(jnp.where(lane == 128 + r, bounds, 0.0), axis=1, keepdims=True)
            inside = ((row >= ends[0:1, :]) & (row < ends[1:2, :])).astype(F32).astype(BF)
            if k >= groups:
                values = soft[n * rows : (n + 1) * rows, :]
            else:
                values = [ref[...] for ref in mine[n * each : (n + 1) * each]]
                values = values[0] if each == 1 else jnp.concatenate(values, axis=0)
            chosen = codes * inside
            total = total + lax.dot_general(chosen, values, dims, preferred_element_type=F32)
            ones = jnp.broadcast_to(inside, (rows, META))
            mass = mass + lax.dot_general(ones, values, dims, preferred_element_type=F32)
        sums[c] = total.T
        masses[c] = jnp.concatenate(
            [mass[0:1, q * width : (q + 1) * width] for q in range(count)], axis=0
        )
        return 0

    lax.fori_loop(0, 4, one, 0)
    for n in range(2):
        out[n] = sums[n] + centres[n].astype(F32)
        mass_out[n] = masses[n] + 1.0
        give[n, :fine, :] = sums[2 + n].astype(BF)
        terms = [t.astype(F32) for t in three(masses[2 + n])]
        rest = jnp.zeros((META - 3 * count, width), F32)
        give[n, fine:, :] = jnp.concatenate(terms + [rest], axis=0).astype(BF)


def unpack_body(starts, slot, *refs):
    *refs, out = refs
    frames, fine = out.shape
    picks = []
    for start, ref in zip(starts, refs):
        lane = lax.broadcasted_iota(jnp.int32, (frames, ref.shape[0]), 1)
        picks.append((slot[...] == lane + start).astype(F32).astype(BF))
    pick = jnp.concatenate(picks, axis=1)
    width = 256
    for q in range(fine // width):
        span = slice(q * width, (q + 1) * width)
        values = jnp.concatenate([ref[:, span] for ref in refs], axis=0)
        out[:, span] = jnp.dot(pick, values, preferred_element_type=F32).astype(BF)


def finish_body(mine, mass, got, out):
    fine, width = out.shape[1:]
    spans = fine // width
    for n in range(out.shape[0]):
        tail = got[n, fine:, :].astype(F32)
        total = mass[n]
        for t in range(3):
            total = total + tail[t * spans : (t + 1) * spans, :]
        inverse = 1.0 / total
        for q in range(spans):
            column = jnp.broadcast_to(inverse[q : q + 1, :], (8, width)).T[:, 0:1]
            span = slice(q * width, (q + 1) * width)
            out[n, span, :] = (mine[n, span, :] + got[n, span, :].astype(F32)) * column


def shards(codes, labels, centroids, sharpness):
    route = lax.axis_size("route")
    frames, width = codes.shape
    per_device, fine, _ = centroids.shape
    groups = route // GRP
    rows = GRP * max(8, 2 * frames // route)
    def turn(x, steps, places=range(groups)):
        ring = [k ^ (k >> 1) for k in range(groups)]
        pairs = [(ring[k], ring[(k + steps) % groups]) for k in places]
        return lax.ppermute(
            x, "route", [(GRP * a + m, GRP * b + m) for a, b in pairs for m in range(GRP)]
        )

    here = lax.axis_index("route").astype(jnp.int32).reshape(1)

    def swap(x, mask):
        return lax.ppermute(x, "route", [(r, r ^ mask) for r in range(route)])

    sharp = sharpness.reshape(per_device, 1)
    own, far = [], []
    for c in range(per_device):
        own.append(
            call(
                functools.partial(share_body, c),
                jax.ShapeDtypeStruct((fine + 8 * (fine // width), width), BF),
                2,
                SCALE * 4 * 8 * fine * width,
                SCALE * fine * width * 4,
            )(sharp, centroids)
        )
        far.append(swap(own[c], 2))
    here, _ = lax.optimization_barrier((here, own[0]))
    block_shape = jax.ShapeDtypeStruct((rows + META, width), BF)
    *send, slot = call(
        functools.partial(pack_body, groups, rows),
        [block_shape] * groups + [jax.ShapeDtypeStruct((frames, 1), jnp.int32)],
        3,
        SCALE * 2 * groups * rows * frames * width,
        SCALE * frames * width * 8,
        in_specs=[SMEM, VMEM, VMEM],
    )(here, labels.reshape(1, frames), codes)
    *send, _ = lax.optimization_barrier((*send, own[1]))
    blocks = {0: send[0]}
    for k in range(1, groups):
        blocks[k] = turn(send[k], k)
    arrived = [blocks[k] for k in range(1, groups)]
    busy = here
    if groups == 4:
        busy = call(
            functools.partial(busy_body, groups, rows),
            jax.ShapeDtypeStruct((1,), jnp.int32),
            1 + groups,
            1000,
            1000,
            in_specs=[SMEM] + [VMEM] * groups,
            out_specs=SMEM,
        )(here, *[blocks[k] for k in range(groups)])
    near = [swap(lax.optimization_barrier((x, *arrived))[0], 1) for x in own]
    last = [swap(lax.optimization_barrier((x, busy, *arrived))[0], 1) for x in far]

    halves = 2 if groups == 4 else 1
    work = 2 * rows * fine * width * 2 * GRP
    held = [call(copy_body, jax.ShapeDtypeStruct(x.shape, BF), 1, 0, 0)(x) for x in (*own, *near, *far, *last)]
    half = jax.ShapeDtypeStruct((rows // halves, fine), BF)
    top = groups - 1
    first = call(
        functools.partial(soft_body, rows, len(held)),
        [half] * halves,
        1 + len(held),
        SCALE * work,
        SCALE * GRP * per_device * fine * width * 2,
    )(blocks[top], *held)

    def refine(places, first, held, gathered, slot, centroids):
        others = swap(gathered, 2)
        out = call(
            functools.partial(softs_body, rows, len(held), top - 1),
            [half] * (halves * top),
            1 + len(held),
            SCALE * top * work,
            SCALE * GRP * per_device * fine * width * 2,
        )(gathered, *held)
        soft = {k: out[k * halves : (k + 1) * halves] for k in range(top)}
        soft[top] = first
        back = dict(soft)
        for k in range(top, 0, -1):
            back[k] = [turn(soft[k][0], -k)] + [turn(x, -k, places) for x in soft[k][1:]]
        others, _, back[top] = lax.optimization_barrier((others, soft[0][0], back[top]))
        other_soft = call(
            functools.partial(other_body, groups, rows),
            jax.ShapeDtypeStruct((groups * rows, fine), BF),
            1 + 2 * per_device,
            LIGHT * 2 * groups * work,
            LIGHT * groups * rows * fine * 2,
        )(others, *held[: 2 * per_device])
        mass_shape = ((2 * per_device, fine // width, width), F32)
        mine, mass, give = call(
            functools.partial(sums_body, groups, rows),
            [
                jax.ShapeDtypeStruct(centroids.shape, F32),
                jax.ShapeDtypeStruct((per_device, fine // width, width), F32),
                jax.ShapeDtypeStruct((per_device, fine + META, width), BF),
            ],
            4 + halves * groups,
            LIGHT * 16 * groups * rows * fine * width,
            LIGHT * groups * rows * fine * 4,
            scratch=[((2 * per_device, fine, width), F32), mass_shape],
        )(gathered, others, other_soft, centroids, *[x for k in range(groups) for x in soft[k]])
        got = swap(give, 1)
        pieces = [
            (k * rows + n * (rows // halves), x) for k in range(groups) for n, x in enumerate(back[k])
        ]
        soft_labels = call(
            functools.partial(unpack_body, [start for start, _ in pieces]),
            jax.ShapeDtypeStruct((slot.shape[0], fine), BF),
            1 + len(pieces),
            HEAVY * slot.shape[0] * groups * rows * fine,
            HEAVY * groups * rows * fine * 2,
        )(slot, *[x for _, x in pieces])
        new_centroids = call(
            finish_body,
            jax.ShapeDtypeStruct(centroids.shape, F32),
            3,
            4 * per_device * fine * width,
            per_device * fine * width * 10,
        )(mine, mass, got)
        return soft_labels, new_centroids

    gathered = jnp.concatenate([blocks[k] for k in range(groups)], axis=0)
    shared = (first, held, gathered, slot, centroids)
    if halves == 1:
        return refine(range(groups), *shared)
    cases = [functools.partial(refine, c) for c in ((0, 2), (1, 3), range(groups))]
    return lax.switch(busy[0], cases, *shared)


def solution(mesh):
    placed = (
        P(("parts", "route"), None),
        P(("parts", "route")),
        P(("parts", "route"), None, None),
        P(("parts", "route")),
    )
    return jax.shard_map(
        shards,
        mesh=mesh,
        in_specs=placed,
        out_specs=(P(("parts", "route"), None), P(("parts", "route"), None, None)),
        check_vma=False,
    )
```

time: 87.7 us -> 81.8 us (0.933)
  waiting for transfers between devices: 48.3 us -> 30 us
  Pallas kernels: 23.9 us -> 30.3 us
  starting transfers between devices: 12.5 us -> 18 us
  local copies, waits for them, and re-layouts: 2 us -> 0.78 us
    ppermute x14 -> x8, waiting for transfers between devices: 48.3 us -> 10.1 us  [swap(): return lax.ppermute(x, 'route', [(r, r ^ mask) for r in range(route)])]
    ppermute x0 -> x9, waiting for transfers between devices: none -> 19.9 us  [turn(): lax.ppermute(x, 'route', [(GRP * a + m, GRP * b + m) for a, b in pairs fo...]
    ppermute x0 -> x9, starting transfers between devices: none -> 13.2 us  [turn(): lax.ppermute(x, 'route', [(GRP * a + m, GRP * b + m) for a, b in pairs fo...]
    ppermute x14 -> x8, starting transfers between devices: 12.5 us -> 4.84 us  [swap(): return lax.ppermute(x, 'route', [(r, r ^ mask) for r in range(route)])]
    pallas_call x9 -> x15, Pallas kernels: 21.4 us -> 26.5 us  [the longest x1 9.17 us: refine(): call(functools.partial(sums_body, groups, rows), [jax.ShapeDtypeStruct(ce...]
    pallas_call x2, Pallas kernels: 0.88 us -> 2.2 us  [shards(): call(functools.partial(share_body, c), jax.ShapeDtypeStruct((fine + 8 * (...]
    unnamed x8, local copies, waits for them, and re-layouts: 1.24 us -> 0.02 us
  transfers between devices with their start and end apart: 14 -> 17, of which waited for: 7 -> 7; matrix products, arithmetic and copies ran while one was open for 0% -> 0% of each run, Pallas kernels for 24% -> 31%
where the time goes in v3:
time: 81.8 us; the launch traced here: 80.8 us
  Pallas kernels  30.3 us (37%)
  waiting for transfers between devices  30 us (37%)
  starting transfers between devices  18 us (22%)
  between operations  1.44 us (2%)
    ppermute x9, waiting for transfers between devices, turn(): lax.ppermute(x, 'route', [(GRP * a + m, GRP * b + m) for a, b in pairs fo...  19.9 us
    ppermute x9, starting transfers between devices, turn(): lax.ppermute(x, 'route', [(GRP * a + m, GRP * b + m) for a, b in pairs fo...  13.2 us
    ppermute x8, waiting for transfers between devices, swap(): return lax.ppermute(x, 'route', [(r, r ^ mask) for r in range(route)])  10.1 us
    pallas_call x1, Pallas kernels, refine(): call(functools.partial(sums_body, groups, rows), [jax.ShapeDtypeStruct(ce...  9.17 us
    pallas_call x1, Pallas kernels, refine(): call(functools.partial(softs_body, rows, len(held), top - 1), [half] * (h...  5.39 us
    pallas_call x1, Pallas kernels, refine(): call(functools.partial(other_body, groups, rows), jax.ShapeDtypeStruct((g...  5.02 us
    ppermute x8, starting transfers between devices, swap(): return lax.ppermute(x, 'route', [(r, r ^ mask) for r in range(route)])  4.84 us
    pallas_call x1, Pallas kernels, refine(): call(functools.partial(unpack_body, [start for start, _ in pieces]), jax....  2.25 us
  transfers between devices with their start and end apart: 17, of which 7 were waited for; matrix products, arithmetic and copies ran while one was open for 0% of the time, Pallas kernels for 31%

profile of v3, /device:TPU:8, one launch (start us, length us, event | category | flops | bytes accessed | tf_op | source)
XLA Modules:
  0.0 80.8 jit_solution(4839289372760443988)
XLA Ops:
  0.6 0.8 copy.12.sharp
  1.4 1.8 %shard_map.67.x = bf16[1056,256]{1,0:T(8,128)(2,1)S(1)} custom-call(bf16[2,1]{1,0:T(2,128)(2,1)S(1)} %copy.12.sharp, bf16[2,1024,256]{2,1,0:T(8,128)(2,1)} %centres.3), custom_call_target="tpu_custom_call" | custom-call | flops 41943040 | bytes 5242880 | tf_op jit(solution)/shard_map/pallas_call | solution.py:319
  3.1 0.0 copy-start
  3.2 0.0 copy-start.1
  3.2 1.6 %collective-permute-start.30 = (bf16[1056,256]{1,0:T(8,128)(2,1)S(1)}, bf16[1056,256]{1,0:T(8,128)(2,1)S(1)}, u32[]{:S(2)}, u32[]{:S(2)}) collective-permute-start(bf16[1056,256]{1,0:T(8,128)(2,1)S(1)} %shard_map.67.x), channel_id=1, source_target_pairs={{0,2},{1,3},{2,0},{3,1},{4,6},{5,7},{6,4},{7,5},{8,10},{9,11},{10,... | collective-permute-start | bytes 1622024 | tf_op jit(solution)/shard_map/ppermute | solution.py:313
  4.8 0.4 shard_map.65.x
  5.2 0.6 collective-permute-start.29
  5.8 1.6 %shard_map.66 = (bf16[272,256]{1,0:T(8,128)(2,1)S(1)}, bf16[272,256]{1,0:T(8,128)(2,1)S(1)}, bf16[272,256]{1,0:T(8,128)(2,1)S(1)}, bf16[272,256]{1,0:T(8,128)(2,1)S(1)}, s32[512,1]{1,0:T(8,128)S(1)}) custom-call(s32[1]{0:T(128)} %bitcast.here, s32[1,512]{1,0:T(1,128)S(1)} %bitcast.4, f32[512,256]{1,0:T(8,128)S(1)} %copy-done), custom_call_target="tpu_custom_call" | custom-call | flops 1342177280 | bytes 5242880 | tf_op jit(solution)/shard_map/pallas_call | solution.py:330
  7.4 2.6 %collective-permute-start.24 = (bf16[272,256]{1,0:T(8,128)(2,1)S(1)}, bf16[272,256]{1,0:T(8,128)(2,1)S(1)}, u32[]{:S(2)}, u32[]{:S(2)}) collective-permute-start(bf16[272,256]{1,0:T(8,128)(2,1)S(1)} %get-tuple-element.177), channel_id=1, source_target_pairs={{0,4},{1,5},{2,6},{3,7},{4,12},{5,13},{6,14},{7,15},{12,8},{13,9},... | collective-permute-start | bytes 417800 | tf_op jit(solution)/shard_map/ppermute | solution.py:306
  10.1 0.0 collective-permute-start.25
  10.1 1.9 %collective-permute-start.26 = (bf16[272,256]{1,0:T(8,128)(2,1)S(1)}, bf16[272,256]{1,0:T(8,128)(2,1)S(1)}, u32[]{:S(2)}, u32[]{:S(2)}) collective-permute-start(bf16[272,256]{1,0:T(8,128)(2,1)S(1)} %get-tuple-element.179), channel_id=1, source_target_pairs={{0,8},{1,9},{2,10},{3,11},{4,0},{5,1},{6,2},{7,3},{12,4},{13,5},{1... | collective-permute-start | bytes 417800 | tf_op jit(solution)/shard_map/ppermute | solution.py:306
  12.0 7.9 %collective-permute-done.24.refs_1_ = bf16[272,256]{1,0:T(8,128)(2,1)S(1)} collective-permute-done((bf16[272,256]{1,0:T(8,128)(2,1)S(1)}, bf16[272,256]{1,0:T(8,128)(2,1)S(1)}, u32[]{:S(2)}, u32[]{:S(2)}) %collective-permute-start.24) | collective-permute-done | bytes 139296 | tf_op jit(solution)/shard_map/ppermute | solution.py:306
  19.8 1.6 %collective-permute-done.25.refs_2_ = bf16[272,256]{1,0:T(8,128)(2,1)S(1)} collective-permute-done((bf16[272,256]{1,0:T(8,128)(2,1)S(1)}, bf16[272,256]{1,0:T(8,128)(2,1)S(1)}, u32[]{:S(2)}, u32[]{:S(2)}) %collective-permute-start.25) | collective-permute-done | bytes 139296 | tf_op jit(solution)/shard_map/ppermute | solution.py:306
  21.4 0.0 collective-permute-done.26.refs_3_.block
  21.4 0.0 collective-permute-start.27
  21.4 0.5 collective-permute-start.28
  21.9 0.7 shard_map.68
  22.6 0.0 collective-permute-done.30.x
  22.6 6.2 %collective-permute-done.29.x = bf16[1056,256]{1,0:T(8,128)(2,1)S(1)} collective-permute-done((bf16[1056,256]{1,0:T(8,128)(2,1)S(1)}, bf16[1056,256]{1,0:T(8,128)(2,1)S(1)}, u32[]{:S(2)}, u32[]{:S(2)}) %collective-permute-start.29) | collective-permute-done | bytes 540704 | tf_op jit(solution)/shard_map/ppermute | solution.py:313
  28.8 0.0 collective-permute-start.31
  28.8 0.5 collective-permute-start.32
  30.2 0.0 collective-permute-done.27.x
  30.3 0.0 collective-permute-done.28.x
  30.3 0.4 collective-permute-done.31.x
  30.8 0.7 collective-permute-done.32.x
  31.6 0.0 copy-start.3
  31.6 1.7 %shard_map.77 = (bf16[128,1024]{1,0:T(8,128)(2,1)S(1)}, bf16[128,1024]{1,0:T(8,128)(2,1)S(1)}) custom-call(bf16[272,256]{1,0:T(8,128)(2,1)S(1)} %collective-permute-done.26.refs_3_.block, bf16[1056,256]{1,0:T(8,128)(2,1)S(1)} %shard_map.69.refs_0_, bf16[1056,256]{1,0:T(8,128)(2,1)S(1)} %shard_map.70.refs_1_, bf16[1056,256]{1,0:T(8,128)(2,1)S(1)} %shard_map.71.refs_2_, ...), custom_call_target="tpu_custom_call" | custom-call | flops 5368709120 | bytes 20971520 | tf_op jit(solution)/shard_map/pallas_call | solution.py:362
  33.4 47.4 %conditional.1 = (bf16[512,1024]{1,0:T(8,128)(2,1)}, f32[2,1024,256]{2,1,0:T(8,128)}) conditional(s32[]{:T(128)} %bitcast.3, (bf16[1088,256]{1,0:T(8,128)(2,1)S(1)}, bf16[1056,256]{1,0:T(8,128)(2,1)S(1)}, bf16[1056,256]{1,0:T(8,128)(2,1)S(1)}, bf16[1056,256]{1,0:T(8,128)(2,1)S(1)}, bf16[1056,256]{1,0:T(8,128)(2,1)S(1)}, ...), branch_computations={%region_0.0_spmd, %region_1.0_spmd, %region_2.0_spmd} | conditional | flops 82680217600 | bytes 255000912 | solution.py:430
  33.4 2.6 %collective-permute-start.5 = (bf16[128,1024]{1,0:T(8,128)(2,1)S(1)}, bf16[128,1024]{1,0:T(8,128)(2,1)S(1)}, u32[]{:S(2)}, u32[]{:S(2)}) collective-permute-start(bf16[128,1024]{1,0:T(8,128)(2,1)S(1)} %get-tuple-element.94.refs_6_), channel_id=1, source_target_pairs={{0,4},{1,5},{2,6},{3,7},{4,12},{5,13},{6,14},{7,15},{12,8},{13,9},... | collective-permute-start | bytes 786440 | tf_op jit(solution)/shard_map/cond/branch_0_fun/ppermute | solution.py:306
  36.0 1.3 %collective-permute-start.6 = (bf16[128,1024]{1,0:T(8,128)(2,1)S(1)}, bf16[128,1024]{1,0:T(8,128)(2,1)S(1)}, u32[]{:S(2)}, u32[]{:S(2)}) collective-permute-start(bf16[128,1024]{1,0:T(8,128)(2,1)S(1)} %get-tuple-element.95.refs_7_), channel_id=1, source_target_pairs={{0,4},{1,5},{2,6},{3,7},{12,8},{13,9},{14,10},{15,11},{16,20},{17,... | collective-permute-start | bytes 786440 | tf_op jit(solution)/shard_map/cond/branch_0_fun/ppermute | solution.py:306
  37.3 1.6 %collective-permute-start.4 = (bf16[1088,256]{1,0:T(8,128)(2,1)S(1)}, bf16[1088,256]{1,0:T(8,128)(2,1)S(1)}, u32[]{:S(2)}, u32[]{:S(2)}) collective-permute-start(bf16[1088,256]{1,0:T(8,128)(2,1)S(1)} %get-tuple-element.79.blocks), channel_id=1, source_target_pairs={{0,2},{1,3},{2,0},{3,1},{4,6},{5,7},{6,4},{7,5},{8,10},{9,11},{10,... | collective-permute-start | bytes 1671176 | tf_op jit(solution)/shard_map/cond/branch_0_fun/ppermute | solution.py:313
  38.9 5.4 %branch_0_fun.5 = (bf16[128,1024]{1,0:T(8,128)(2,1)S(1)}, bf16[128,1024]{1,0:T(8,128)(2,1)S(1)}, bf16[128,1024]{1,0:T(8,128)(2,1)S(1)}, bf16[128,1024]{1,0:T(8,1...) custom-call(bf16[1088,256]{1,0:T(8,128)(2,1)S(1)} %get-tuple-element.79.blocks, ...), custom_call_target="tpu_custom_call" | custom-call | flops 16106127360 | bytes 20971520 | tf_op jit(solution)/shard_map/cond/branch_0_fun/pallas_call | solution.py:372
  44.3 2.7 %collective-permute-start = (bf16[128,1024]{1,0:T(8,128)(2,1)S(1)}, bf16[128,1024]{1,0:T(8,128)(2,1)S(1)}, u32[]{:S(2)}, u32[]{:S(2)}) collective-permute-start(bf16[128,1024]{1,0:T(8,128)(2,1)S(1)} %get-tuple-element.90.refs_2_), channel_id=1, source_target_pairs={{0,8},{1,9},{2,10},{3,11},{4,0},{5,1},{6,2},{7,3},{12,4},{13,5},{1... | collective-permute-start | bytes 786440 | tf_op jit(solution)/shard_map/cond/branch_0_fun/ppermute | solution.py:306
  47.0 1.3 %collective-permute-start.1 = (bf16[128,1024]{1,0:T(8,128)(2,1)S(1)}, bf16[128,1024]{1,0:T(8,128)(2,1)S(1)}, u32[]{:S(2)}, u32[]{:S(2)}) collective-permute-start(bf16[128,1024]{1,0:T(8,128)(2,1)S(1)} %get-tuple-element.91.refs_3_), channel_id=1, source_target_pairs={{0,8},{1,9},{2,10},{3,11},{12,4},{13,5},{14,6},{15,7},{16,24},{17,... | collective-permute-start | bytes 786440 | tf_op jit(solution)/shard_map/cond/branch_0_fun/ppermute | solution.py:306
  48.3 0.0 collective-permute-done.5.refs_6_
  48.3 0.1 collective-permute-start.2
  48.4 0.0 collective-permute-done.6.refs_7_
  48.4 0.7 collective-permute-start.3
  49.1 2.7 %collective-permute-done.4.blocks.others = bf16[1088,256]{1,0:T(8,128)(2,1)S(1)} collective-permute-done((bf16[1088,256]{1,0:T(8,128)(2,1)S(1)}, bf16[1088,256]{1,0:T(8,128)(2,1)S(1)}, u32[]{:S(2)}, u32[]{:S(2)}) %collective-permute-start.4) | collective-permute-done | bytes 557088 | tf_op jit(solution)/shard_map/cond/branch_0_fun/ppermute | solution.py:313
  51.8 5.0 %branch_0_fun.7.soft = bf16[1024,1024]{1,0:T(8,128)(2,1)S(1)} custom-call(bf16[1088,256]{1,0:T(8,128)(2,1)S(1)} %collective-permute-done.4.blocks.others, bf16[1056,256]{1,0:T(8,128)(2,1)S(1)} %get-tuple-element.80.refs_0_, bf16[1056,256]{1,0:T(8,128)(2,1)S(1)} %get-tuple-element.81.refs_1_, bf16[1056,256]{1,0:T(8,128)(2,1)S(1)} %get-tuple-element.82.refs_2_, ...), custom_call_target="tpu_custom_call" | custom-call | flops 8589934592 | bytes 2097152 | tf_op jit(solution)/shard_map/cond/branch_0_fun/pallas_call | solution.py:385
  56.8 9.2 %branch_0_fun.8 = (f32[2,1024,256]{2,1,0:T(8,128)S(1)}, f32[2,4,256]{2,1,0:T(4,128)S(1)}, bf16[2,1040,256]{2,1,0:T(8,128)(2,1)S(1)}) custom-call(bf16[1088,256]{1,0:T(8,128)(2,1)S(1)} %get-tuple-element.79.blocks, bf16[1088,256]{1,0:T(8,128)(2,1)S(1)} %collective-permute-done.4.blocks.others, bf16[1024,1024]{1,0:T(8,128)(2,1)S(1)} %branch_0_fun.7.soft, ...), custom_call_target="tpu_custom_call" | custom-call | flops 4294967296 | bytes 4194304 | tf_op jit(solution)/shard_map/cond/branch_0_fun/pallas_call | solution.py:393
  66.0 0.1 collective-permute-start.7
  66.0 0.0 collective-permute-done.refs_2_
  66.1 10.4 %collective-permute-done.2.refs_4_ = bf16[128,1024]{1,0:T(8,128)(2,1)S(1)} collective-permute-done((bf16[128,1024]{1,0:T(8,128)(2,1)S(1)}, bf16[128,1024]{1,0:T(8,128)(2,1)S(1)}, u32[]{:S(2)}, u32[]{:S(2)}) %collective-permute-start.2) | collective-permute-done | bytes 262176 | tf_op jit(solution)/shard_map/cond/branch_0_fun/ppermute | solution.py:306
  76.5 0.0 collective-permute-done.3.refs_5_
  76.5 2.3 %branch_0_fun.6 = bf16[512,1024]{1,0:T(8,128)(2,1)} custom-call(s32[512,1]{1,0:T(8,128)S(1)} %get-tuple-element.78.slot, bf16[128,1024]{1,0:T(8,128)(2,1)S(1)} %get-tuple-element.88.refs_0_, bf16[128,1024]{1,0:T(8,128)(2,1)S(1)} %get-tuple-element.89.refs_1_, bf16[128,1024]{1,0:T(8,128)(2,1)S(1)} %collective-permute-done.refs_2_, ...), custom_call_target="tpu_custom_call" | custom-call | flops 53687091200 | bytes 209715200 | tf_op jit(solution)/shard_map/cond/branch_0_fun/pallas_call | solution.py:409
  78.8 0.0 collective-permute-done.7.got
  78.8 2.0 %branch_0_fun.9 = f32[2,1024,256]{2,1,0:T(8,128)} custom-call(f32[2,1024,256]{2,1,0:T(8,128)S(1)} %get-tuple-element.100.mine, f32[2,4,256]{2,1,0:T(4,128)S(1)} %get-tuple-element.101.mass, bf16[2,1040,256]{2,1,0:T(8,128)(2,1)S(1)} %collective-permute-done.7.got), custom_call_target="tpu_custom_call" | custom-call | flops 2097152 | bytes 5242880 | tf_op jit(solution)/shard_map/cond/branch_0_fun/pallas_call | solution.py:416
  (15 shorter events, 0.3 us)
Async XLA Ops:
  1.4 3.4 %copy-start.2 = (bf16[2,1024,256]{2,1,0:T(8,128)(2,1)S(1)}, bf16[2,1024,256]{2,1,0:T(8,128)(2,1)}, u32[]{:S(2)}) copy-start(bf16[2,1024,256]{2,1,0:T(8,128)(2,1)} %centres.3) | copy-start | bytes 3145732
  3.1 2.6 %copy-start = (f32[512,256]{1,0:T(8,128)S(1)}, f32[512,256]{1,0:T(8,128)}, u32[]{:S(2)}) copy-start(f32[512,256]{1,0:T(8,128)} %codes.1) | copy-start | bytes 1572868
  3.2 2.6 %copy-start.1 = (s32[512]{0:T(512)S(1)}, s32[512]{0:T(512)}, u32[]{:S(2)}) copy-start(s32[512]{0:T(512)} %param.8) | copy-start | bytes 6148
  3.2 19.4 %collective-permute-start.30 = (bf16[1056,256]{1,0:T(8,128)(2,1)S(1)}, bf16[1056,256]{1,0:T(8,128)(2,1)S(1)}, u32[]{:S(2)}, u32[]{:S(2)}) collective-permute-start(bf16[1056,256]{1,0:T(8,128)(2,1)S(1)} %shard_map.67.x), channel_id=1, source_target_pairs={{0,2},{1,3},{2,0},{3,1},{4,6},{5,7},{6,4},{7,5},{8,10},{9,11},{10,... | collective-permute-start | bytes 1622024 | tf_op jit(solution)/shard_map/ppermute | solution.py:313
  5.2 23.6 %collective-permute-start.29 = (bf16[1056,256]{1,0:T(8,128)(2,1)S(1)}, bf16[1056,256]{1,0:T(8,128)(2,1)S(1)}, u32[]{:S(2)}, u32[]{:S(2)}) collective-permute-start(bf16[1056,256]{1,0:T(8,128)(2,1)S(1)} %shard_map.65.x), channel_id=1, source_target_pairs={{0,2},{1,3},{2,0},{3,1},{4,6},{5,7},{6,4},{7,5},{8,10},{9,11},{10,... | collective-permute-start | bytes 1622024 | tf_op jit(solution)/shard_map/ppermute | solution.py:313
  7.4 12.4 %collective-permute-start.24 = (bf16[272,256]{1,0:T(8,128)(2,1)S(1)}, bf16[272,256]{1,0:T(8,128)(2,1)S(1)}, u32[]{:S(2)}, u32[]{:S(2)}) collective-permute-start(bf16[272,256]{1,0:T(8,128)(2,1)S(1)} %get-tuple-element.177), channel_id=1, source_target_pairs={{0,4},{1,5},{2,6},{3,7},{4,12},{5,13},{6,14},{7,15},{12,8},{13,9},... | collective-permute-start | bytes 417800 | tf_op jit(solution)/shard_map/ppermute | solution.py:306
  10.1 11.4 %collective-permute-start.25 = (bf16[272,256]{1,0:T(8,128)(2,1)S(1)}, bf16[272,256]{1,0:T(8,128)(2,1)S(1)}, u32[]{:S(2)}, u32[]{:S(2)}) collective-permute-start(bf16[272,256]{1,0:T(8,128)(2,1)S(1)} %get-tuple-element.178), channel_id=1, source_target_pairs={{0,12},{1,13},{2,14},{3,15},{4,8},{5,9},{6,10},{7,11},{12,0},{13,1... | collective-permute-start | bytes 417800 | tf_op jit(solution)/shard_map/ppermute | solution.py:306
  10.1 11.4 %collective-permute-start.26 = (bf16[272,256]{1,0:T(8,128)(2,1)S(1)}, bf16[272,256]{1,0:T(8,128)(2,1)S(1)}, u32[]{:S(2)}, u32[]{:S(2)}) collective-permute-start(bf16[272,256]{1,0:T(8,128)(2,1)S(1)} %get-tuple-element.179), channel_id=1, source_target_pairs={{0,8},{1,9},{2,10},{3,11},{4,0},{5,1},{6,2},{7,3},{12,4},{13,5},{1... | collective-permute-start | bytes 417800 | tf_op jit(solution)/shard_map/ppermute | solution.py:306
  21.4 8.8 %collective-permute-start.27 = (bf16[1056,256]{1,0:T(8,128)(2,1)S(1)}, bf16[1056,256]{1,0:T(8,128)(2,1)S(1)}, u32[]{:S(2)}, u32[]{:S(2)}) collective-permute-start(bf16[1056,256]{1,0:T(8,128)(2,1)S(1)} %shard_map.65.x), channel_id=1, source_target_pairs={{0,1},{1,0},{2,3},{3,2},{4,5},{5,4},{6,7},{7,6},{8,9},{9,8},{10,11... | collective-permute-start | bytes 1622024 | tf_op jit(solution)/shard_map/ppermute | solution.py:313
  21.4 8.9 %collective-permute-start.28 = (bf16[1056,256]{1,0:T(8,128)(2,1)S(1)}, bf16[1056,256]{1,0:T(8,128)(2,1)S(1)}, u32[]{:S(2)}, u32[]{:S(2)}) collective-permute-start(bf16[1056,256]{1,0:T(8,128)(2,1)S(1)} %shard_map.67.x), channel_id=1, source_target_pairs={{0,1},{1,0},{2,3},{3,2},{4,5},{5,4},{6,7},{7,6},{8,9},{9,8},{10,11... | collective-permute-start | bytes 1622024 | tf_op jit(solution)/shard_map/ppermute | solution.py:313
  28.8 1.9 %collective-permute-start.31 = (bf16[1056,256]{1,0:T(8,128)(2,1)S(1)}, bf16[1056,256]{1,0:T(8,128)(2,1)S(1)}, u32[]{:S(2)}, u32[]{:S(2)}) collective-permute-start(bf16[1056,256]{1,0:T(8,128)(2,1)S(1)} %collective-permute-done.29.x), channel_id=1, source_target_pairs={{0,1},{1,0},{2,3},{3,2},{4,5},{5,4},{6,7},{7,6},{8,9},{9,8},{10,11... | collective-permute-start | bytes 1622024 | tf_op jit(solution)/shard_map/ppermute | solution.py:313
  28.8 2.7 %collective-permute-start.32 = (bf16[1056,256]{1,0:T(8,128)(2,1)S(1)}, bf16[1056,256]{1,0:T(8,128)(2,1)S(1)}, u32[]{:S(2)}, u32[]{:S(2)}) collective-permute-start(bf16[1056,256]{1,0:T(8,128)(2,1)S(1)} %collective-permute-done.30.x), channel_id=1, source_target_pairs={{0,1},{1,0},{2,3},{3,2},{4,5},{5,4},{6,7},{7,6},{8,9},{9,8},{10,11... | collective-permute-start | bytes 1622024 | tf_op jit(solution)/shard_map/ppermute | solution.py:313
  31.6 1.8 %copy-start.3 = (bf16[2,1024,256]{2,1,0:T(8,128)(2,1)S(1)}, bf16[2,1024,256]{2,1,0:T(8,128)(2,1)}, u32[]{:S(2)}) copy-start(bf16[2,1024,256]{2,1,0:T(8,128)(2,1)} %centres.3) | copy-start | bytes 3145732
  33.4 14.9 %collective-permute-start.5 = (bf16[128,1024]{1,0:T(8,128)(2,1)S(1)}, bf16[128,1024]{1,0:T(8,128)(2,1)S(1)}, u32[]{:S(2)}, u32[]{:S(2)}) collective-permute-start(bf16[128,1024]{1,0:T(8,128)(2,1)S(1)} %get-tuple-element.94.refs_6_), channel_id=1, source_target_pairs={{0,4},{1,5},{2,6},{3,7},{4,12},{5,13},{6,14},{7,15},{12,8},{13,9},... | collective-permute-start | bytes 786440 | tf_op jit(solution)/shard_map/cond/branch_0_fun/ppermute | solution.py:306
  36.0 12.4 %collective-permute-start.6 = (bf16[128,1024]{1,0:T(8,128)(2,1)S(1)}, bf16[128,1024]{1,0:T(8,128)(2,1)S(1)}, u32[]{:S(2)}, u32[]{:S(2)}) collective-permute-start(bf16[128,1024]{1,0:T(8,128)(2,1)S(1)} %get-tuple-element.95.refs_7_), channel_id=1, source_target_pairs={{0,4},{1,5},{2,6},{3,7},{12,8},{13,9},{14,10},{15,11},{16,20},{17,... | collective-permute-start | bytes 786440 | tf_op jit(solution)/shard_map/cond/branch_0_fun/ppermute | solution.py:306
  37.3 14.5 %collective-permute-start.4 = (bf16[1088,256]{1,0:T(8,128)(2,1)S(1)}, bf16[1088,256]{1,0:T(8,128)(2,1)S(1)}, u32[]{:S(2)}, u32[]{:S(2)}) collective-permute-start(bf16[1088,256]{1,0:T(8,128)(2,1)S(1)} %get-tuple-element.79.blocks), channel_id=1, source_target_pairs={{0,2},{1,3},{2,0},{3,1},{4,6},{5,7},{6,4},{7,5},{8,10},{9,11},{10,... | collective-permute-start | bytes 1671176 | tf_op jit(solution)/shard_map/cond/branch_0_fun/ppermute | solution.py:313
  44.3 21.7 %collective-permute-start = (bf16[128,1024]{1,0:T(8,128)(2,1)S(1)}, bf16[128,1024]{1,0:T(8,128)(2,1)S(1)}, u32[]{:S(2)}, u32[]{:S(2)}) collective-permute-start(bf16[128,1024]{1,0:T(8,128)(2,1)S(1)} %get-tuple-element.90.refs_2_), channel_id=1, source_target_pairs={{0,8},{1,9},{2,10},{3,11},{4,0},{5,1},{6,2},{7,3},{12,4},{13,5},{1... | collective-permute-start | bytes 786440 | tf_op jit(solution)/shard_map/cond/branch_0_fun/ppermute | solution.py:306
  47.0 19.0 %collective-permute-start.1 = (bf16[128,1024]{1,0:T(8,128)(2,1)S(1)}, bf16[128,1024]{1,0:T(8,128)(2,1)S(1)}, u32[]{:S(2)}, u32[]{:S(2)}) collective-permute-start(bf16[128,1024]{1,0:T(8,128)(2,1)S(1)} %get-tuple-element.91.refs_3_), channel_id=1, source_target_pairs={{0,8},{1,9},{2,10},{3,11},{12,4},{13,5},{14,6},{15,7},{16,24},{17,... | collective-permute-start | bytes 786440 | tf_op jit(solution)/shard_map/cond/branch_0_fun/ppermute | solution.py:306
  48.3 28.2 %collective-permute-start.2 = (bf16[128,1024]{1,0:T(8,128)(2,1)S(1)}, bf16[128,1024]{1,0:T(8,128)(2,1)S(1)}, u32[]{:S(2)}, u32[]{:S(2)}) collective-permute-start(bf16[128,1024]{1,0:T(8,128)(2,1)S(1)} %get-tuple-element.92.refs_4_), channel_id=1, source_target_pairs={{0,12},{1,13},{2,14},{3,15},{4,8},{5,9},{6,10},{7,11},{12,0},{13,1... | collective-permute-start | bytes 786440 | tf_op jit(solution)/shard_map/cond/branch_0_fun/ppermute | solution.py:306
  48.4 28.1 %collective-permute-start.3 = (bf16[128,1024]{1,0:T(8,128)(2,1)S(1)}, bf16[128,1024]{1,0:T(8,128)(2,1)S(1)}, u32[]{:S(2)}, u32[]{:S(2)}) collective-permute-start(bf16[128,1024]{1,0:T(8,128)(2,1)S(1)} %get-tuple-element.93.refs_5_), channel_id=1, source_target_pairs={{0,12},{1,13},{2,14},{3,15},{12,0},{13,1},{14,2},{15,3},{16,28},{1... | collective-permute-start | bytes 786440 | tf_op jit(solution)/shard_map/cond/branch_0_fun/ppermute | solution.py:306
  66.0 12.8 %collective-permute-start.7 = (bf16[2,1040,256]{2,1,0:T(8,128)(2,1)S(1)}, bf16[2,1040,256]{2,1,0:T(8,128)(2,1)S(1)}, u32[]{:S(2)}, u32[]{:S(2)}) collective-permute-start(bf16[2,1040,256]{2,1,0:T(8,128)(2,1)S(1)} %get-tuple-element.102), channel_id=1, source_target_pairs={{0,1},{1,0},{2,3},{3,2},{4,5},{5,4},{6,7},{7,6},{8,9},{9,8},{10,11... | collective-permute-start | bytes 3194888 | tf_op jit(solution)/shard_map/cond/branch_0_fun/ppermute | solution.py:313

commit v4 on v3

--- a/solution.py
+++ b/solution.py
@@ -44,18 +44,10 @@
     return jnp.where(lane < 128, lane >> 4, lane - 128)
 
 
-def ring_place(group):
-    for shift in (1, 2, 4, 8):
-        group = group ^ (group >> shift)
-    return group
-
-
 def pack_body(groups, rows, here, labels, codes, *outs):
     frames, width = codes.shape
     group, place = here[0] // GRP, here[0] % GRP
-    wide = jnp.broadcast_to(labels[...], (8, frames))
-    steps = (ring_place(wide >> 3) - ring_place(group)) & (groups - 1)
-    kr = steps * 8 + ((wide & 7) ^ (place * 2))
+    kr = jnp.broadcast_to(labels[...], (8, frames)) ^ (group * 8 + place * 2)
     kc = kr.T[:, 0:1]
     kr = kr[0:1, :]
     lane = lax.broadcasted_iota(jnp.int32, (1, frames), 1)
@@ -88,20 +80,21 @@
 def busy_body(groups, rows, here, *refs):
     out = refs[groups]
     lane = lax.broadcasted_iota(jnp.int32, (1, refs[0].shape[1]), 1)
-    place = ring_place(here[0] // GRP)
+    group = here[0] // GRP
     flags = [0, 0]
     for d in range(groups):
         most = jnp.zeros(lane.shape, F32)
         for s in range(groups):
             counts = refs[s][rows:, :].astype(F32)[2:3, :]
-            most = jnp.maximum(most, jnp.where(lane == (d + s) % groups, counts, 0.0))
+            most = jnp.maximum(most, jnp.where(lane == d ^ s, counts, 0.0))
         flag = (jnp.max(most) > float(rows // 2)).astype(jnp.int32)
-        flags[d % 2] = flags[d % 2] | flag
-    odd = place & 1
-    own, other = flags
-    even = jnp.where(odd == 0, own, other)
-    uneven = jnp.where(odd == 0, other, own)
-    out[0] = jnp.where(uneven == 0, 0, jnp.where(even == 0, 1, 2))
+        side = (d ^ (d >> 1)) & 1
+        flags[side] = flags[side] | flag
+    between = (group ^ (group >> 1)) & 1
+    same, other = flags
+    outer = jnp.where(between == 0, same, other)
+    inner = jnp.where(between == 0, other, same)
+    out[0] = jnp.where(inner == 0, 0, jnp.where(outer == 0, 1, 2))
 
 
 def share_body(c, sharp, centres, out):
@@ -186,23 +179,26 @@
     halve(soft_rows(block, rows, 0, refs[:count], outs[0].shape[1]), outs)
 
 
-def softs_body(rows, count, last, blocks, *refs):
+def softs_body(rows, count, order, blocks, *refs):
     outs = refs[count:]
-    each = len(outs) // (last + 1)
+    each = len(outs) // len(order)
     step = rows + META
 
     def one(n, _):
-        block = blocks[pl.ds(pl.multiple_of((last - n) * step, 16), step), :]
+        k = 0
+        for m, number in enumerate(order):
+            k = jnp.where(n == m, number, k)
+        block = blocks[pl.ds(pl.multiple_of(k * step, 16), step), :]
         values = soft_rows(block, rows, 0, refs[:count], outs[0].shape[1])
-        for k in range(last + 1):
-
-            @pl.when(n == last - k)
-            def _(k=k):
-                halve(values, outs[k * each : (k + 1) * each])
+        for m in range(len(order)):
+
+            @pl.when(n == m)
+            def _(m=m):
+                halve(values, outs[m * each : (m + 1) * each])
 
         return 0
 
-    lax.fori_loop(0, last + 1, one, 0)
+    lax.fori_loop(0, len(order), one, 0)
 
 
 def other_body(groups, rows, blocks, *refs):
@@ -218,48 +214,63 @@
     lax.fori_loop(0, groups, one, 0)
 
 
-def sums_body(groups, rows, blocks, others, soft, centres, *refs):
-    *mine, out, mass_out, give, sums, masses = refs
-    each = len(mine) // groups
+def sums(rows, first, blocks, pieces, across, put):
     width = blocks.shape[1]
+    step = rows + META
+    count = blocks.shape[0] // step
+    lane = lax.broadcasted_iota(jnp.int32, (1, width), 1)
+    row = lax.broadcasted_iota(jnp.int32, (rows, 1), 0).astype(F32)
+    start = 0
+    for ref in pieces:
+        across[:, start : start + ref.shape[0]] = ref[...].T
+        start += ref.shape[0]
+
+    def one(c, _):
+        chosen = []
+        for n in range(count):
+            bounds = blocks[n * step + rows : (n + 1) * step, :].astype(F32)
+            ends = jnp.sum(jnp.where(lane == 128 + c + first, bounds, 0.0), axis=1, keepdims=True)
+            inside = (row >= ends[0:1, :]) & (row < ends[1:2, :])
+            chosen.append(blocks[n * step : n * step + rows, :] * inside.astype(F32).astype(BF))
+        put(c, jnp.dot(across[...], jnp.concatenate(chosen, axis=0), preferred_element_type=F32))
+        return 0
+
+    lax.fori_loop(0, 4, one, 0)
+    members = []
+    for n in range(count):
+        ends = blocks[n * step + rows : (n + 1) * step, :].astype(F32)[:, 128:256]
+        members.append(((row >= ends[0:1, :]) & (row < ends[1:2, :])).astype(F32).astype(BF))
+    masses = jnp.dot(across[...], jnp.concatenate(members, axis=0), preferred_element_type=F32).T
+    return masses[first : first + 4, :]
+
+
+def here_body(rows, blocks, *refs):
+    *pieces, out, mass_out, across = refs
+
+    def put(c, value):
+        out[c] = value
+
+    mass_out[...] = sums(rows, 0, blocks, pieces, across, put)
+
+
+def sums_body(rows, others, soft, centres, before, mass_before, out, mass_out, give, across, total):
+    width = others.shape[1]
     fine = soft.shape[1]
     count = fine // width
-    step = rows + META
-    dims = (((0,), (0,)), ((), ()))
-    lane = lax.broadcasted_iota(jnp.int32, (1, width), 1)
-    row = lax.broadcasted_iota(jnp.int32, (rows, 1), 0).astype(F32)
-
-    def one(c, _):
-        total, mass = 0.0, 0.0
-        for k in range(2 * groups):
-            source = blocks if k < groups else others
-            n = k % groups
-            codes = source[n * step : n * step + rows, :]
-            bounds = source[n * step + rows : (n + 1) * step, :].astype(F32)
-            r = c if k < groups else c + 4
-            ends = jnp.sum(jnp.where(lane == 128 + r, bounds, 0.0), axis=1, keepdims=True)
-            inside = ((row >= ends[0:1, :]) & (row < ends[1:2, :])).astype(F32).astype(BF)
-            if k >= groups:
-                values = soft[n * rows : (n + 1) * rows, :]
-            else:
-                values = [ref[...] for ref in mine[n * each : (n + 1) * each]]
-                values = values[0] if each == 1 else jnp.concatenate(values, axis=0)
-            chosen = codes * inside
-            total = total + lax.dot_general(chosen, values, dims, preferred_element_type=F32)
-            ones = jnp.broadcast_to(inside, (rows, META))
-            mass = mass + lax.dot_general(ones, values, dims, preferred_element_type=F32)
-        sums[c] = total.T
-        masses[c] = jnp.concatenate(
-            [mass[0:1, q * width : (q + 1) * width] for q in range(count)], axis=0
-        )
-        return 0
-
-    lax.fori_loop(0, 4, one, 0)
+
+    def put(c, value):
+        total[c] = before[c] + value
+
+    masses = mass_before[...] + sums(rows, 4, others, [soft], across, put)
     for n in range(2):
-        out[n] = sums[n] + centres[n].astype(F32)
-        mass_out[n] = masses[n] + 1.0
-        give[n, :fine, :] = sums[2 + n].astype(BF)
-        terms = [t.astype(F32) for t in three(masses[2 + n])]
+        out[n] = total[n] + centres[n].astype(F32)
+        give[n, :fine, :] = total[2 + n].astype(BF)
+        own, other = [
+            jnp.concatenate([masses[m : m + 1, q * width : (q + 1) * width] for q in range(count)], axis=0)
+            for m in (n, 2 + n)
+        ]
+        mass_out[n] = own + 1.0
+        terms = [t.astype(F32) for t in three(other)]
         rest = jnp.zeros((META - 3 * count, width), F32)
         give[n, fine:, :] = jnp.concatenate(terms + [rest], axis=0).astype(BF)
 
@@ -300,12 +311,9 @@
     per_device, fine, _ = centroids.shape
     groups = route // GRP
     rows = GRP * max(8, 2 * frames // route)
-    def turn(x, steps, places=range(groups)):
-        ring = [k ^ (k >> 1) for k in range(groups)]
-        pairs = [(ring[k], ring[(k + steps) % groups]) for k in places]
-        return lax.ppermute(
-            x, "route", [(GRP * a + m, GRP * b + m) for a, b in pairs for m in range(GRP)]
-        )
+    def turn(x, distance, places=range(groups)):
+        pairs = [(GRP * g + m, GRP * (g ^ distance) + m) for g in places for m in range(GRP)]
+        return lax.ppermute(x, "route", pairs)
 
     here = lax.axis_index("route").astype(jnp.int32).reshape(1)
 
@@ -358,54 +366,73 @@
     work = 2 * rows * fine * width * 2 * GRP
     held = [call(copy_body, jax.ShapeDtypeStruct(x.shape, BF), 1, 0, 0)(x) for x in (*own, *near, *far, *last)]
     half = jax.ShapeDtypeStruct((rows // halves, fine), BF)
-    top = groups - 1
-    first = call(
-        functools.partial(soft_body, rows, len(held)),
-        [half] * halves,
-        1 + len(held),
-        SCALE * work,
-        SCALE * GRP * per_device * fine * width * 2,
-    )(blocks[top], *held)
+    early = [1, 2] if groups > 2 else [1]
+    late = [k for k in range(groups - 1, -1, -1) if k not in early]
+    first = [
+        call(
+            functools.partial(soft_body, rows, len(held)),
+            [half] * halves if k > 1 else [jax.ShapeDtypeStruct((rows, fine), BF)],
+            1 + len(held),
+            SCALE * work,
+            SCALE * GRP * per_device * fine * width * 2,
+        )(blocks[k], *held)
+        for k in early
+    ]
 
     def refine(places, first, held, gathered, slot, centroids):
         others = swap(gathered, 2)
         out = call(
-            functools.partial(softs_body, rows, len(held), top - 1),
-            [half] * (halves * top),
+            functools.partial(softs_body, rows, len(held), late),
+            [half] * (halves * len(late)),
             1 + len(held),
-            SCALE * top * work,
+            SCALE * len(late) * work,
             SCALE * GRP * per_device * fine * width * 2,
         )(gathered, *held)
-        soft = {k: out[k * halves : (k + 1) * halves] for k in range(top)}
-        soft[top] = first
+        soft = dict(zip(early, first))
+        for n, k in enumerate(late):
+            soft[k] = out[n * halves : (n + 1) * halves]
         back = dict(soft)
-        for k in range(top, 0, -1):
-            back[k] = [turn(soft[k][0], -k)] + [turn(x, -k, places) for x in soft[k][1:]]
-        others, _, back[top] = lax.optimization_barrier((others, soft[0][0], back[top]))
+        for k in early + late:
+            if k:
+                back[k] = [turn(soft[k][0], k)] + [turn(x, k, places) for x in soft[k][1:]]
+        sums_shape = ((2 * per_device, fine, width), F32)
+        across = ((fine, groups * rows), BF)
+        work_sums = LIGHT * 8 * groups * rows * fine * width
+        before, mass_before = call(
+            functools.partial(here_body, rows),
+            [jax.ShapeDtypeStruct(*sums_shape), jax.ShapeDtypeStruct((2 * per_device, fine), F32)],
+            1 + sum(len(soft[k]) for k in range(groups)),
+            work_sums,
+            LIGHT * groups * rows * fine * 4,
+            scratch=[across],
+        )(gathered, *[x for k in range(groups) for x in soft[k]])
+        others, mass_before = lax.optimization_barrier((others, mass_before))
         other_soft = call(
             functools.partial(other_body, groups, rows),
             jax.ShapeDtypeStruct((groups * rows, fine), BF),
             1 + 2 * per_device,
-            LIGHT * 2 * groups * work,
-            LIGHT * groups * rows * fine * 2,
+            0,
+            0,
         )(others, *held[: 2 * per_device])
-        mass_shape = ((2 * per_device, fine // width, width), F32)
+        if groups > 2:
+            other_soft, back[2] = lax.optimization_barrier((other_soft, back[2]))
         mine, mass, give = call(
-            functools.partial(sums_body, groups, rows),
+            functools.partial(sums_body, rows),
             [
                 jax.ShapeDtypeStruct(centroids.shape, F32),
                 jax.ShapeDtypeStruct((per_device, fine // width, width), F32),
                 jax.ShapeDtypeStruct((per_device, fine + META, width), BF),
             ],
-            4 + halves * groups,
-            LIGHT * 16 * groups * rows * fine * width,
+            5,
+            work_sums,
             LIGHT * groups * rows * fine * 4,
-            scratch=[((2 * per_device, fine, width), F32), mass_shape],
-        )(gathered, others, other_soft, centroids, *[x for k in range(groups) for x in soft[k]])
+            scratch=[across, sums_shape],
+        )(others, other_soft, centroids, before, mass_before)
         got = swap(give, 1)
-        pieces = [
-            (k * rows + n * (rows // halves), x) for k in range(groups) for n, x in enumerate(back[k])
-        ]
+        pieces = []
+        for k in range(groups):
+            size = rows // len(back[k])
+            pieces += [(k * rows + n * size, x) for n, x in enumerate(back[k])]
         soft_labels = call(
             functools.partial(unpack_body, [start for start, _ in pieces]),
             jax.ShapeDtypeStruct((slot.shape[0], fine), BF),
@@ -426,7 +453,7 @@
     shared = (first, held, gathered, slot, centroids)
     if halves == 1:
         return refine(range(groups), *shared)
-    cases = [functools.partial(refine, c) for c in ((0, 2), (1, 3), range(groups))]
+    cases = [functools.partial(refine, c) for c in ((0, 3), (1, 2), range(groups))]
     return lax.switch(busy[0], cases, *shared)
 
 

time: 81.8 us -> 78.1 us (0.955); the launches traced: 80.8 us -> 77.9 us
  waiting for transfers between devices: 30 us -> 23.6 us
  starting transfers between devices: 18 us -> 20.7 us
    ppermute x9 -> x8, waiting for transfers between devices: 19.9 us -> 16.1 us  [turn(): return lax.ppermute(x, 'route', pairs)]
    ppermute x9 -> x8, starting transfers between devices: 13.2 us -> 16.1 us  [turn(): return lax.ppermute(x, 'route', pairs)]
    ppermute x8, waiting for transfers between devices: 10.1 us -> 7.56 us  [swap(): return lax.ppermute(x, 'route', [(r, r ^ mask) for r in range(route)])]
    pallas_call x3 -> x5, Pallas kernels: 16.3 us -> 16.9 us  [the longest x1 5.08 us: refine(): call(functools.partial(sums_body, rows), [jax.ShapeDtypeStruct(centroids....]
  transfers between devices with their start and end apart: 17 -> 16, of which waited for: 7 -> 8; matrix products, arithmetic and copies ran while one was open for 0% -> 0% of each run, Pallas kernels for 31% -> 30%
where the time goes in v4:
time: 78.1 us; the launch traced here: 77.9 us
  Pallas kernels  31 us (40%)
  waiting for transfers between devices  23.6 us (30%)
  starting transfers between devices  20.7 us (27%)
  between operations  1.48 us (2%)
  local copies, waits for them, and re-layouts  0.83 us (1%)
    ppermute x8, starting transfers between devices, turn(): return lax.ppermute(x, 'route', pairs)  16.1 us
    ppermute x8, waiting for transfers between devices, turn(): return lax.ppermute(x, 'route', pairs)  16.1 us
    ppermute x8, waiting for transfers between devices, swap(): return lax.ppermute(x, 'route', [(r, r ^ mask) for r in range(route)])  7.56 us
    pallas_call x1, Pallas kernels, refine(): call(functools.partial(sums_body, rows), [jax.ShapeDtypeStruct(centroids....  5.08 us
    pallas_call x1, Pallas kernels, refine(): call(functools.partial(other_body, groups, rows), jax.ShapeDtypeStruct((g...  5.02 us
    pallas_call x1, Pallas kernels, refine(): call(functools.partial(here_body, rows), [jax.ShapeDtypeStruct(*sums_shap...  4.78 us
    ppermute x8, starting transfers between devices, swap(): return lax.ppermute(x, 'route', [(r, r ^ mask) for r in range(route)])  4.55 us
    pallas_call x1, Pallas kernels, refine(): call(functools.partial(softs_body, rows, len(held), late), [half] * (halv...  3.59 us
  transfers between devices with their start and end apart: 16, of which 8 were waited for; matrix products, arithmetic and copies ran while one was open for 0% of the time, Pallas kernels for 30%

profile of v4, /device:TPU:8, one launch (start us, length us, event | category | flops | bytes accessed | tf_op | source)
XLA Modules:
  0.0 77.9 jit_solution(9048977809975415189)
XLA Ops:
  0.6 0.0 copy-start.1
  0.6 0.8 %copy.12.sharp = bf16[2,1]{1,0:T(2,128)(2,1)S(1)} copy(bf16[2,1]{0,1:T(2,128)(2,1)} %bitcast.5) | data formatting | bytes 8 | tf_op jit(solution)/shard_map/reshape | solution.py:323
  1.5 1.8 %shard_map.65.x = bf16[1056,256]{1,0:T(8,128)(2,1)S(1)} custom-call(bf16[2,1]{1,0:T(2,128)(2,1)S(1)} %copy.12.sharp, bf16[2,1024,256]{2,1,0:T(8,128)(2,1)} %centres.3), custom_call_target="tpu_custom_call" | custom-call | flops 41943040 | bytes 5242880 | tf_op jit(solution)/shard_map/pallas_call | solution.py:327
  3.2 1.6 %collective-permute-start.26 = (bf16[1056,256]{1,0:T(8,128)(2,1)S(1)}, bf16[1056,256]{1,0:T(8,128)(2,1)S(1)}, u32[]{:S(2)}, u32[]{:S(2)}) collective-permute-start(bf16[1056,256]{1,0:T(8,128)(2,1)S(1)} %shard_map.65.x), channel_id=1, source_target_pairs={{0,2},{1,3},{2,0},{3,1},{4,6},{5,7},{6,4},{7,5},{8,10},{9,11},{10,... | collective-permute-start | bytes 1622024 | tf_op jit(solution)/shard_map/ppermute | solution.py:321
  4.8 0.4 shard_map.67.x
  5.3 0.6 collective-permute-start.27
  5.8 1.6 %shard_map.66 = (bf16[272,256]{1,0:T(8,128)(2,1)S(1)}, bf16[272,256]{1,0:T(8,128)(2,1)S(1)}, bf16[272,256]{1,0:T(8,128)(2,1)S(1)}, bf16[272,256]{1,0:T(8,128)(2,1)S(1)}, s32[512,1]{1,0:T(8,128)S(1)}) custom-call(s32[1]{0:T(128)} %bitcast.here, s32[1,512]{1,0:T(1,128)S(1)} %bitcast.4, f32[512,256]{1,0:T(8,128)S(1)} %copy-done), custom_call_target="tpu_custom_call" | custom-call | flops 1342177280 | bytes 5242880 | tf_op jit(solution)/shard_map/pallas_call | solution.py:338
  7.5 0.1 collective-permute-start.21
  7.5 3.0 %collective-permute-start.22 = (bf16[272,256]{1,0:T(8,128)(2,1)S(1)}, bf16[272,256]{1,0:T(8,128)(2,1)S(1)}, u32[]{:S(2)}, u32[]{:S(2)}) collective-permute-start(bf16[272,256]{1,0:T(8,128)(2,1)S(1)} %get-tuple-element.193), channel_id=1, source_target_pairs={{0,8},{1,9},{2,10},{3,11},{4,12},{5,13},{6,14},{7,15},{8,0},{9,1},... | collective-permute-start | bytes 417800 | tf_op jit(solution)/shard_map/ppermute | solution.py:316
  10.6 0.4 collective-permute-start.23
  11.0 2.5 %collective-permute-done.21.refs_1_.block = bf16[272,256]{1,0:T(8,128)(2,1)S(1)} collective-permute-done((bf16[272,256]{1,0:T(8,128)(2,1)S(1)}, bf16[272,256]{1,0:T(8,128)(2,1)S(1)}, u32[]{:S(2)}, u32[]{:S(2)}) %collective-permute-start.21) | collective-permute-done | bytes 139296 | tf_op jit(solution)/shard_map/ppermute | solution.py:316
  13.5 6.6 %collective-permute-done.22.refs_2_.block = bf16[272,256]{1,0:T(8,128)(2,1)S(1)} collective-permute-done((bf16[272,256]{1,0:T(8,128)(2,1)S(1)}, bf16[272,256]{1,0:T(8,128)(2,1)S(1)}, u32[]{:S(2)}, u32[]{:S(2)}) %collective-permute-start.22) | collective-permute-done | bytes 139296 | tf_op jit(solution)/shard_map/ppermute | solution.py:316
  20.1 2.4 %collective-permute-done.23.refs_3_ = bf16[272,256]{1,0:T(8,128)(2,1)S(1)} collective-permute-done((bf16[272,256]{1,0:T(8,128)(2,1)S(1)}, bf16[272,256]{1,0:T(8,128)(2,1)S(1)}, u32[]{:S(2)}, u32[]{:S(2)}) %collective-permute-start.23) | collective-permute-done | bytes 139296 | tf_op jit(solution)/shard_map/ppermute | solution.py:316
  22.6 0.0 collective-permute-start.24
  22.6 0.5 collective-permute-start.25
  23.1 0.7 shard_map.68
  23.7 0.0 collective-permute-done.26.x
  23.7 0.1 collective-permute-start.28
  23.8 5.1 %collective-permute-done.27.x = bf16[1056,256]{1,0:T(8,128)(2,1)S(1)} collective-permute-done((bf16[1056,256]{1,0:T(8,128)(2,1)S(1)}, bf16[1056,256]{1,0:T(8,128)(2,1)S(1)}, u32[]{:S(2)}, u32[]{:S(2)}) %collective-permute-start.27) | collective-permute-done | bytes 540704 | tf_op jit(solution)/shard_map/ppermute | solution.py:321
  28.9 0.0 collective-permute-start.29
  29.8 0.0 collective-permute-done.24.x
  29.8 0.0 collective-permute-done.25.x
  29.9 0.0 collective-permute-done.28.x
  29.9 0.9 %collective-permute-done.29.x = bf16[1056,256]{1,0:T(8,128)(2,1)S(1)} collective-permute-done((bf16[1056,256]{1,0:T(8,128)(2,1)S(1)}, bf16[1056,256]{1,0:T(8,128)(2,1)S(1)}, u32[]{:S(2)}, u32[]{:S(2)}) %collective-permute-start.29) | collective-permute-done | bytes 540704 | tf_op jit(solution)/shard_map/ppermute | solution.py:321
  30.9 1.7 %shard_map.77 = bf16[256,1024]{1,0:T(8,128)(2,1)S(1)} custom-call(bf16[272,256]{1,0:T(8,128)(2,1)S(1)} %collective-permute-done.21.refs_1_.block, bf16[1056,256]{1,0:T(8,128)(2,1)S(1)} %shard_map.69.refs_0_, bf16[1056,256]{1,0:T(8,128)(2,1)S(1)} %shard_map.70.refs_1_, bf16[1056,256]{1,0:T(8,128)(2,1)S(1)} %shard_map.71.refs_2_, ...), custom_call_target="tpu_custom_call" | custom-call | flops 5368709120 | bytes 20971520 | tf_op jit(solution)/shard_map/pallas_call | solution.py:372
  32.6 0.0 copy-start.3
  32.6 1.7 %shard_map.78 = (bf16[128,1024]{1,0:T(8,128)(2,1)S(1)}, bf16[128,1024]{1,0:T(8,128)(2,1)S(1)}) custom-call(bf16[272,256]{1,0:T(8,128)(2,1)S(1)} %collective-permute-done.22.refs_2_.block, bf16[1056,256]{1,0:T(8,128)(2,1)S(1)} %shard_map.69.refs_0_, bf16[1056,256]{1,0:T(8,128)(2,1)S(1)} %shard_map.70.refs_1_, bf16[1056,256]{1,0:T(8,128)(2,1)S(1)} %shard_map.71.refs_2_, ...), custom_call_target="tpu_custom_call" | custom-call | flops 5368709120 | bytes 20971520 | tf_op jit(solution)/shard_map/pallas_call | solution.py:372
  34.4 43.5 %conditional.1 = (bf16[512,1024]{1,0:T(8,128)(2,1)}, f32[2,1024,256]{2,1,0:T(8,128)}) conditional(s32[]{:T(128)} %bitcast.3, (bf16[1088,256]{1,0:T(8,128)(2,1)S(1)}, bf16[1056,256]{1,0:T(8,128)(2,1)S(1)}, bf16[1056,256]{1,0:T(8,128)(2,1)S(1)}, bf16[1056,256]{1,0:T(8,128)(2,1)S(1)}, bf16[1056,256]{1,0:T(8,128)(2,1)S(1)}, ...), branch_computations={%region_0.0_spmd, %region_1.0_spmd, %region_2.0_spmd} | conditional | flops 68721573888 | bytes 257098000 | solution.py:457
  34.6 0.3 collective-permute-start.7
  34.9 1.7 %collective-permute-start.8 = (bf16[1088,256]{1,0:T(8,128)(2,1)S(1)}, bf16[1088,256]{1,0:T(8,128)(2,1)S(1)}, u32[]{:S(2)}, u32[]{:S(2)}) collective-permute-start(bf16[1088,256]{1,0:T(8,128)(2,1)S(1)} %get-tuple-element.113.blocks), channel_id=1, source_target_pairs={{0,2},{1,3},{2,0},{3,1},{4,6},{5,7},{6,4},{7,5},{8,10},{9,11},{10,... | collective-permute-start | bytes 1671176 | tf_op jit(solution)/shard_map/cond/branch_1_fun/ppermute | solution.py:321
  36.7 2.6 %collective-permute-start.9 = (bf16[128,1024]{1,0:T(8,128)(2,1)S(1)}, bf16[128,1024]{1,0:T(8,128)(2,1)S(1)}, u32[]{:S(2)}, u32[]{:S(2)}) collective-permute-start(bf16[128,1024]{1,0:T(8,128)(2,1)S(1)} %get-tuple-element.125.refs_3_), channel_id=1, source_target_pairs={{0,8},{1,9},{2,10},{3,11},{4,12},{5,13},{6,14},{7,15},{8,0},{9,1},... | collective-permute-start | bytes 786440 | tf_op jit(solution)/shard_map/cond/branch_1_fun/ppermute | solution.py:316
  39.3 2.2 %collective-permute-start.10 = (bf16[128,1024]{1,0:T(8,128)(2,1)S(1)}, bf16[128,1024]{1,0:T(8,128)(2,1)S(1)}, u32[]{:S(2)}, u32[]{:S(2)}) collective-permute-start(bf16[128,1024]{1,0:T(8,128)(2,1)S(1)} %get-tuple-element.126.refs_4_), channel_id=1, source_target_pairs={{4,12},{5,13},{6,14},{7,15},{8,0},{9,1},{10,2},{11,3},{20,28},{21,... | collective-permute-start | bytes 786440 | tf_op jit(solution)/shard_map/cond/branch_1_fun/ppermute | solution.py:316
  41.5 3.6 %branch_1_fun.6 = (bf16[128,1024]{1,0:T(8,128)(2,1)S(1)}, bf16[128,1024]{1,0:T(8,128)(2,1)S(1)}, bf16[128,1024]{1,0:T(8,128)(2,1)S(1)}, bf16[128,1024]{1,0:T(8,128)(2,1)S(1)}) custom-call(bf16[1088,256]{1,0:T(8,128)(2,1)S(1)} %get-tuple-element.113.blocks, bf16[1056,256]{1,0:T(8,128)(2,1)S(1)} %get-tuple-element.114.refs_0_, ...), custom_call_target="tpu_custom_call" | custom-call | flops 10737418240 | bytes 20971520 | tf_op jit(solution)/shard_map/cond/branch_1_fun/pallas_call | solution.py:384
  45.1 2.8 %collective-permute-start.11 = (bf16[128,1024]{1,0:T(8,128)(2,1)S(1)}, bf16[128,1024]{1,0:T(8,128)(2,1)S(1)}, u32[]{:S(2)}, u32[]{:S(2)}) collective-permute-start(bf16[128,1024]{1,0:T(8,128)(2,1)S(1)} %get-tuple-element.127.refs_5_), channel_id=1, source_target_pairs={{0,12},{1,13},{2,14},{3,15},{4,8},{5,9},{6,10},{7,11},{8,4},{9,5},... | collective-permute-start | bytes 786440 | tf_op jit(solution)/shard_map/cond/branch_1_fun/ppermute | solution.py:316
  47.9 1.6 %collective-permute-done.8.blocks.others = bf16[1088,256]{1,0:T(8,128)(2,1)S(1)} collective-permute-done((bf16[1088,256]{1,0:T(8,128)(2,1)S(1)}, bf16[1088,256]{1,0:T(8,128)(2,1)S(1)}, u32[]{:S(2)}, u32[]{:S(2)}) %collective-permute-start.8) | collective-permute-done | bytes 557088 | tf_op jit(solution)/shard_map/cond/branch_1_fun/ppermute | solution.py:321
  49.5 4.7 %collective-permute-start.12 = (bf16[128,1024]{1,0:T(8,128)(2,1)S(1)}, bf16[128,1024]{1,0:T(8,128)(2,1)S(1)}, u32[]{:S(2)}, u32[]{:S(2)}) collective-permute-start(bf16[128,1024]{1,0:T(8,128)(2,1)S(1)} %get-tuple-element.128.refs_6_), channel_id=1, source_target_pairs={{4,8},{5,9},{6,10},{7,11},{8,4},{9,5},{10,6},{11,7},{20,24},{21,25... | collective-permute-start | bytes 786440 | tf_op jit(solution)/shard_map/cond/branch_1_fun/ppermute | solution.py:316
  54.2 4.8 %branch_1_fun.7 = (f32[4,1024,256]{2,1,0:T(8,128)S(1)}, f32[4,1024]{1,0:T(4,128)S(1)}) custom-call(bf16[1088,256]{1,0:T(8,128)(2,1)S(1)} %get-tuple-element.113.blocks, bf16[128,1024]{1,0:T(8,128)(2,1)S(1)} %get-tuple-element.122.refs_0_, bf16[128,1024]{1,0:T(8,128)(2,1)S(1)} %get-tuple-element.123.refs_1_, ...), custom_call_target="tpu_custom_call" | custom-call | flops 2147483648 | bytes 4194304 | tf_op jit(solution)/shard_map/cond/branch_1_fun/pallas_call | solution.py:401
  58.9 5.0 %branch_1_fun.8.soft = bf16[1024,1024]{1,0:T(8,128)(2,1)S(1)} custom-call(bf16[1088,256]{1,0:T(8,128)(2,1)S(1)} %collective-permute-done.8.blocks.others, bf16[1056,256]{1,0:T(8,128)(2,1)S(1)} %get-tuple-element.114.refs_0_, bf16[1056,256]{1,0:T(8,128)(2,1)S(1)} %get-tuple-element.115.refs_1_, bf16[1056,256]{1,0:T(8,128)(2,1)S(1)} %get-tuple-element.116.refs_2_, ...), custom_call_target="tpu_custom_call" | custom-call | tf_op jit(solution)/shard_map/cond/branch_1_fun/pallas_call | solution.py:410
  64.0 0.0 collective-permute-done.9.refs_3_
  64.0 0.0 collective-permute-done.10.refs_4_
  64.0 5.1 %branch_1_fun.10 = (f32[2,1024,256]{2,1,0:T(8,128)S(1)}, f32[2,4,256]{2,1,0:T(4,128)S(1)}, bf16[2,1040,256]{2,1,0:T(8,128)(2,1)S(1)}) custom-call(bf16[1088,256]{1,0:T(8,128)(2,1)S(1)} %collective-permute-done.8.blocks.others, bf16[1024,1024]{1,0:T(8,128)(2,1)S(1)} %branch_1_fun.8.soft, bf16[2,1024,256]{2,1,0:T(8,128)(2,1)S(1)} %get-tuple-element.134.centres, ...), custom_call_target="tpu_custom_call" | custom-call | flops 2147483648 | bytes 4194304 | tf_op jit(solution)/shard_map/cond/branch_1_fun/pallas_call | solution.py:419
  69.1 0.1 collective-permute-start.13
  69.1 0.3 collective-permute-done.11.refs_5_
  69.4 4.2 %collective-permute-done.12.refs_6_ = bf16[128,1024]{1,0:T(8,128)(2,1)S(1)} collective-permute-done((bf16[128,1024]{1,0:T(8,128)(2,1)S(1)}, bf16[128,1024]{1,0:T(8,128)(2,1)S(1)}, u32[]{:S(2)}, u32[]{:S(2)}) %collective-permute-start.12) | collective-permute-done | bytes 262176 | tf_op jit(solution)/shard_map/cond/branch_1_fun/ppermute | solution.py:316
  73.7 0.0 collective-permute-done.7.refs_2_
  73.7 2.3 %branch_1_fun.9 = bf16[512,1024]{1,0:T(8,128)(2,1)} custom-call(s32[512,1]{1,0:T(8,128)S(1)} %get-tuple-element.112.slot, bf16[128,1024]{1,0:T(8,128)(2,1)S(1)} %get-tuple-element.122.refs_0_, bf16[128,1024]{1,0:T(8,128)(2,1)S(1)} %get-tuple-element.123.refs_1_, bf16[256,1024]{1,0:T(8,128)(2,1)S(1)} %collective-permute-done.7.refs_2_, ...), custom_call_target="tpu_custom_call" | custom-call | flops 53687091200 | bytes 209715200 | tf_op jit(solution)/shard_map/cond/branch_1_fun/pallas_call | solution.py:436
  75.9 0.0 collective-permute-done.13.got
  75.9 2.0 %branch_1_fun.11 = f32[2,1024,256]{2,1,0:T(8,128)} custom-call(f32[2,1024,256]{2,1,0:T(8,128)S(1)} %get-tuple-element.137.mine, f32[2,4,256]{2,1,0:T(4,128)S(1)} %get-tuple-element.138.mass, bf16[2,1040,256]{2,1,0:T(8,128)(2,1)S(1)} %collective-permute-done.13.got), custom_call_target="tpu_custom_call" | custom-call | flops 2097152 | bytes 5242880 | tf_op jit(solution)/shard_map/cond/branch_1_fun/pallas_call | solution.py:443
  (15 shorter events, 0.3 us)
Async XLA Ops:
  0.6 5.2 %copy-start.1 = (s32[512]{0:T(512)S(1)}, s32[512]{0:T(512)}, u32[]{:S(2)}) copy-start(s32[512]{0:T(512)} %param.8) | copy-start | bytes 6148
  0.6 5.2 %copy-start = (f32[512,256]{1,0:T(8,128)S(1)}, f32[512,256]{1,0:T(8,128)}, u32[]{:S(2)}) copy-start(f32[512,256]{1,0:T(8,128)} %codes.1) | copy-start | bytes 1572868
  1.5 3.4 %copy-start.2 = (bf16[2,1024,256]{2,1,0:T(8,128)(2,1)S(1)}, bf16[2,1024,256]{2,1,0:T(8,128)(2,1)}, u32[]{:S(2)}) copy-start(bf16[2,1024,256]{2,1,0:T(8,128)(2,1)} %centres.3) | copy-start | bytes 3145732
  3.2 20.5 %collective-permute-start.26 = (bf16[1056,256]{1,0:T(8,128)(2,1)S(1)}, bf16[1056,256]{1,0:T(8,128)(2,1)S(1)}, u32[]{:S(2)}, u32[]{:S(2)}) collective-permute-start(bf16[1056,256]{1,0:T(8,128)(2,1)S(1)} %shard_map.65.x), channel_id=1, source_target_pairs={{0,2},{1,3},{2,0},{3,1},{4,6},{5,7},{6,4},{7,5},{8,10},{9,11},{10,... | collective-permute-start | bytes 1622024 | tf_op jit(solution)/shard_map/ppermute | solution.py:321
  5.3 23.6 %collective-permute-start.27 = (bf16[1056,256]{1,0:T(8,128)(2,1)S(1)}, bf16[1056,256]{1,0:T(8,128)(2,1)S(1)}, u32[]{:S(2)}, u32[]{:S(2)}) collective-permute-start(bf16[1056,256]{1,0:T(8,128)(2,1)S(1)} %shard_map.67.x), channel_id=1, source_target_pairs={{0,2},{1,3},{2,0},{3,1},{4,6},{5,7},{6,4},{7,5},{8,10},{9,11},{10,... | collective-permute-start | bytes 1622024 | tf_op jit(solution)/shard_map/ppermute | solution.py:321
  7.5 6.1 %collective-permute-start.21 = (bf16[272,256]{1,0:T(8,128)(2,1)S(1)}, bf16[272,256]{1,0:T(8,128)(2,1)S(1)}, u32[]{:S(2)}, u32[]{:S(2)}) collective-permute-start(bf16[272,256]{1,0:T(8,128)(2,1)S(1)} %get-tuple-element.192), channel_id=1, source_target_pairs={{0,4},{1,5},{2,6},{3,7},{4,0},{5,1},{6,2},{7,3},{8,12},{9,13},{10,... | collective-permute-start | bytes 417800 | tf_op jit(solution)/shard_map/ppermute | solution.py:316
  7.5 12.6 %collective-permute-start.22 = (bf16[272,256]{1,0:T(8,128)(2,1)S(1)}, bf16[272,256]{1,0:T(8,128)(2,1)S(1)}, u32[]{:S(2)}, u32[]{:S(2)}) collective-permute-start(bf16[272,256]{1,0:T(8,128)(2,1)S(1)} %get-tuple-element.193), channel_id=1, source_target_pairs={{0,8},{1,9},{2,10},{3,11},{4,12},{5,13},{6,14},{7,15},{8,0},{9,1},... | collective-permute-start | bytes 417800 | tf_op jit(solution)/shard_map/ppermute | solution.py:316
  10.6 12.0 %collective-permute-start.23 = (bf16[272,256]{1,0:T(8,128)(2,1)S(1)}, bf16[272,256]{1,0:T(8,128)(2,1)S(1)}, u32[]{:S(2)}, u32[]{:S(2)}) collective-permute-start(bf16[272,256]{1,0:T(8,128)(2,1)S(1)} %get-tuple-element.194), channel_id=1, source_target_pairs={{0,12},{1,13},{2,14},{3,15},{4,8},{5,9},{6,10},{7,11},{8,4},{9,5},... | collective-permute-start | bytes 417800 | tf_op jit(solution)/shard_map/ppermute | solution.py:316
  22.6 7.2 %collective-permute-start.24 = (bf16[1056,256]{1,0:T(8,128)(2,1)S(1)}, bf16[1056,256]{1,0:T(8,128)(2,1)S(1)}, u32[]{:S(2)}, u32[]{:S(2)}) collective-permute-start(bf16[1056,256]{1,0:T(8,128)(2,1)S(1)} %shard_map.65.x), channel_id=1, source_target_pairs={{0,1},{1,0},{2,3},{3,2},{4,5},{5,4},{6,7},{7,6},{8,9},{9,8},{10,11... | collective-permute-start | bytes 1622024 | tf_op jit(solution)/shard_map/ppermute | solution.py:321
  22.6 7.3 %collective-permute-start.25 = (bf16[1056,256]{1,0:T(8,128)(2,1)S(1)}, bf16[1056,256]{1,0:T(8,128)(2,1)S(1)}, u32[]{:S(2)}, u32[]{:S(2)}) collective-permute-start(bf16[1056,256]{1,0:T(8,128)(2,1)S(1)} %shard_map.67.x), channel_id=1, source_target_pairs={{0,1},{1,0},{2,3},{3,2},{4,5},{5,4},{6,7},{7,6},{8,9},{9,8},{10,11... | collective-permute-start | bytes 1622024 | tf_op jit(solution)/shard_map/ppermute | solution.py:321
  23.7 6.1 %collective-permute-start.28 = (bf16[1056,256]{1,0:T(8,128)(2,1)S(1)}, bf16[1056,256]{1,0:T(8,128)(2,1)S(1)}, u32[]{:S(2)}, u32[]{:S(2)}) collective-permute-start(bf16[1056,256]{1,0:T(8,128)(2,1)S(1)} %collective-permute-done.26.x), channel_id=1, source_target_pairs={{0,1},{1,0},{2,3},{3,2},{4,5},{5,4},{6,7},{7,6},{8,9},{9,8},{10,11... | collective-permute-start | bytes 1622024 | tf_op jit(solution)/shard_map/ppermute | solution.py:321
  28.9 1.9 %collective-permute-start.29 = (bf16[1056,256]{1,0:T(8,128)(2,1)S(1)}, bf16[1056,256]{1,0:T(8,128)(2,1)S(1)}, u32[]{:S(2)}, u32[]{:S(2)}) collective-permute-start(bf16[1056,256]{1,0:T(8,128)(2,1)S(1)} %collective-permute-done.27.x), channel_id=1, source_target_pairs={{0,1},{1,0},{2,3},{3,2},{4,5},{5,4},{6,7},{7,6},{8,9},{9,8},{10,11... | collective-permute-start | bytes 1622024 | tf_op jit(solution)/shard_map/ppermute | solution.py:321
  32.6 1.8 %copy-start.3 = (bf16[2,1024,256]{2,1,0:T(8,128)(2,1)S(1)}, bf16[2,1024,256]{2,1,0:T(8,128)(2,1)}, u32[]{:S(2)}) copy-start(bf16[2,1024,256]{2,1,0:T(8,128)(2,1)} %centres.3) | copy-start | bytes 3145732
  34.6 39.0 %collective-permute-start.7 = (bf16[256,1024]{1,0:T(8,128)(2,1)S(1)}, bf16[256,1024]{1,0:T(8,128)(2,1)S(1)}, u32[]{:S(2)}, u32[]{:S(2)}) collective-permute-start(bf16[256,1024]{1,0:T(8,128)(2,1)S(1)} %get-tuple-element.124.refs_2_), channel_id=1, source_target_pairs={{0,4},{1,5},{2,6},{3,7},{4,0},{5,1},{6,2},{7,3},{8,12},{9,13},{10,... | collective-permute-start | bytes 1572872 | tf_op jit(solution)/shard_map/cond/branch_1_fun/ppermute | solution.py:316
  34.9 14.5 %collective-permute-start.8 = (bf16[1088,256]{1,0:T(8,128)(2,1)S(1)}, bf16[1088,256]{1,0:T(8,128)(2,1)S(1)}, u32[]{:S(2)}, u32[]{:S(2)}) collective-permute-start(bf16[1088,256]{1,0:T(8,128)(2,1)S(1)} %get-tuple-element.113.blocks), channel_id=1, source_target_pairs={{0,2},{1,3},{2,0},{3,1},{4,6},{5,7},{6,4},{7,5},{8,10},{9,11},{10,... | collective-permute-start | bytes 1671176 | tf_op jit(solution)/shard_map/cond/branch_1_fun/ppermute | solution.py:321
  36.7 27.3 %collective-permute-start.9 = (bf16[128,1024]{1,0:T(8,128)(2,1)S(1)}, bf16[128,1024]{1,0:T(8,128)(2,1)S(1)}, u32[]{:S(2)}, u32[]{:S(2)}) collective-permute-start(bf16[128,1024]{1,0:T(8,128)(2,1)S(1)} %get-tuple-element.125.refs_3_), channel_id=1, source_target_pairs={{0,8},{1,9},{2,10},{3,11},{4,12},{5,13},{6,14},{7,15},{8,0},{9,1},... | collective-permute-start | bytes 786440 | tf_op jit(solution)/shard_map/cond/branch_1_fun/ppermute | solution.py:316
  39.3 24.7 %collective-permute-start.10 = (bf16[128,1024]{1,0:T(8,128)(2,1)S(1)}, bf16[128,1024]{1,0:T(8,128)(2,1)S(1)}, u32[]{:S(2)}, u32[]{:S(2)}) collective-permute-start(bf16[128,1024]{1,0:T(8,128)(2,1)S(1)} %get-tuple-element.126.refs_4_), channel_id=1, source_target_pairs={{4,12},{5,13},{6,14},{7,15},{8,0},{9,1},{10,2},{11,3},{20,28},{21,... | collective-permute-start | bytes 786440 | tf_op jit(solution)/shard_map/cond/branch_1_fun/ppermute | solution.py:316
  45.1 24.3 %collective-permute-start.11 = (bf16[128,1024]{1,0:T(8,128)(2,1)S(1)}, bf16[128,1024]{1,0:T(8,128)(2,1)S(1)}, u32[]{:S(2)}, u32[]{:S(2)}) collective-permute-start(bf16[128,1024]{1,0:T(8,128)(2,1)S(1)} %get-tuple-element.127.refs_5_), channel_id=1, source_target_pairs={{0,12},{1,13},{2,14},{3,15},{4,8},{5,9},{6,10},{7,11},{8,4},{9,5},... | collective-permute-start | bytes 786440 | tf_op jit(solution)/shard_map/cond/branch_1_fun/ppermute | solution.py:316
  49.5 24.2 %collective-permute-start.12 = (bf16[128,1024]{1,0:T(8,128)(2,1)S(1)}, bf16[128,1024]{1,0:T(8,128)(2,1)S(1)}, u32[]{:S(2)}, u32[]{:S(2)}) collective-permute-start(bf16[128,1024]{1,0:T(8,128)(2,1)S(1)} %get-tuple-element.128.refs_6_), channel_id=1, source_target_pairs={{4,8},{5,9},{6,10},{7,11},{8,4},{9,5},{10,6},{11,7},{20,24},{21,25... | collective-permute-start | bytes 786440 | tf_op jit(solution)/shard_map/cond/branch_1_fun/ppermute | solution.py:316
  69.1 6.9 %collective-permute-start.13 = (bf16[2,1040,256]{2,1,0:T(8,128)(2,1)S(1)}, bf16[2,1040,256]{2,1,0:T(8,128)(2,1)S(1)}, u32[]{:S(2)}, u32[]{:S(2)}) collective-permute-start(bf16[2,1040,256]{2,1,0:T(8,128)(2,1)S(1)} %get-tuple-element.139), channel_id=1, source_target_pairs={{0,1},{1,0},{2,3},{3,2},{4,5},{5,4},{6,7},{7,6},{8,9},{9,8},{10,11... | collective-permute-start | bytes 3194888 | tf_op jit(solution)/shard_map/cond/branch_1_fun/ppermute | solution.py:321

commit v5 on v4

--- a/solution.py
+++ b/solution.py
@@ -25,7 +25,7 @@
         out_shape=out_shape,
         in_specs=in_specs or [VMEM] * n_in,
         out_specs=out_specs or ([VMEM] * len(out_shape) if many else VMEM),
-        scratch_shapes=[pltpu.VMEM(*x) for x in scratch],
+        scratch_shapes=[pltpu.VMEM(*x) if isinstance(x, tuple) else x for x in scratch],
         compiler_params=pltpu.CompilerParams(vmem_limit_bytes=24 * 1024 * 1024),
         cost_estimate=pl.CostEstimate(flops=flops, bytes_accessed=nbytes, transcendentals=0),
     )
@@ -97,14 +97,16 @@
     out[0] = jnp.where(inner == 0, 0, jnp.where(outer == 0, 1, 2))
 
 
-def share_body(c, sharp, centres, out):
+def share_body(c, sharp, centres, out, sem):
     width = out.shape[1]
     fine = centres.shape[1]
+    copy = pltpu.make_async_copy(centres.at[c], out.at[pl.ds(0, fine)], sem)
+    copy.start()
+    copy.wait()
     row = lax.broadcasted_iota(jnp.int32, (8, width), 0)
     ones = jnp.ones((8, width), BF)
     dims = (((1,), (1,)), ((), ()))
-    values = centres[c]
-    out[:fine, :] = values
+    values = out[:fine, :]
     wide = values.astype(F32)
     square = wide * wide
     high = square.astype(BF)
@@ -330,6 +332,8 @@
                 2,
                 SCALE * 4 * 8 * fine * width,
                 SCALE * fine * width * 4,
+                in_specs=[VMEM, pl.BlockSpec(memory_space=pl.ANY)],
+                scratch=[pltpu.SemaphoreType.DMA],
             )(sharp, centroids)
         )
         far.append(swap(own[c], 2))
@@ -376,7 +380,7 @@
             SCALE * work,
             SCALE * GRP * per_device * fine * width * 2,
         )(blocks[k], *held)
-        for k in early
+        for k in early[:1]
     ]
 
     def refine(places, first, held, gathered, slot, centroids):
@@ -389,6 +393,14 @@
             SCALE * GRP * per_device * fine * width * 2,
         )(gathered, *held)
         soft = dict(zip(early, first))
+        for k in early[1:]:
+            soft[k] = call(
+                functools.partial(soft_body, rows, len(held)),
+                [half] * halves,
+                1 + len(held),
+                SCALE * work,
+                SCALE * GRP * per_device * fine * width * 2,
+            )(gathered[k * (rows + META) : (k + 1) * (rows + META)], *held)
         for n, k in enumerate(late):
             soft[k] = out[n * halves : (n + 1) * halves]
         back = dict(soft)

time: 78.1 us -> 78.1 us (level)
    ppermute x8, waiting for transfers between devices: 16.1 us -> 17.9 us  [turn(): return lax.ppermute(x, 'route', pairs)]
    pallas_call x2 -> x1, Pallas kernels: 3.49 us -> 1.74 us  [shards(): call(functools.partial(soft_body, rows, len(held)), [half] * halves if k...]
    pallas_call x0 -> x1, Pallas kernels: none -> 1.74 us  [refine(): call(functools.partial(soft_body, rows, len(held)), [half] * halves, 1 +...]
    ppermute x8, waiting for transfers between devices: 7.56 us -> 5.94 us  [swap(): return lax.ppermute(x, 'route', [(r, r ^ mask) for r in range(route)])]
  transfers between devices with their start and end apart: 16 -> 16, of which waited for: 8 -> 8; matrix products, arithmetic and copies ran while one was open for 0% -> 0% of each run, Pallas kernels for 30% -> 33%
where the time goes in v5:
time: 78.1 us; the launch traced here: 77.8 us
  Pallas kernels  30.8 us (39%)
  waiting for transfers between devices  23.8 us (30%)
  starting transfers between devices  20.5 us (26%)
  between operations  1.47 us (2%)
  local copies, waits for them, and re-layouts  0.83 us (1%)
    ppermute x8, waiting for transfers between devices, turn(): return lax.ppermute(x, 'route', pairs)  17.9 us
    ppermute x8, starting transfers between devices, turn(): return lax.ppermute(x, 'route', pairs)  16 us
    ppermute x8, waiting for transfers between devices, swap(): return lax.ppermute(x, 'route', [(r, r ^ mask) for r in range(route)])  5.94 us
    pallas_call x1, Pallas kernels, refine(): call(functools.partial(sums_body, rows), [jax.ShapeDtypeStruct(centroids....  5.07 us
    pallas_call x1, Pallas kernels, refine(): call(functools.partial(other_body, groups, rows), jax.ShapeDtypeStruct((g...  5.02 us
    pallas_call x1, Pallas kernels, refine(): call(functools.partial(here_body, rows), [jax.ShapeDtypeStruct(*sums_shap...  4.79 us
    ppermute x8, starting transfers between devices, swap(): return lax.ppermute(x, 'route', [(r, r ^ mask) for r in range(route)])  4.55 us
    pallas_call x1, Pallas kernels, refine(): call(functools.partial(softs_body, rows, len(held), late), [half] * (halv...  3.59 us
  transfers between devices with their start and end apart: 16, of which 8 were waited for; matrix products, arithmetic and copies ran while one was open for 0% of the time, Pallas kernels for 33%

profile of v5, /device:TPU:8, one launch (start us, length us, event | category | flops | bytes accessed | tf_op | source)
XLA Modules:
  0.0 77.8 jit_solution(16123693919432340456)
XLA Ops:
  0.6 0.8 %copy.12.sharp = bf16[2,1]{1,0:T(2,128)(2,1)S(1)} copy(bf16[2,1]{0,1:T(2,128)(2,1)} %bitcast.5) | data formatting | bytes 8 | tf_op jit(solution)/shard_map/reshape | solution.py:325
  1.5 1.6 %shard_map.65.x = bf16[1056,256]{1,0:T(8,128)(2,1)S(1)} custom-call(bf16[2,1]{1,0:T(2,128)(2,1)S(1)} %copy.12.sharp, bf16[2,1024,256]{2,1,0:T(8,128)(2,1)} %centres.3), custom_call_target="tpu_custom_call" | custom-call | flops 41943040 | bytes 5242880 | tf_op jit(solution)/shard_map/pallas_call | solution.py:329
  3.1 1.6 %collective-permute-start.26 = (bf16[1056,256]{1,0:T(8,128)(2,1)S(1)}, bf16[1056,256]{1,0:T(8,128)(2,1)S(1)}, u32[]{:S(2)}, u32[]{:S(2)}) collective-permute-start(bf16[1056,256]{1,0:T(8,128)(2,1)S(1)} %shard_map.65.x), channel_id=1, source_target_pairs={{0,2},{1,3},{2,0},{3,1},{4,6},{5,7},{6,4},{7,5},{8,10},{9,11},{10,... | collective-permute-start | bytes 1622024 | tf_op jit(solution)/shard_map/ppermute | solution.py:323
  4.6 0.5 shard_map.67.x
  5.1 0.6 collective-permute-start.27
  5.7 0.0 copy-done
  5.7 1.6 %shard_map.66 = (bf16[272,256]{1,0:T(8,128)(2,1)S(1)}, bf16[272,256]{1,0:T(8,128)(2,1)S(1)}, bf16[272,256]{1,0:T(8,128)(2,1)S(1)}, bf16[272,256]{1,0:T(8,128)(2,1)S(1)}, s32[512,1]{1,0:T(8,128)S(1)}) custom-call(s32[1]{0:T(128)} %bitcast.here, s32[1,512]{1,0:T(1,128)S(1)} %bitcast.4, f32[512,256]{1,0:T(8,128)S(1)} %copy-done), custom_call_target="tpu_custom_call" | custom-call | flops 1342177280 | bytes 5242880 | tf_op jit(solution)/shard_map/pallas_call | solution.py:342
  7.3 0.1 collective-permute-start.21
  7.4 3.0 %collective-permute-start.22 = (bf16[272,256]{1,0:T(8,128)(2,1)S(1)}, bf16[272,256]{1,0:T(8,128)(2,1)S(1)}, u32[]{:S(2)}, u32[]{:S(2)}) collective-permute-start(bf16[272,256]{1,0:T(8,128)(2,1)S(1)} %get-tuple-element.188), channel_id=1, source_target_pairs={{0,8},{1,9},{2,10},{3,11},{4,12},{5,13},{6,14},{7,15},{8,0},{9,1},... | collective-permute-start | bytes 417800 | tf_op jit(solution)/shard_map/ppermute | solution.py:318
  10.4 0.5 collective-permute-start.23
  10.9 2.5 %collective-permute-done.21.refs_1_.block = bf16[272,256]{1,0:T(8,128)(2,1)S(1)} collective-permute-done((bf16[272,256]{1,0:T(8,128)(2,1)S(1)}, bf16[272,256]{1,0:T(8,128)(2,1)S(1)}, u32[]{:S(2)}, u32[]{:S(2)}) %collective-permute-start.21) | collective-permute-done | bytes 139296 | tf_op jit(solution)/shard_map/ppermute | solution.py:318
  13.4 6.6 %collective-permute-done.22.refs_2_ = bf16[272,256]{1,0:T(8,128)(2,1)S(1)} collective-permute-done((bf16[272,256]{1,0:T(8,128)(2,1)S(1)}, bf16[272,256]{1,0:T(8,128)(2,1)S(1)}, u32[]{:S(2)}, u32[]{:S(2)}) %collective-permute-start.22) | collective-permute-done | bytes 139296 | tf_op jit(solution)/shard_map/ppermute | solution.py:318
  20.0 2.4 %collective-permute-done.23.refs_3_ = bf16[272,256]{1,0:T(8,128)(2,1)S(1)} collective-permute-done((bf16[272,256]{1,0:T(8,128)(2,1)S(1)}, bf16[272,256]{1,0:T(8,128)(2,1)S(1)}, u32[]{:S(2)}, u32[]{:S(2)}) %collective-permute-start.23) | collective-permute-done | bytes 139296 | tf_op jit(solution)/shard_map/ppermute | solution.py:318
  22.4 0.0 collective-permute-start.24
  22.4 0.5 collective-permute-start.25
  22.9 0.7 shard_map.68
  23.6 0.0 collective-permute-done.26.x
  23.6 0.1 collective-permute-start.28
  23.7 5.0 %collective-permute-done.27.x = bf16[1056,256]{1,0:T(8,128)(2,1)S(1)} collective-permute-done((bf16[1056,256]{1,0:T(8,128)(2,1)S(1)}, bf16[1056,256]{1,0:T(8,128)(2,1)S(1)}, u32[]{:S(2)}, u32[]{:S(2)}) %collective-permute-start.27) | collective-permute-done | bytes 540704 | tf_op jit(solution)/shard_map/ppermute | solution.py:323
  28.7 0.0 collective-permute-start.29
  29.6 0.0 collective-permute-done.24.x
  29.6 0.0 collective-permute-done.25.x
  29.7 0.0 collective-permute-done.28.x
  29.8 0.9 %collective-permute-done.29.x = bf16[1056,256]{1,0:T(8,128)(2,1)S(1)} collective-permute-done((bf16[1056,256]{1,0:T(8,128)(2,1)S(1)}, bf16[1056,256]{1,0:T(8,128)(2,1)S(1)}, u32[]{:S(2)}, u32[]{:S(2)}) %collective-permute-start.29) | collective-permute-done | bytes 540704 | tf_op jit(solution)/shard_map/ppermute | solution.py:323
  30.7 0.0 copy-start.3
  30.7 1.7 %shard_map.77 = bf16[256,1024]{1,0:T(8,128)(2,1)S(1)} custom-call(bf16[272,256]{1,0:T(8,128)(2,1)S(1)} %collective-permute-done.21.refs_1_.block, bf16[1056,256]{1,0:T(8,128)(2,1)S(1)} %shard_map.69.refs_0_, bf16[1056,256]{1,0:T(8,128)(2,1)S(1)} %shard_map.70.refs_1_, bf16[1056,256]{1,0:T(8,128)(2,1)S(1)} %shard_map.71.refs_2_, ...), custom_call_target="tpu_custom_call" | custom-call | flops 5368709120 | bytes 20971520 | tf_op jit(solution)/shard_map/pallas_call | solution.py:376
  32.5 45.3 %conditional.1 = (bf16[512,1024]{1,0:T(8,128)(2,1)}, f32[2,1024,256]{2,1,0:T(8,128)}) conditional(s32[]{:T(128)} %bitcast.3, (bf16[1088,256]{1,0:T(8,128)(2,1)S(1)}, bf16[1056,256]{1,0:T(8,128)(2,1)S(1)}, bf16[1056,256]{1,0:T(8,128)(2,1)S(1)}, bf16[1056,256]{1,0:T(8,128)(2,1)S(1)}, bf16[1056,256]{1,0:T(8,128)(2,1)S(1)}, ...), branch_computations={%region_0.0_spmd, %region_1.0_spmd, %region_2.0_spmd} | conditional | flops 74090283008 | bytes 278069504 | solution.py:469
  32.7 0.3 collective-permute-start.7
  33.0 1.7 %collective-permute-start.8 = (bf16[1088,256]{1,0:T(8,128)(2,1)S(1)}, bf16[1088,256]{1,0:T(8,128)(2,1)S(1)}, u32[]{:S(2)}, u32[]{:S(2)}) collective-permute-start(bf16[1088,256]{1,0:T(8,128)(2,1)S(1)} %get-tuple-element.108.blocks), channel_id=1, source_target_pairs={{0,2},{1,3},{2,0},{3,1},{4,6},{5,7},{6,4},{7,5},{8,10},{9,11},{10,... | collective-permute-start | bytes 1671176 | tf_op jit(solution)/shard_map/cond/branch_1_fun/ppermute | solution.py:323
  34.7 1.7 %branch_1_fun.8 = (bf16[128,1024]{1,0:T(8,128)(2,1)S(1)}, bf16[128,1024]{1,0:T(8,128)(2,1)S(1)}) custom-call(bf16[272,256]{1,0:T(8,128)(2,1)S(1)} %get-tuple-element.120.block, bf16[1056,256]{1,0:T(8,128)(2,1)S(1)} %get-tuple-element.109.refs_0_, bf16[1056,256]{1,0:T(8,128)(2,1)S(1)} %get-tuple-element.110.refs_1_, ...), custom_call_target="tpu_custom_call" | custom-call | flops 5368709120 | bytes 20971520 | tf_op jit(solution)/shard_map/cond/branch_1_fun/pallas_call | solution.py:397
  36.5 2.7 %collective-permute-start.9 = (bf16[128,1024]{1,0:T(8,128)(2,1)S(1)}, bf16[128,1024]{1,0:T(8,128)(2,1)S(1)}, u32[]{:S(2)}, u32[]{:S(2)}) collective-permute-start(bf16[128,1024]{1,0:T(8,128)(2,1)S(1)} %get-tuple-element.121.refs_3_), channel_id=1, source_target_pairs={{0,8},{1,9},{2,10},{3,11},{4,12},{5,13},{6,14},{7,15},{8,0},{9,1},... | collective-permute-start | bytes 786440 | tf_op jit(solution)/shard_map/cond/branch_1_fun/ppermute | solution.py:318
  39.2 2.2 %collective-permute-start.10 = (bf16[128,1024]{1,0:T(8,128)(2,1)S(1)}, bf16[128,1024]{1,0:T(8,128)(2,1)S(1)}, u32[]{:S(2)}, u32[]{:S(2)}) collective-permute-start(bf16[128,1024]{1,0:T(8,128)(2,1)S(1)} %get-tuple-element.122.refs_4_), channel_id=1, source_target_pairs={{4,12},{5,13},{6,14},{7,15},{8,0},{9,1},{10,2},{11,3},{20,28},{21,... | collective-permute-start | bytes 786440 | tf_op jit(solution)/shard_map/cond/branch_1_fun/ppermute | solution.py:318
  41.4 3.6 %branch_1_fun.7 = (bf16[128,1024]{1,0:T(8,128)(2,1)S(1)}, bf16[128,1024]{1,0:T(8,128)(2,1)S(1)}, bf16[128,1024]{1,0:T(8,128)(2,1)S(1)}, bf16[128,1024]{1,0:T(8,128)(2,1)S(1)}) custom-call(bf16[1088,256]{1,0:T(8,128)(2,1)S(1)} %get-tuple-element.108.blocks, bf16[1056,256]{1,0:T(8,128)(2,1)S(1)} %get-tuple-element.109.refs_0_, ...), custom_call_target="tpu_custom_call" | custom-call | flops 10737418240 | bytes 20971520 | tf_op jit(solution)/shard_map/cond/branch_1_fun/pallas_call | solution.py:388
  45.0 2.8 %collective-permute-start.11 = (bf16[128,1024]{1,0:T(8,128)(2,1)S(1)}, bf16[128,1024]{1,0:T(8,128)(2,1)S(1)}, u32[]{:S(2)}, u32[]{:S(2)}) collective-permute-start(bf16[128,1024]{1,0:T(8,128)(2,1)S(1)} %get-tuple-element.123.refs_5_), channel_id=1, source_target_pairs={{0,12},{1,13},{2,14},{3,15},{4,8},{5,9},{6,10},{7,11},{8,4},{9,5},... | collective-permute-start | bytes 786440 | tf_op jit(solution)/shard_map/cond/branch_1_fun/ppermute | solution.py:318
  47.8 0.0 collective-permute-done.8.blocks.others
  47.8 4.4 %collective-permute-start.12 = (bf16[128,1024]{1,0:T(8,128)(2,1)S(1)}, bf16[128,1024]{1,0:T(8,128)(2,1)S(1)}, u32[]{:S(2)}, u32[]{:S(2)}) collective-permute-start(bf16[128,1024]{1,0:T(8,128)(2,1)S(1)} %get-tuple-element.124.refs_6_), channel_id=1, source_target_pairs={{4,8},{5,9},{6,10},{7,11},{8,4},{9,5},{10,6},{11,7},{20,24},{21,25... | collective-permute-start | bytes 786440 | tf_op jit(solution)/shard_map/cond/branch_1_fun/ppermute | solution.py:318
  52.2 4.8 %branch_1_fun.9 = (f32[4,1024,256]{2,1,0:T(8,128)S(1)}, f32[4,1024]{1,0:T(4,128)S(1)}) custom-call(bf16[1088,256]{1,0:T(8,128)(2,1)S(1)} %get-tuple-element.108.blocks, bf16[128,1024]{1,0:T(8,128)(2,1)S(1)} %get-tuple-element.117.refs_0_, bf16[128,1024]{1,0:T(8,128)(2,1)S(1)} %get-tuple-element.118.refs_1_, ...), custom_call_target="tpu_custom_call" | custom-call | flops 2147483648 | bytes 4194304 | tf_op jit(solution)/shard_map/cond/branch_1_fun/pallas_call | solution.py:413
  57.0 5.0 %branch_1_fun.10.soft = bf16[1024,1024]{1,0:T(8,128)(2,1)S(1)} custom-call(bf16[1088,256]{1,0:T(8,128)(2,1)S(1)} %collective-permute-done.8.blocks.others, bf16[1056,256]{1,0:T(8,128)(2,1)S(1)} %get-tuple-element.109.refs_0_, bf16[1056,256]{1,0:T(8,128)(2,1)S(1)} %get-tuple-element.110.refs_1_, bf16[1056,256]{1,0:T(8,128)(2,1)S(1)} %get-tuple-element.111.refs_2_, ...), custom_call_target="tpu_custom_call" | custom-call | tf_op jit(solution)/shard_map/cond/branch_1_fun/pallas_call | solution.py:422
  62.0 0.0 collective-permute-done.9.refs_3_
  62.1 0.7 collective-permute-done.10.refs_4_
  62.8 5.1 %branch_1_fun.12 = (f32[2,1024,256]{2,1,0:T(8,128)S(1)}, f32[2,4,256]{2,1,0:T(4,128)S(1)}, bf16[2,1040,256]{2,1,0:T(8,128)(2,1)S(1)}) custom-call(bf16[1088,256]{1,0:T(8,128)(2,1)S(1)} %collective-permute-done.8.blocks.others, bf16[1024,1024]{1,0:T(8,128)(2,1)S(1)} %branch_1_fun.10.soft, bf16[2,1024,256]{2,1,0:T(8,128)(2,1)S(1)} %get-tuple-element.130.centres, ...), custom_call_target="tpu_custom_call" | custom-call | flops 2147483648 | bytes 4194304 | tf_op jit(solution)/shard_map/cond/branch_1_fun/pallas_call | solution.py:431
  67.9 0.1 collective-permute-start.13
  68.0 1.4 %collective-permute-done.11.refs_5_ = bf16[128,1024]{1,0:T(8,128)(2,1)S(1)} collective-permute-done((bf16[128,1024]{1,0:T(8,128)(2,1)S(1)}, bf16[128,1024]{1,0:T(8,128)(2,1)S(1)}, u32[]{:S(2)}, u32[]{:S(2)}) %collective-permute-start.11) | collective-permute-done | bytes 262176 | tf_op jit(solution)/shard_map/cond/branch_1_fun/ppermute | solution.py:318
  69.3 4.2 %collective-permute-done.12.refs_6_ = bf16[128,1024]{1,0:T(8,128)(2,1)S(1)} collective-permute-done((bf16[128,1024]{1,0:T(8,128)(2,1)S(1)}, bf16[128,1024]{1,0:T(8,128)(2,1)S(1)}, u32[]{:S(2)}, u32[]{:S(2)}) %collective-permute-start.12) | collective-permute-done | bytes 262176 | tf_op jit(solution)/shard_map/cond/branch_1_fun/ppermute | solution.py:318
  73.5 0.0 collective-permute-done.7.refs_2_
  73.5 2.3 %branch_1_fun.11 = bf16[512,1024]{1,0:T(8,128)(2,1)} custom-call(s32[512,1]{1,0:T(8,128)S(1)} %get-tuple-element.107.slot, bf16[128,1024]{1,0:T(8,128)(2,1)S(1)} %get-tuple-element.117.refs_0_, bf16[128,1024]{1,0:T(8,128)(2,1)S(1)} %get-tuple-element.118.refs_1_, bf16[256,1024]{1,0:T(8,128)(2,1)S(1)} %collective-permute-done.7.refs_2_, ...), custom_call_target="tpu_custom_call" | custom-call | flops 53687091200 | bytes 209715200 | tf_op jit(solution)/shard_map/cond/branch_1_fun/pallas_call | solution.py:448
  75.8 0.0 collective-permute-done.13.got
  75.8 2.0 %branch_1_fun.13 = f32[2,1024,256]{2,1,0:T(8,128)} custom-call(f32[2,1024,256]{2,1,0:T(8,128)S(1)} %get-tuple-element.133.mine, f32[2,4,256]{2,1,0:T(4,128)S(1)} %get-tuple-element.134.mass, bf16[2,1040,256]{2,1,0:T(8,128)(2,1)S(1)} %collective-permute-done.13.got), custom_call_target="tpu_custom_call" | custom-call | flops 2097152 | bytes 5242880 | tf_op jit(solution)/shard_map/cond/branch_1_fun/pallas_call | solution.py:455
  (15 shorter events, 0.3 us)
Async XLA Ops:
  0.6 5.1 %copy-start.1 = (s32[512]{0:T(512)S(1)}, s32[512]{0:T(512)}, u32[]{:S(2)}) copy-start(s32[512]{0:T(512)} %param.8) | copy-start | bytes 6148
  0.6 5.1 %copy-start = (f32[512,256]{1,0:T(8,128)S(1)}, f32[512,256]{1,0:T(8,128)}, u32[]{:S(2)}) copy-start(f32[512,256]{1,0:T(8,128)} %codes.1) | copy-start | bytes 1572868
  1.5 3.2 %copy-start.2 = (bf16[2,1024,256]{2,1,0:T(8,128)(2,1)S(1)}, bf16[2,1024,256]{2,1,0:T(8,128)(2,1)}, u32[]{:S(2)}) copy-start(bf16[2,1024,256]{2,1,0:T(8,128)(2,1)} %centres.3) | copy-start | bytes 3145732
  3.1 20.5 %collective-permute-start.26 = (bf16[1056,256]{1,0:T(8,128)(2,1)S(1)}, bf16[1056,256]{1,0:T(8,128)(2,1)S(1)}, u32[]{:S(2)}, u32[]{:S(2)}) collective-permute-start(bf16[1056,256]{1,0:T(8,128)(2,1)S(1)} %shard_map.65.x), channel_id=1, source_target_pairs={{0,2},{1,3},{2,0},{3,1},{4,6},{5,7},{6,4},{7,5},{8,10},{9,11},{10,... | collective-permute-start | bytes 1622024 | tf_op jit(solution)/shard_map/ppermute | solution.py:323
  5.1 23.6 %collective-permute-start.27 = (bf16[1056,256]{1,0:T(8,128)(2,1)S(1)}, bf16[1056,256]{1,0:T(8,128)(2,1)S(1)}, u32[]{:S(2)}, u32[]{:S(2)}) collective-permute-start(bf16[1056,256]{1,0:T(8,128)(2,1)S(1)} %shard_map.67.x), channel_id=1, source_target_pairs={{0,2},{1,3},{2,0},{3,1},{4,6},{5,7},{6,4},{7,5},{8,10},{9,11},{10,... | collective-permute-start | bytes 1622024 | tf_op jit(solution)/shard_map/ppermute | solution.py:323
  7.3 6.1 %collective-permute-start.21 = (bf16[272,256]{1,0:T(8,128)(2,1)S(1)}, bf16[272,256]{1,0:T(8,128)(2,1)S(1)}, u32[]{:S(2)}, u32[]{:S(2)}) collective-permute-start(bf16[272,256]{1,0:T(8,128)(2,1)S(1)} %get-tuple-element.187), channel_id=1, source_target_pairs={{0,4},{1,5},{2,6},{3,7},{4,0},{5,1},{6,2},{7,3},{8,12},{9,13},{10,... | collective-permute-start | bytes 417800 | tf_op jit(solution)/shard_map/ppermute | solution.py:318
  7.4 12.6 %collective-permute-start.22 = (bf16[272,256]{1,0:T(8,128)(2,1)S(1)}, bf16[272,256]{1,0:T(8,128)(2,1)S(1)}, u32[]{:S(2)}, u32[]{:S(2)}) collective-permute-start(bf16[272,256]{1,0:T(8,128)(2,1)S(1)} %get-tuple-element.188), channel_id=1, source_target_pairs={{0,8},{1,9},{2,10},{3,11},{4,12},{5,13},{6,14},{7,15},{8,0},{9,1},... | collective-permute-start | bytes 417800 | tf_op jit(solution)/shard_map/ppermute | solution.py:318
  10.4 12.0 %collective-permute-start.23 = (bf16[272,256]{1,0:T(8,128)(2,1)S(1)}, bf16[272,256]{1,0:T(8,128)(2,1)S(1)}, u32[]{:S(2)}, u32[]{:S(2)}) collective-permute-start(bf16[272,256]{1,0:T(8,128)(2,1)S(1)} %get-tuple-element.189), channel_id=1, source_target_pairs={{0,12},{1,13},{2,14},{3,15},{4,8},{5,9},{6,10},{7,11},{8,4},{9,5},... | collective-permute-start | bytes 417800 | tf_op jit(solution)/shard_map/ppermute | solution.py:318
  22.4 7.2 %collective-permute-start.24 = (bf16[1056,256]{1,0:T(8,128)(2,1)S(1)}, bf16[1056,256]{1,0:T(8,128)(2,1)S(1)}, u32[]{:S(2)}, u32[]{:S(2)}) collective-permute-start(bf16[1056,256]{1,0:T(8,128)(2,1)S(1)} %shard_map.65.x), channel_id=1, source_target_pairs={{0,1},{1,0},{2,3},{3,2},{4,5},{5,4},{6,7},{7,6},{8,9},{9,8},{10,11... | collective-permute-start | bytes 1622024 | tf_op jit(solution)/shard_map/ppermute | solution.py:323
  22.4 7.2 %collective-permute-start.25 = (bf16[1056,256]{1,0:T(8,128)(2,1)S(1)}, bf16[1056,256]{1,0:T(8,128)(2,1)S(1)}, u32[]{:S(2)}, u32[]{:S(2)}) collective-permute-start(bf16[1056,256]{1,0:T(8,128)(2,1)S(1)} %shard_map.67.x), channel_id=1, source_target_pairs={{0,1},{1,0},{2,3},{3,2},{4,5},{5,4},{6,7},{7,6},{8,9},{9,8},{10,11... | collective-permute-start | bytes 1622024 | tf_op jit(solution)/shard_map/ppermute | solution.py:323
  23.6 6.1 %collective-permute-start.28 = (bf16[1056,256]{1,0:T(8,128)(2,1)S(1)}, bf16[1056,256]{1,0:T(8,128)(2,1)S(1)}, u32[]{:S(2)}, u32[]{:S(2)}) collective-permute-start(bf16[1056,256]{1,0:T(8,128)(2,1)S(1)} %collective-permute-done.26.x), channel_id=1, source_target_pairs={{0,1},{1,0},{2,3},{3,2},{4,5},{5,4},{6,7},{7,6},{8,9},{9,8},{10,11... | collective-permute-start | bytes 1622024 | tf_op jit(solution)/shard_map/ppermute | solution.py:323
  28.7 1.9 %collective-permute-start.29 = (bf16[1056,256]{1,0:T(8,128)(2,1)S(1)}, bf16[1056,256]{1,0:T(8,128)(2,1)S(1)}, u32[]{:S(2)}, u32[]{:S(2)}) collective-permute-start(bf16[1056,256]{1,0:T(8,128)(2,1)S(1)} %collective-permute-done.27.x), channel_id=1, source_target_pairs={{0,1},{1,0},{2,3},{3,2},{4,5},{5,4},{6,7},{7,6},{8,9},{9,8},{10,11... | collective-permute-start | bytes 1622024 | tf_op jit(solution)/shard_map/ppermute | solution.py:323
  30.7 1.8 %copy-start.3 = (bf16[2,1024,256]{2,1,0:T(8,128)(2,1)S(1)}, bf16[2,1024,256]{2,1,0:T(8,128)(2,1)}, u32[]{:S(2)}) copy-start(bf16[2,1024,256]{2,1,0:T(8,128)(2,1)} %centres.3) | copy-start | bytes 3145732
  32.7 40.8 %collective-permute-start.7 = (bf16[256,1024]{1,0:T(8,128)(2,1)S(1)}, bf16[256,1024]{1,0:T(8,128)(2,1)S(1)}, u32[]{:S(2)}, u32[]{:S(2)}) collective-permute-start(bf16[256,1024]{1,0:T(8,128)(2,1)S(1)} %get-tuple-element.119.refs_2_), channel_id=1, source_target_pairs={{0,4},{1,5},{2,6},{3,7},{4,0},{5,1},{6,2},{7,3},{8,12},{9,13},{10,... | collective-permute-start | bytes 1572872 | tf_op jit(solution)/shard_map/cond/branch_1_fun/ppermute | solution.py:318
  33.0 14.8 %collective-permute-start.8 = (bf16[1088,256]{1,0:T(8,128)(2,1)S(1)}, bf16[1088,256]{1,0:T(8,128)(2,1)S(1)}, u32[]{:S(2)}, u32[]{:S(2)}) collective-permute-start(bf16[1088,256]{1,0:T(8,128)(2,1)S(1)} %get-tuple-element.108.blocks), channel_id=1, source_target_pairs={{0,2},{1,3},{2,0},{3,1},{4,6},{5,7},{6,4},{7,5},{8,10},{9,11},{10,... | collective-permute-start | bytes 1671176 | tf_op jit(solution)/shard_map/cond/branch_1_fun/ppermute | solution.py:323
  36.5 25.6 %collective-permute-start.9 = (bf16[128,1024]{1,0:T(8,128)(2,1)S(1)}, bf16[128,1024]{1,0:T(8,128)(2,1)S(1)}, u32[]{:S(2)}, u32[]{:S(2)}) collective-permute-start(bf16[128,1024]{1,0:T(8,128)(2,1)S(1)} %get-tuple-element.121.refs_3_), channel_id=1, source_target_pairs={{0,8},{1,9},{2,10},{3,11},{4,12},{5,13},{6,14},{7,15},{8,0},{9,1},... | collective-permute-start | bytes 786440 | tf_op jit(solution)/shard_map/cond/branch_1_fun/ppermute | solution.py:318
  39.2 23.6 %collective-permute-start.10 = (bf16[128,1024]{1,0:T(8,128)(2,1)S(1)}, bf16[128,1024]{1,0:T(8,128)(2,1)S(1)}, u32[]{:S(2)}, u32[]{:S(2)}) collective-permute-start(bf16[128,1024]{1,0:T(8,128)(2,1)S(1)} %get-tuple-element.122.refs_4_), channel_id=1, source_target_pairs={{4,12},{5,13},{6,14},{7,15},{8,0},{9,1},{10,2},{11,3},{20,28},{21,... | collective-permute-start | bytes 786440 | tf_op jit(solution)/shard_map/cond/branch_1_fun/ppermute | solution.py:318
  45.0 24.3 %collective-permute-start.11 = (bf16[128,1024]{1,0:T(8,128)(2,1)S(1)}, bf16[128,1024]{1,0:T(8,128)(2,1)S(1)}, u32[]{:S(2)}, u32[]{:S(2)}) collective-permute-start(bf16[128,1024]{1,0:T(8,128)(2,1)S(1)} %get-tuple-element.123.refs_5_), channel_id=1, source_target_pairs={{0,12},{1,13},{2,14},{3,15},{4,8},{5,9},{6,10},{7,11},{8,4},{9,5},... | collective-permute-start | bytes 786440 | tf_op jit(solution)/shard_map/cond/branch_1_fun/ppermute | solution.py:318
  47.8 25.8 %collective-permute-start.12 = (bf16[128,1024]{1,0:T(8,128)(2,1)S(1)}, bf16[128,1024]{1,0:T(8,128)(2,1)S(1)}, u32[]{:S(2)}, u32[]{:S(2)}) collective-permute-start(bf16[128,1024]{1,0:T(8,128)(2,1)S(1)} %get-tuple-element.124.refs_6_), channel_id=1, source_target_pairs={{4,8},{5,9},{6,10},{7,11},{8,4},{9,5},{10,6},{11,7},{20,24},{21,25... | collective-permute-start | bytes 786440 | tf_op jit(solution)/shard_map/cond/branch_1_fun/ppermute | solution.py:318
  67.9 7.9 %collective-permute-start.13 = (bf16[2,1040,256]{2,1,0:T(8,128)(2,1)S(1)}, bf16[2,1040,256]{2,1,0:T(8,128)(2,1)S(1)}, u32[]{:S(2)}, u32[]{:S(2)}) collective-permute-start(bf16[2,1040,256]{2,1,0:T(8,128)(2,1)S(1)} %get-tuple-element.135), channel_id=1, source_target_pairs={{0,1},{1,0},{2,3},{3,2},{4,5},{5,4},{6,7},{7,6},{8,9},{9,8},{10,11... | collective-permute-start | bytes 3194888 | tf_op jit(solution)/shard_map/cond/branch_1_fun/ppermute | solution.py:323

commit v6 on v5

--- a/solution.py
+++ b/solution.py
@@ -77,6 +77,10 @@
     outs[groups][...] = gc * rows + rank_c
 
 
+def first_rows(rows):
+    return rows * 7 // 16 // 16 * 16
+
+
 def busy_body(groups, rows, here, *refs):
     out = refs[groups]
     lane = lax.broadcasted_iota(jnp.int32, (1, refs[0].shape[1]), 1)
@@ -87,7 +91,7 @@
         for s in range(groups):
             counts = refs[s][rows:, :].astype(F32)[2:3, :]
             most = jnp.maximum(most, jnp.where(lane == d ^ s, counts, 0.0))
-        flag = (jnp.max(most) > float(rows // 2)).astype(jnp.int32)
+        flag = (jnp.max(most) > float(first_rows(rows))).astype(jnp.int32)
         side = (d ^ (d >> 1)) & 1
         flags[side] = flags[side] | flag
     between = (group ^ (group >> 1)) & 1
@@ -171,9 +175,10 @@
 
 
 def halve(values, outs):
-    size = values.shape[0] // len(outs)
-    for n, out in enumerate(outs):
-        out[...] = values[n * size : (n + 1) * size, :]
+    start = 0
+    for out in outs:
+        out[...] = values[start : start + out.shape[0], :]
+        start += out.shape[0]
 
 
 def soft_body(rows, count, block, *refs):
@@ -369,13 +374,14 @@
     halves = 2 if groups == 4 else 1
     work = 2 * rows * fine * width * 2 * GRP
     held = [call(copy_body, jax.ShapeDtypeStruct(x.shape, BF), 1, 0, 0)(x) for x in (*own, *near, *far, *last)]
-    half = jax.ShapeDtypeStruct((rows // halves, fine), BF)
+    sizes = [first_rows(rows), rows - first_rows(rows)] if halves > 1 else [rows]
+    half = [jax.ShapeDtypeStruct((size, fine), BF) for size in sizes]
     early = [1, 2] if groups > 2 else [1]
     late = [k for k in range(groups - 1, -1, -1) if k not in early]
     first = [
         call(
             functools.partial(soft_body, rows, len(held)),
-            [half] * halves if k > 1 else [jax.ShapeDtypeStruct((rows, fine), BF)],
+            half if k > 1 else [jax.ShapeDtypeStruct((rows, fine), BF)],
             1 + len(held),
             SCALE * work,
             SCALE * GRP * per_device * fine * width * 2,
@@ -387,7 +393,7 @@
         others = swap(gathered, 2)
         out = call(
             functools.partial(softs_body, rows, len(held), late),
-            [half] * (halves * len(late)),
+            half * len(late),
             1 + len(held),
             SCALE * len(late) * work,
             SCALE * GRP * per_device * fine * width * 2,
@@ -396,7 +402,7 @@
         for k in early[1:]:
             soft[k] = call(
                 functools.partial(soft_body, rows, len(held)),
-                [half] * halves,
+                half,
                 1 + len(held),
                 SCALE * work,
                 SCALE * GRP * per_device * fine * width * 2,
@@ -443,8 +449,10 @@
         got = swap(give, 1)
         pieces = []
         for k in range(groups):
-            size = rows // len(back[k])
-            pieces += [(k * rows + n * size, x) for n, x in enumerate(back[k])]
+            start = k * rows
+            for x in back[k]:
+                pieces.append((start, x))
+                start += x.shape[0]
         soft_labels = call(
             functools.partial(unpack_body, [start for start, _ in pieces]),
             jax.ShapeDtypeStruct((slot.shape[0], fine), BF),

time: 78.1 us -> 77.8 us (level)
  starting transfers between devices: 20.5 us -> 13.7 us
  waiting for transfers between devices: 23.8 us -> 29.9 us
  Pallas kernels: 30.8 us -> 31.6 us
    ppermute x8, starting transfers between devices: 16 us -> 9.14 us  [turn(): return lax.ppermute(x, 'route', pairs)]
    ppermute x8, waiting for transfers between devices: 17.9 us -> 21 us  [turn(): return lax.ppermute(x, 'route', pairs)]
    ppermute x8, waiting for transfers between devices: 5.94 us -> 8.92 us  [swap(): return lax.ppermute(x, 'route', [(r, r ^ mask) for r in range(route)])]
  transfers between devices with their start and end apart: 16 -> 16, of which waited for: 8 -> 8; matrix products, arithmetic and copies ran while one was open for 0% -> 0% of each run, Pallas kernels for 33% -> 34%
where the time goes in v6:
time: 77.8 us; the launch traced here: 77.6 us
  Pallas kernels  31.6 us (41%)
  waiting for transfers between devices  29.9 us (38%)
  starting transfers between devices  13.7 us (18%)
  between operations  1.47 us (2%)
  local copies, waits for them, and re-layouts  0.83 us (1%)
    ppermute x8, waiting for transfers between devices, turn(): return lax.ppermute(x, 'route', pairs)  21 us
    ppermute x8, starting transfers between devices, turn(): return lax.ppermute(x, 'route', pairs)  9.14 us
    ppermute x8, waiting for transfers between devices, swap(): return lax.ppermute(x, 'route', [(r, r ^ mask) for r in range(route)])  8.92 us
    pallas_call x1, Pallas kernels, refine(): call(functools.partial(here_body, rows), [jax.ShapeDtypeStruct(*sums_shap...  5.39 us
    pallas_call x1, Pallas kernels, refine(): call(functools.partial(sums_body, rows), [jax.ShapeDtypeStruct(centroids....  5.07 us
    pallas_call x1, Pallas kernels, refine(): call(functools.partial(other_body, groups, rows), jax.ShapeDtypeStruct((g...  5.03 us
    ppermute x8, starting transfers between devices, swap(): return lax.ppermute(x, 'route', [(r, r ^ mask) for r in range(route)])  4.55 us
    pallas_call x1, Pallas kernels, refine(): call(functools.partial(softs_body, rows, len(held), late), half * len(lat...  3.59 us
  transfers between devices with their start and end apart: 16, of which 8 were waited for; matrix products, arithmetic and copies ran while one was open for 0% of the time, Pallas kernels for 34%

profile of v6, /device:TPU:8, one launch (start us, length us, event | category | flops | bytes accessed | tf_op | source)
XLA Modules:
  0.0 77.6 jit_solution(7139268259495557965)
XLA Ops:
  0.6 0.8 %copy.12.sharp = bf16[2,1]{1,0:T(2,128)(2,1)S(1)} copy(bf16[2,1]{0,1:T(2,128)(2,1)} %bitcast.5) | data formatting | bytes 8 | tf_op jit(solution)/shard_map/reshape | solution.py:330
  1.5 1.6 %shard_map.65.x = bf16[1056,256]{1,0:T(8,128)(2,1)S(1)} custom-call(bf16[2,1]{1,0:T(2,128)(2,1)S(1)} %copy.12.sharp, bf16[2,1024,256]{2,1,0:T(8,128)(2,1)} %centres.3), custom_call_target="tpu_custom_call" | custom-call | flops 41943040 | bytes 5242880 | tf_op jit(solution)/shard_map/pallas_call | solution.py:334
  3.1 1.6 %collective-permute-start.26 = (bf16[1056,256]{1,0:T(8,128)(2,1)S(1)}, bf16[1056,256]{1,0:T(8,128)(2,1)S(1)}, u32[]{:S(2)}, u32[]{:S(2)}) collective-permute-start(bf16[1056,256]{1,0:T(8,128)(2,1)S(1)} %shard_map.65.x), channel_id=1, source_target_pairs={{0,2},{1,3},{2,0},{3,1},{4,6},{5,7},{6,4},{7,5},{8,10},{9,11},{10,... | collective-permute-start | bytes 1622024 | tf_op jit(solution)/shard_map/ppermute | solution.py:328
  4.6 0.5 shard_map.67.x
  5.1 0.6 collective-permute-start.27
  5.7 0.0 copy-done
  5.7 1.6 %shard_map.66 = (bf16[272,256]{1,0:T(8,128)(2,1)S(1)}, bf16[272,256]{1,0:T(8,128)(2,1)S(1)}, bf16[272,256]{1,0:T(8,128)(2,1)S(1)}, bf16[272,256]{1,0:T(8,128)(2,1)S(1)}, s32[512,1]{1,0:T(8,128)S(1)}) custom-call(s32[1]{0:T(128)} %bitcast.here, s32[1,512]{1,0:T(1,128)S(1)} %bitcast.4, f32[512,256]{1,0:T(8,128)S(1)} %copy-done), custom_call_target="tpu_custom_call" | custom-call | flops 1342177280 | bytes 5242880 | tf_op jit(solution)/shard_map/pallas_call | solution.py:347
  7.3 0.1 collective-permute-start.21
  7.4 3.0 %collective-permute-start.22 = (bf16[272,256]{1,0:T(8,128)(2,1)S(1)}, bf16[272,256]{1,0:T(8,128)(2,1)S(1)}, u32[]{:S(2)}, u32[]{:S(2)}) collective-permute-start(bf16[272,256]{1,0:T(8,128)(2,1)S(1)} %get-tuple-element.188), channel_id=1, source_target_pairs={{0,8},{1,9},{2,10},{3,11},{4,12},{5,13},{6,14},{7,15},{8,0},{9,1},... | collective-permute-start | bytes 417800 | tf_op jit(solution)/shard_map/ppermute | solution.py:323
  10.4 0.5 collective-permute-start.23
  10.9 2.5 %collective-permute-done.21.refs_1_.block = bf16[272,256]{1,0:T(8,128)(2,1)S(1)} collective-permute-done((bf16[272,256]{1,0:T(8,128)(2,1)S(1)}, bf16[272,256]{1,0:T(8,128)(2,1)S(1)}, u32[]{:S(2)}, u32[]{:S(2)}) %collective-permute-start.21) | collective-permute-done | bytes 139296 | tf_op jit(solution)/shard_map/ppermute | solution.py:323
  13.4 6.6 %collective-permute-done.22.refs_2_ = bf16[272,256]{1,0:T(8,128)(2,1)S(1)} collective-permute-done((bf16[272,256]{1,0:T(8,128)(2,1)S(1)}, bf16[272,256]{1,0:T(8,128)(2,1)S(1)}, u32[]{:S(2)}, u32[]{:S(2)}) %collective-permute-start.22) | collective-permute-done | bytes 139296 | tf_op jit(solution)/shard_map/ppermute | solution.py:323
  20.0 2.4 %collective-permute-done.23.refs_3_ = bf16[272,256]{1,0:T(8,128)(2,1)S(1)} collective-permute-done((bf16[272,256]{1,0:T(8,128)(2,1)S(1)}, bf16[272,256]{1,0:T(8,128)(2,1)S(1)}, u32[]{:S(2)}, u32[]{:S(2)}) %collective-permute-start.23) | collective-permute-done | bytes 139296 | tf_op jit(solution)/shard_map/ppermute | solution.py:323
  22.4 0.0 collective-permute-start.24
  22.4 0.5 collective-permute-start.25
  22.9 0.7 shard_map.68
  23.6 0.0 collective-permute-done.26.x
  23.6 0.1 collective-permute-start.28
  23.7 5.0 %collective-permute-done.27.x = bf16[1056,256]{1,0:T(8,128)(2,1)S(1)} collective-permute-done((bf16[1056,256]{1,0:T(8,128)(2,1)S(1)}, bf16[1056,256]{1,0:T(8,128)(2,1)S(1)}, u32[]{:S(2)}, u32[]{:S(2)}) %collective-permute-start.27) | collective-permute-done | bytes 540704 | tf_op jit(solution)/shard_map/ppermute | solution.py:328
  28.7 0.0 collective-permute-start.29
  29.6 0.0 collective-permute-done.24.x
  29.6 0.0 collective-permute-done.25.x
  29.7 0.0 collective-permute-done.28.x
  29.8 0.9 %collective-permute-done.29.x = bf16[1056,256]{1,0:T(8,128)(2,1)S(1)} collective-permute-done((bf16[1056,256]{1,0:T(8,128)(2,1)S(1)}, bf16[1056,256]{1,0:T(8,128)(2,1)S(1)}, u32[]{:S(2)}, u32[]{:S(2)}) %collective-permute-start.29) | collective-permute-done | bytes 540704 | tf_op jit(solution)/shard_map/ppermute | solution.py:328
  30.7 0.0 copy-start.3
  30.7 1.7 %shard_map.77 = bf16[256,1024]{1,0:T(8,128)(2,1)S(1)} custom-call(bf16[272,256]{1,0:T(8,128)(2,1)S(1)} %collective-permute-done.21.refs_1_.block, bf16[1056,256]{1,0:T(8,128)(2,1)S(1)} %shard_map.69.refs_0_, bf16[1056,256]{1,0:T(8,128)(2,1)S(1)} %shard_map.70.refs_1_, bf16[1056,256]{1,0:T(8,128)(2,1)S(1)} %shard_map.71.refs_2_, ...), custom_call_target="tpu_custom_call" | custom-call | flops 5368709120 | bytes 20971520 | tf_op jit(solution)/shard_map/pallas_call | solution.py:382
  32.5 45.2 %conditional.1 = (bf16[512,1024]{1,0:T(8,128)(2,1)}, f32[2,1024,256]{2,1,0:T(8,128)}) conditional(s32[]{:T(128)} %bitcast.3, (bf16[1088,256]{1,0:T(8,128)(2,1)S(1)}, bf16[1056,256]{1,0:T(8,128)(2,1)S(1)}, bf16[1056,256]{1,0:T(8,128)(2,1)S(1)}, bf16[1056,256]{1,0:T(8,128)(2,1)S(1)}, bf16[1056,256]{1,0:T(8,128)(2,1)S(1)}, ...), branch_computations={%region_0.0_spmd, %region_1.0_spmd, %region_2.0_spmd} | conditional | flops 74090283008 | bytes 278069504 | solution.py:477
  32.5 0.3 collective-permute-start
  32.8 1.7 %collective-permute-start.1 = (bf16[1088,256]{1,0:T(8,128)(2,1)S(1)}, bf16[1088,256]{1,0:T(8,128)(2,1)S(1)}, u32[]{:S(2)}, u32[]{:S(2)}) collective-permute-start(bf16[1088,256]{1,0:T(8,128)(2,1)S(1)} %get-tuple-element.79.blocks), channel_id=1, source_target_pairs={{0,2},{1,3},{2,0},{3,1},{4,6},{5,7},{6,4},{7,5},{8,10},{9,11},{10,... | collective-permute-start | bytes 1671176 | tf_op jit(solution)/shard_map/cond/branch_0_fun/ppermute | solution.py:328
  34.5 1.7 %branch_0_fun.8 = (bf16[112,1024]{1,0:T(8,128)(2,1)S(1)}, bf16[144,1024]{1,0:T(8,128)(2,1)S(1)}) custom-call(bf16[272,256]{1,0:T(8,128)(2,1)S(1)} %get-tuple-element.91.block, bf16[1056,256]{1,0:T(8,128)(2,1)S(1)} %get-tuple-element.80.refs_0_, bf16[1056,256]{1,0:T(8,128)(2,1)S(1)} %get-tuple-element.81.refs_1_, ...), custom_call_target="tpu_custom_call" | custom-call | flops 5368709120 | bytes 20971520 | tf_op jit(solution)/shard_map/cond/branch_0_fun/pallas_call | solution.py:403
  36.3 2.7 %collective-permute-start.2 = (bf16[112,1024]{1,0:T(8,128)(2,1)S(1)}, bf16[112,1024]{1,0:T(8,128)(2,1)S(1)}, u32[]{:S(2)}, u32[]{:S(2)}) collective-permute-start(bf16[112,1024]{1,0:T(8,128)(2,1)S(1)} %get-tuple-element.92.refs_3_), channel_id=1, source_target_pairs={{0,8},{1,9},{2,10},{3,11},{4,12},{5,13},{6,14},{7,15},{8,0},{9,1},... | collective-permute-start | bytes 688136 | tf_op jit(solution)/shard_map/cond/branch_0_fun/ppermute | solution.py:323
  38.9 1.3 %collective-permute-start.3 = (bf16[144,1024]{1,0:T(8,128)(2,1)S(1)}, bf16[144,1024]{1,0:T(8,128)(2,1)S(1)}, u32[]{:S(2)}, u32[]{:S(2)}) collective-permute-start(bf16[144,1024]{1,0:T(8,128)(2,1)S(1)} %get-tuple-element.93.refs_4_), channel_id=1, source_target_pairs={{0,8},{1,9},{2,10},{3,11},{12,4},{13,5},{14,6},{15,7},{16,24},{17,... | collective-permute-start | bytes 884744 | tf_op jit(solution)/shard_map/cond/branch_0_fun/ppermute | solution.py:323
  40.2 3.6 %branch_0_fun.7 = (bf16[112,1024]{1,0:T(8,128)(2,1)S(1)}, bf16[144,1024]{1,0:T(8,128)(2,1)S(1)}, bf16[112,1024]{1,0:T(8,128)(2,1)S(1)}, bf16[144,1024]{1,0:T(8,128)(2,1)S(1)}) custom-call(bf16[1088,256]{1,0:T(8,128)(2,1)S(1)} %get-tuple-element.79.blocks, bf16[1056,256]{1,0:T(8,128)(2,1)S(1)} %get-tuple-element.80.refs_0_, ...), custom_call_target="tpu_custom_call" | custom-call | flops 10737418240 | bytes 20971520 | tf_op jit(solution)/shard_map/cond/branch_0_fun/pallas_call | solution.py:394
  43.8 0.5 collective-permute-start.4
  44.3 3.0 %collective-permute-done.1.blocks.others = bf16[1088,256]{1,0:T(8,128)(2,1)S(1)} collective-permute-done((bf16[1088,256]{1,0:T(8,128)(2,1)S(1)}, bf16[1088,256]{1,0:T(8,128)(2,1)S(1)}, u32[]{:S(2)}, u32[]{:S(2)}) %collective-permute-start.1) | collective-permute-done | bytes 557088 | tf_op jit(solution)/shard_map/cond/branch_0_fun/ppermute | solution.py:328
  47.3 0.8 %collective-permute-start.5 = (bf16[144,1024]{1,0:T(8,128)(2,1)S(1)}, bf16[144,1024]{1,0:T(8,128)(2,1)S(1)}, u32[]{:S(2)}, u32[]{:S(2)}) collective-permute-start(bf16[144,1024]{1,0:T(8,128)(2,1)S(1)} %get-tuple-element.95.refs_6_), channel_id=1, source_target_pairs={{0,12},{1,13},{2,14},{3,15},{12,0},{13,1},{14,2},{15,3},{16,28},{1... | collective-permute-start | bytes 884744 | tf_op jit(solution)/shard_map/cond/branch_0_fun/ppermute | solution.py:323
  48.2 5.4 %branch_0_fun.9 = (f32[4,1024,256]{2,1,0:T(8,128)S(1)}, f32[4,1024]{1,0:T(4,128)S(1)}) custom-call(bf16[1088,256]{1,0:T(8,128)(2,1)S(1)} %get-tuple-element.79.blocks, bf16[112,1024]{1,0:T(8,128)(2,1)S(1)} %get-tuple-element.88.refs_0_, bf16[144,1024]{1,0:T(8,128)(2,1)S(1)} %get-tuple-element.89.refs_1_, bf16[256,1024]{1,0:T(8,128)(2,1)S(1)} %get-tuple-element.90.refs_2_, ...), custom_call_target="tpu_custom_call" | custom-call | flops 2147483648 | bytes 4194304 | tf_op jit(solution)/shard_map/cond/branch_0_fun/pallas_call | solution.py:419
  53.5 5.0 %branch_0_fun.10.soft = bf16[1024,1024]{1,0:T(8,128)(2,1)S(1)} custom-call(bf16[1088,256]{1,0:T(8,128)(2,1)S(1)} %collective-permute-done.1.blocks.others, bf16[1056,256]{1,0:T(8,128)(2,1)S(1)} %get-tuple-element.80.refs_0_, bf16[1056,256]{1,0:T(8,128)(2,1)S(1)} %get-tuple-element.81.refs_1_, bf16[1056,256]{1,0:T(8,128)(2,1)S(1)} %get-tuple-element.82.refs_2_, ...), custom_call_target="tpu_custom_call" | custom-call | tf_op jit(solution)/shard_map/cond/branch_0_fun/pallas_call | solution.py:428
  58.6 0.0 collective-permute-done.2.refs_3_
  58.6 1.1 %collective-permute-done.3.refs_4_ = bf16[144,1024]{1,0:T(8,128)(2,1)S(1)} collective-permute-done((bf16[144,1024]{1,0:T(8,128)(2,1)S(1)}, bf16[144,1024]{1,0:T(8,128)(2,1)S(1)}, u32[]{:S(2)}, u32[]{:S(2)}) %collective-permute-start.3) | collective-permute-done | bytes 294944 | tf_op jit(solution)/shard_map/cond/branch_0_fun/ppermute | solution.py:323
  59.7 5.1 %branch_0_fun.12 = (f32[2,1024,256]{2,1,0:T(8,128)S(1)}, f32[2,4,256]{2,1,0:T(4,128)S(1)}, bf16[2,1040,256]{2,1,0:T(8,128)(2,1)S(1)}) custom-call(bf16[1088,256]{1,0:T(8,128)(2,1)S(1)} %collective-permute-done.1.blocks.others, bf16[1024,1024]{1,0:T(8,128)(2,1)S(1)} %branch_0_fun.10.soft, bf16[2,1024,256]{2,1,0:T(8,128)(2,1)S(1)} %get-tuple-element.101.centres, ...), custom_call_target="tpu_custom_call" | custom-call | flops 2147483648 | bytes 4194304 | tf_op jit(solution)/shard_map/cond/branch_0_fun/pallas_call | solution.py:437
  64.7 0.1 collective-permute-start.6
  64.8 8.3 %collective-permute-done.4.refs_5_ = bf16[112,1024]{1,0:T(8,128)(2,1)S(1)} collective-permute-done((bf16[112,1024]{1,0:T(8,128)(2,1)S(1)}, bf16[112,1024]{1,0:T(8,128)(2,1)S(1)}, u32[]{:S(2)}, u32[]{:S(2)}) %collective-permute-start.4) | collective-permute-done | bytes 229408 | tf_op jit(solution)/shard_map/cond/branch_0_fun/ppermute | solution.py:323
  73.1 0.0 collective-permute-done.5.refs_6_
  73.1 0.0 collective-permute-done.refs_2_
  73.1 2.5 %branch_0_fun.11 = bf16[512,1024]{1,0:T(8,128)(2,1)} custom-call(s32[512,1]{1,0:T(8,128)S(1)} %get-tuple-element.78.slot, bf16[112,1024]{1,0:T(8,128)(2,1)S(1)} %get-tuple-element.88.refs_0_, bf16[144,1024]{1,0:T(8,128)(2,1)S(1)} %get-tuple-element.89.refs_1_, bf16[256,1024]{1,0:T(8,128)(2,1)S(1)} %collective-permute-done.refs_2_, ...), custom_call_target="tpu_custom_call" | custom-call | flops 53687091200 | bytes 209715200 | tf_op jit(solution)/shard_map/cond/branch_0_fun/pallas_call | solution.py:456
  75.6 0.0 collective-permute-done.6.got
  75.6 2.0 %branch_0_fun.13 = f32[2,1024,256]{2,1,0:T(8,128)} custom-call(f32[2,1024,256]{2,1,0:T(8,128)S(1)} %get-tuple-element.104.mine, f32[2,4,256]{2,1,0:T(4,128)S(1)} %get-tuple-element.105.mass, bf16[2,1040,256]{2,1,0:T(8,128)(2,1)S(1)} %collective-permute-done.6.got), custom_call_target="tpu_custom_call" | custom-call | flops 2097152 | bytes 5242880 | tf_op jit(solution)/shard_map/cond/branch_0_fun/pallas_call | solution.py:463
  (15 shorter events, 0.3 us)
Async XLA Ops:
  0.6 5.1 %copy-start.1 = (s32[512]{0:T(512)S(1)}, s32[512]{0:T(512)}, u32[]{:S(2)}) copy-start(s32[512]{0:T(512)} %param.8) | copy-start | bytes 6148
  0.6 5.1 %copy-start = (f32[512,256]{1,0:T(8,128)S(1)}, f32[512,256]{1,0:T(8,128)}, u32[]{:S(2)}) copy-start(f32[512,256]{1,0:T(8,128)} %codes.1) | copy-start | bytes 1572868
  1.5 3.2 %copy-start.2 = (bf16[2,1024,256]{2,1,0:T(8,128)(2,1)S(1)}, bf16[2,1024,256]{2,1,0:T(8,128)(2,1)}, u32[]{:S(2)}) copy-start(bf16[2,1024,256]{2,1,0:T(8,128)(2,1)} %centres.3) | copy-start | bytes 3145732
  3.1 20.5 %collective-permute-start.26 = (bf16[1056,256]{1,0:T(8,128)(2,1)S(1)}, bf16[1056,256]{1,0:T(8,128)(2,1)S(1)}, u32[]{:S(2)}, u32[]{:S(2)}) collective-permute-start(bf16[1056,256]{1,0:T(8,128)(2,1)S(1)} %shard_map.65.x), channel_id=1, source_target_pairs={{0,2},{1,3},{2,0},{3,1},{4,6},{5,7},{6,4},{7,5},{8,10},{9,11},{10,... | collective-permute-start | bytes 1622024 | tf_op jit(solution)/shard_map/ppermute | solution.py:328
  5.1 23.6 %collective-permute-start.27 = (bf16[1056,256]{1,0:T(8,128)(2,1)S(1)}, bf16[1056,256]{1,0:T(8,128)(2,1)S(1)}, u32[]{:S(2)}, u32[]{:S(2)}) collective-permute-start(bf16[1056,256]{1,0:T(8,128)(2,1)S(1)} %shard_map.67.x), channel_id=1, source_target_pairs={{0,2},{1,3},{2,0},{3,1},{4,6},{5,7},{6,4},{7,5},{8,10},{9,11},{10,... | collective-permute-start | bytes 1622024 | tf_op jit(solution)/shard_map/ppermute | solution.py:328
  7.3 6.1 %collective-permute-start.21 = (bf16[272,256]{1,0:T(8,128)(2,1)S(1)}, bf16[272,256]{1,0:T(8,128)(2,1)S(1)}, u32[]{:S(2)}, u32[]{:S(2)}) collective-permute-start(bf16[272,256]{1,0:T(8,128)(2,1)S(1)} %get-tuple-element.187), channel_id=1, source_target_pairs={{0,4},{1,5},{2,6},{3,7},{4,0},{5,1},{6,2},{7,3},{8,12},{9,13},{10,... | collective-permute-start | bytes 417800 | tf_op jit(solution)/shard_map/ppermute | solution.py:323
  7.4 12.6 %collective-permute-start.22 = (bf16[272,256]{1,0:T(8,128)(2,1)S(1)}, bf16[272,256]{1,0:T(8,128)(2,1)S(1)}, u32[]{:S(2)}, u32[]{:S(2)}) collective-permute-start(bf16[272,256]{1,0:T(8,128)(2,1)S(1)} %get-tuple-element.188), channel_id=1, source_target_pairs={{0,8},{1,9},{2,10},{3,11},{4,12},{5,13},{6,14},{7,15},{8,0},{9,1},... | collective-permute-start | bytes 417800 | tf_op jit(solution)/shard_map/ppermute | solution.py:323
  10.4 12.0 %collective-permute-start.23 = (bf16[272,256]{1,0:T(8,128)(2,1)S(1)}, bf16[272,256]{1,0:T(8,128)(2,1)S(1)}, u32[]{:S(2)}, u32[]{:S(2)}) collective-permute-start(bf16[272,256]{1,0:T(8,128)(2,1)S(1)} %get-tuple-element.189), channel_id=1, source_target_pairs={{0,12},{1,13},{2,14},{3,15},{4,8},{5,9},{6,10},{7,11},{8,4},{9,5},... | collective-permute-start | bytes 417800 | tf_op jit(solution)/shard_map/ppermute | solution.py:323
  22.4 7.2 %collective-permute-start.24 = (bf16[1056,256]{1,0:T(8,128)(2,1)S(1)}, bf16[1056,256]{1,0:T(8,128)(2,1)S(1)}, u32[]{:S(2)}, u32[]{:S(2)}) collective-permute-start(bf16[1056,256]{1,0:T(8,128)(2,1)S(1)} %shard_map.65.x), channel_id=1, source_target_pairs={{0,1},{1,0},{2,3},{3,2},{4,5},{5,4},{6,7},{7,6},{8,9},{9,8},{10,11... | collective-permute-start | bytes 1622024 | tf_op jit(solution)/shard_map/ppermute | solution.py:328
  22.4 7.2 %collective-permute-start.25 = (bf16[1056,256]{1,0:T(8,128)(2,1)S(1)}, bf16[1056,256]{1,0:T(8,128)(2,1)S(1)}, u32[]{:S(2)}, u32[]{:S(2)}) collective-permute-start(bf16[1056,256]{1,0:T(8,128)(2,1)S(1)} %shard_map.67.x), channel_id=1, source_target_pairs={{0,1},{1,0},{2,3},{3,2},{4,5},{5,4},{6,7},{7,6},{8,9},{9,8},{10,11... | collective-permute-start | bytes 1622024 | tf_op jit(solution)/shard_map/ppermute | solution.py:328
  23.6 6.1 %collective-permute-start.28 = (bf16[1056,256]{1,0:T(8,128)(2,1)S(1)}, bf16[1056,256]{1,0:T(8,128)(2,1)S(1)}, u32[]{:S(2)}, u32[]{:S(2)}) collective-permute-start(bf16[1056,256]{1,0:T(8,128)(2,1)S(1)} %collective-permute-done.26.x), channel_id=1, source_target_pairs={{0,1},{1,0},{2,3},{3,2},{4,5},{5,4},{6,7},{7,6},{8,9},{9,8},{10,11... | collective-permute-start | bytes 1622024 | tf_op jit(solution)/shard_map/ppermute | solution.py:328
  28.7 1.9 %collective-permute-start.29 = (bf16[1056,256]{1,0:T(8,128)(2,1)S(1)}, bf16[1056,256]{1,0:T(8,128)(2,1)S(1)}, u32[]{:S(2)}, u32[]{:S(2)}) collective-permute-start(bf16[1056,256]{1,0:T(8,128)(2,1)S(1)} %collective-permute-done.27.x), channel_id=1, source_target_pairs={{0,1},{1,0},{2,3},{3,2},{4,5},{5,4},{6,7},{7,6},{8,9},{9,8},{10,11... | collective-permute-start | bytes 1622024 | tf_op jit(solution)/shard_map/ppermute | solution.py:328
  30.7 1.8 %copy-start.3 = (bf16[2,1024,256]{2,1,0:T(8,128)(2,1)S(1)}, bf16[2,1024,256]{2,1,0:T(8,128)(2,1)}, u32[]{:S(2)}) copy-start(bf16[2,1024,256]{2,1,0:T(8,128)(2,1)} %centres.3) | copy-start | bytes 3145732
  32.5 40.7 %collective-permute-start = (bf16[256,1024]{1,0:T(8,128)(2,1)S(1)}, bf16[256,1024]{1,0:T(8,128)(2,1)S(1)}, u32[]{:S(2)}, u32[]{:S(2)}) collective-permute-start(bf16[256,1024]{1,0:T(8,128)(2,1)S(1)} %get-tuple-element.90.refs_2_), channel_id=1, source_target_pairs={{0,4},{1,5},{2,6},{3,7},{4,0},{5,1},{6,2},{7,3},{8,12},{9,13},{10,... | collective-permute-start | bytes 1572872 | tf_op jit(solution)/shard_map/cond/branch_0_fun/ppermute | solution.py:323
  32.8 14.5 %collective-permute-start.1 = (bf16[1088,256]{1,0:T(8,128)(2,1)S(1)}, bf16[1088,256]{1,0:T(8,128)(2,1)S(1)}, u32[]{:S(2)}, u32[]{:S(2)}) collective-permute-start(bf16[1088,256]{1,0:T(8,128)(2,1)S(1)} %get-tuple-element.79.blocks), channel_id=1, source_target_pairs={{0,2},{1,3},{2,0},{3,1},{4,6},{5,7},{6,4},{7,5},{8,10},{9,11},{10,... | collective-permute-start | bytes 1671176 | tf_op jit(solution)/shard_map/cond/branch_0_fun/ppermute | solution.py:328
  36.3 22.3 %collective-permute-start.2 = (bf16[112,1024]{1,0:T(8,128)(2,1)S(1)}, bf16[112,1024]{1,0:T(8,128)(2,1)S(1)}, u32[]{:S(2)}, u32[]{:S(2)}) collective-permute-start(bf16[112,1024]{1,0:T(8,128)(2,1)S(1)} %get-tuple-element.92.refs_3_), channel_id=1, source_target_pairs={{0,8},{1,9},{2,10},{3,11},{4,12},{5,13},{6,14},{7,15},{8,0},{9,1},... | collective-permute-start | bytes 688136 | tf_op jit(solution)/shard_map/cond/branch_0_fun/ppermute | solution.py:323
  38.9 20.7 %collective-permute-start.3 = (bf16[144,1024]{1,0:T(8,128)(2,1)S(1)}, bf16[144,1024]{1,0:T(8,128)(2,1)S(1)}, u32[]{:S(2)}, u32[]{:S(2)}) collective-permute-start(bf16[144,1024]{1,0:T(8,128)(2,1)S(1)} %get-tuple-element.93.refs_4_), channel_id=1, source_target_pairs={{0,8},{1,9},{2,10},{3,11},{12,4},{13,5},{14,6},{15,7},{16,24},{17,... | collective-permute-start | bytes 884744 | tf_op jit(solution)/shard_map/cond/branch_0_fun/ppermute | solution.py:323
  43.8 29.3 %collective-permute-start.4 = (bf16[112,1024]{1,0:T(8,128)(2,1)S(1)}, bf16[112,1024]{1,0:T(8,128)(2,1)S(1)}, u32[]{:S(2)}, u32[]{:S(2)}) collective-permute-start(bf16[112,1024]{1,0:T(8,128)(2,1)S(1)} %get-tuple-element.94.refs_5_), channel_id=1, source_target_pairs={{0,12},{1,13},{2,14},{3,15},{4,8},{5,9},{6,10},{7,11},{8,4},{9,5},... | collective-permute-start | bytes 688136 | tf_op jit(solution)/shard_map/cond/branch_0_fun/ppermute | solution.py:323
  47.3 25.8 %collective-permute-start.5 = (bf16[144,1024]{1,0:T(8,128)(2,1)S(1)}, bf16[144,1024]{1,0:T(8,128)(2,1)S(1)}, u32[]{:S(2)}, u32[]{:S(2)}) collective-permute-start(bf16[144,1024]{1,0:T(8,128)(2,1)S(1)} %get-tuple-element.95.refs_6_), channel_id=1, source_target_pairs={{0,12},{1,13},{2,14},{3,15},{12,0},{13,1},{14,2},{15,3},{16,28},{1... | collective-permute-start | bytes 884744 | tf_op jit(solution)/shard_map/cond/branch_0_fun/ppermute | solution.py:323
  64.7 10.9 %collective-permute-start.6 = (bf16[2,1040,256]{2,1,0:T(8,128)(2,1)S(1)}, bf16[2,1040,256]{2,1,0:T(8,128)(2,1)S(1)}, u32[]{:S(2)}, u32[]{:S(2)}) collective-permute-start(bf16[2,1040,256]{2,1,0:T(8,128)(2,1)S(1)} %get-tuple-element.106), channel_id=1, source_target_pairs={{0,1},{1,0},{2,3},{3,2},{4,5},{5,4},{6,7},{7,6},{8,9},{9,8},{10,11... | collective-permute-start | bytes 3194888 | tf_op jit(solution)/shard_map/cond/branch_0_fun/ppermute | solution.py:328

commit v7 on v6

--- a/solution.py
+++ b/solution.py
@@ -120,7 +120,7 @@
     terms = [t.astype(F32) for t in three(-0.5 * norm)]
     tiles = []
     for q in range(fine // width):
-        tile = jnp.where(row == 3, sharp[c : c + 1, 0:1].astype(F32), 0.0)
+        tile = jnp.where(row == 3, sharp[0:1, c : c + 1].astype(F32), 0.0)
         for t in range(3):
             tile = jnp.where(row == t, terms[t][:, q * width : (q + 1) * width], tile)
         tiles.append(tile)
@@ -327,7 +327,7 @@
     def swap(x, mask):
         return lax.ppermute(x, "route", [(r, r ^ mask) for r in range(route)])
 
-    sharp = sharpness.reshape(per_device, 1)
+    sharp = sharpness.reshape(1, per_device)
     own, far = [], []
     for c in range(per_device):
         own.append(

time: 77.8 us -> 77.7 us (level); the launches traced: 77.6 us -> 76.5 us
  waiting for transfers between devices: 29.9 us -> 21.7 us
  starting transfers between devices: 13.7 us -> 20.5 us
    ppermute x8, starting transfers between devices: 9.14 us -> 16 us  [turn(): return lax.ppermute(x, 'route', pairs)]
    ppermute x8, waiting for transfers between devices: 21 us -> 15.7 us  [turn(): return lax.ppermute(x, 'route', pairs)]
    ppermute x8, waiting for transfers between devices: 8.92 us -> 5.94 us  [swap(): return lax.ppermute(x, 'route', [(r, r ^ mask) for r in range(route)])]
    reshape x1 -> x0, local copies, waits for them, and re-layouts: 0.81 us -> none  [shards(): sharp = sharpness.reshape(per_device, 1)]
  transfers between devices with their start and end apart: 16 -> 16, of which waited for: 8 -> 6; matrix products, arithmetic and copies ran while one was open for 0% -> 0% of each run, Pallas kernels for 34% -> 35%
where the time goes in v7:
time: 77.7 us; the launch traced here: 76.5 us
  Pallas kernels  31.9 us (41%)
  waiting for transfers between devices  21.7 us (28%)
  starting transfers between devices  20.5 us (26%)
  between operations  1.46 us (2%)
    ppermute x8, starting transfers between devices, turn(): return lax.ppermute(x, 'route', pairs)  16 us
    ppermute x8, waiting for transfers between devices, turn(): return lax.ppermute(x, 'route', pairs)  15.7 us
    ppermute x8, waiting for transfers between devices, swap(): return lax.ppermute(x, 'route', [(r, r ^ mask) for r in range(route)])  5.94 us
    pallas_call x1, Pallas kernels, refine(): call(functools.partial(here_body, rows), [jax.ShapeDtypeStruct(*sums_shap...  5.39 us
    pallas_call x1, Pallas kernels, refine(): call(functools.partial(sums_body, rows), [jax.ShapeDtypeStruct(centroids....  5.23 us
    pallas_call x1, Pallas kernels, refine(): call(functools.partial(other_body, groups, rows), jax.ShapeDtypeStruct((g...  5.02 us
    ppermute x8, starting transfers between devices, swap(): return lax.ppermute(x, 'route', [(r, r ^ mask) for r in range(route)])  4.55 us
    pallas_call x1, Pallas kernels, refine(): call(functools.partial(softs_body, rows, len(held), late), half * len(lat...  3.59 us
  transfers between devices with their start and end apart: 16, of which 6 were waited for; matrix products, arithmetic and copies ran while one was open for 0% of the time, Pallas kernels for 35%

profile of v7, /device:TPU:8, one launch (start us, length us, event | category | flops | bytes accessed | tf_op | source)
XLA Modules:
  0.0 76.5 jit_solution(17631408597928280154)
XLA Ops:
  0.6 0.6 copy-done
  1.3 1.6 %shard_map.65.x = bf16[1056,256]{1,0:T(8,128)(2,1)S(1)} custom-call(bf16[1,2]{1,0:T(2,128)(2,1)S(1)} %bitcast.4, bf16[2,1024,256]{2,1,0:T(8,128)(2,1)} %centres.3), custom_call_target="tpu_custom_call" | custom-call | flops 41943040 | bytes 5242880 | tf_op jit(solution)/shard_map/pallas_call | solution.py:334
  2.9 1.6 %collective-permute-start.26 = (bf16[1056,256]{1,0:T(8,128)(2,1)S(1)}, bf16[1056,256]{1,0:T(8,128)(2,1)S(1)}, u32[]{:S(2)}, u32[]{:S(2)}) collective-permute-start(bf16[1056,256]{1,0:T(8,128)(2,1)S(1)} %shard_map.65.x), channel_id=1, source_target_pairs={{0,2},{1,3},{2,0},{3,1},{4,6},{5,7},{6,4},{7,5},{8,10},{9,11},{10,... | collective-permute-start | bytes 1622024 | tf_op jit(solution)/shard_map/ppermute | solution.py:328
  4.5 0.0 copy-done.3
  4.5 0.5 shard_map.67.x
  5.0 0.6 collective-permute-start.27
  5.6 1.6 %shard_map.66 = (bf16[272,256]{1,0:T(8,128)(2,1)S(1)}, bf16[272,256]{1,0:T(8,128)(2,1)S(1)}, bf16[272,256]{1,0:T(8,128)(2,1)S(1)}, bf16[272,256]{1,0:T(8,128)(2,1)S(1)}, s32[512,1]{1,0:T(8,128)S(1)}) custom-call(s32[1]{0:T(128)} %bitcast.here, s32[1,512]{1,0:T(1,128)S(1)} %bitcast.6, f32[512,256]{1,0:T(8,128)S(1)} %copy-done.1), custom_call_target="tpu_custom_call" | custom-call | flops 1342177280 | bytes 5242880 | tf_op jit(solution)/shard_map/pallas_call | solution.py:347
  7.2 0.1 collective-permute-start.21
  7.3 3.0 %collective-permute-start.22 = (bf16[272,256]{1,0:T(8,128)(2,1)S(1)}, bf16[272,256]{1,0:T(8,128)(2,1)S(1)}, u32[]{:S(2)}, u32[]{:S(2)}) collective-permute-start(bf16[272,256]{1,0:T(8,128)(2,1)S(1)} %get-tuple-element.188), channel_id=1, source_target_pairs={{0,8},{1,9},{2,10},{3,11},{4,12},{5,13},{6,14},{7,15},{8,0},{9,1},... | collective-permute-start | bytes 417800 | tf_op jit(solution)/shard_map/ppermute | solution.py:323
  10.3 0.4 collective-permute-start.23
  10.7 2.5 %collective-permute-done.21.refs_1_.block = bf16[272,256]{1,0:T(8,128)(2,1)S(1)} collective-permute-done((bf16[272,256]{1,0:T(8,128)(2,1)S(1)}, bf16[272,256]{1,0:T(8,128)(2,1)S(1)}, u32[]{:S(2)}, u32[]{:S(2)}) %collective-permute-start.21) | collective-permute-done | bytes 139296 | tf_op jit(solution)/shard_map/ppermute | solution.py:323
  13.2 6.6 %collective-permute-done.22.refs_2_ = bf16[272,256]{1,0:T(8,128)(2,1)S(1)} collective-permute-done((bf16[272,256]{1,0:T(8,128)(2,1)S(1)}, bf16[272,256]{1,0:T(8,128)(2,1)S(1)}, u32[]{:S(2)}, u32[]{:S(2)}) %collective-permute-start.22) | collective-permute-done | bytes 139296 | tf_op jit(solution)/shard_map/ppermute | solution.py:323
  19.9 2.4 %collective-permute-done.23.refs_3_ = bf16[272,256]{1,0:T(8,128)(2,1)S(1)} collective-permute-done((bf16[272,256]{1,0:T(8,128)(2,1)S(1)}, bf16[272,256]{1,0:T(8,128)(2,1)S(1)}, u32[]{:S(2)}, u32[]{:S(2)}) %collective-permute-start.23) | collective-permute-done | bytes 139296 | tf_op jit(solution)/shard_map/ppermute | solution.py:323
  22.3 0.0 collective-permute-start.24
  22.3 0.5 collective-permute-start.25
  22.8 0.7 shard_map.68
  23.5 0.0 collective-permute-done.26.x
  23.5 0.1 collective-permute-start.28
  23.5 5.0 %collective-permute-done.27.x = bf16[1056,256]{1,0:T(8,128)(2,1)S(1)} collective-permute-done((bf16[1056,256]{1,0:T(8,128)(2,1)S(1)}, bf16[1056,256]{1,0:T(8,128)(2,1)S(1)}, u32[]{:S(2)}, u32[]{:S(2)}) %collective-permute-start.27) | collective-permute-done | bytes 540704 | tf_op jit(solution)/shard_map/ppermute | solution.py:328
  28.6 0.0 collective-permute-start.29
  29.4 0.0 collective-permute-done.24.x
  29.5 0.0 collective-permute-done.25.x
  29.6 0.0 collective-permute-done.28.x
  29.6 0.9 %collective-permute-done.29.x = bf16[1056,256]{1,0:T(8,128)(2,1)S(1)} collective-permute-done((bf16[1056,256]{1,0:T(8,128)(2,1)S(1)}, bf16[1056,256]{1,0:T(8,128)(2,1)S(1)}, u32[]{:S(2)}, u32[]{:S(2)}) %collective-permute-start.29) | collective-permute-done | bytes 540704 | tf_op jit(solution)/shard_map/ppermute | solution.py:328
  30.5 0.0 copy-start.4
  30.6 1.7 %shard_map.77 = bf16[256,1024]{1,0:T(8,128)(2,1)S(1)} custom-call(bf16[272,256]{1,0:T(8,128)(2,1)S(1)} %collective-permute-done.21.refs_1_.block, bf16[1056,256]{1,0:T(8,128)(2,1)S(1)} %shard_map.69.refs_0_, bf16[1056,256]{1,0:T(8,128)(2,1)S(1)} %shard_map.70.refs_1_, bf16[1056,256]{1,0:T(8,128)(2,1)S(1)} %shard_map.71.refs_2_, ...), custom_call_target="tpu_custom_call" | custom-call | flops 5368709120 | bytes 20971520 | tf_op jit(solution)/shard_map/pallas_call | solution.py:382
  32.3 44.2 %conditional.1 = (bf16[512,1024]{1,0:T(8,128)(2,1)}, f32[2,1024,256]{2,1,0:T(8,128)}) conditional(s32[]{:T(128)} %bitcast.3, (bf16[1088,256]{1,0:T(8,128)(2,1)S(1)}, bf16[1056,256]{1,0:T(8,128)(2,1)S(1)}, bf16[1056,256]{1,0:T(8,128)(2,1)S(1)}, bf16[1056,256]{1,0:T(8,128)(2,1)S(1)}, bf16[1056,256]{1,0:T(8,128)(2,1)S(1)}, ...), branch_computations={%region_0.0_spmd, %region_1.0_spmd, %region_2.0_spmd} | conditional | flops 74090283008 | bytes 278069504 | solution.py:477
  32.6 0.3 collective-permute-start.7
  32.9 1.7 %collective-permute-start.8 = (bf16[1088,256]{1,0:T(8,128)(2,1)S(1)}, bf16[1088,256]{1,0:T(8,128)(2,1)S(1)}, u32[]{:S(2)}, u32[]{:S(2)}) collective-permute-start(bf16[1088,256]{1,0:T(8,128)(2,1)S(1)} %get-tuple-element.108.blocks), channel_id=1, source_target_pairs={{0,2},{1,3},{2,0},{3,1},{4,6},{5,7},{6,4},{7,5},{8,10},{9,11},{10,... | collective-permute-start | bytes 1671176 | tf_op jit(solution)/shard_map/cond/branch_1_fun/ppermute | solution.py:328
  34.6 1.7 %branch_1_fun.8 = (bf16[112,1024]{1,0:T(8,128)(2,1)S(1)}, bf16[144,1024]{1,0:T(8,128)(2,1)S(1)}) custom-call(bf16[272,256]{1,0:T(8,128)(2,1)S(1)} %get-tuple-element.120.block, bf16[1056,256]{1,0:T(8,128)(2,1)S(1)} %get-tuple-element.109.refs_0_, bf16[1056,256]{1,0:T(8,128)(2,1)S(1)} %get-tuple-element.110.refs_1_, ...), custom_call_target="tpu_custom_call" | custom-call | flops 5368709120 | bytes 20971520 | tf_op jit(solution)/shard_map/cond/branch_1_fun/pallas_call | solution.py:403
  36.4 2.7 %collective-permute-start.9 = (bf16[112,1024]{1,0:T(8,128)(2,1)S(1)}, bf16[112,1024]{1,0:T(8,128)(2,1)S(1)}, u32[]{:S(2)}, u32[]{:S(2)}) collective-permute-start(bf16[112,1024]{1,0:T(8,128)(2,1)S(1)} %get-tuple-element.121.refs_3_), channel_id=1, source_target_pairs={{0,8},{1,9},{2,10},{3,11},{4,12},{5,13},{6,14},{7,15},{8,0},{9,1},... | collective-permute-start | bytes 688136 | tf_op jit(solution)/shard_map/cond/branch_1_fun/ppermute | solution.py:323
  39.0 2.2 %collective-permute-start.10 = (bf16[144,1024]{1,0:T(8,128)(2,1)S(1)}, bf16[144,1024]{1,0:T(8,128)(2,1)S(1)}, u32[]{:S(2)}, u32[]{:S(2)}) collective-permute-start(bf16[144,1024]{1,0:T(8,128)(2,1)S(1)} %get-tuple-element.122.refs_4_), channel_id=1, source_target_pairs={{4,12},{5,13},{6,14},{7,15},{8,0},{9,1},{10,2},{11,3},{20,28},{21,... | collective-permute-start | bytes 884744 | tf_op jit(solution)/shard_map/cond/branch_1_fun/ppermute | solution.py:323
  41.3 3.6 %branch_1_fun.7 = (bf16[112,1024]{1,0:T(8,128)(2,1)S(1)}, bf16[144,1024]{1,0:T(8,128)(2,1)S(1)}, bf16[112,1024]{1,0:T(8,128)(2,1)S(1)}, bf16[144,1024]{1,0:T(8,128)(2,1)S(1)}) custom-call(bf16[1088,256]{1,0:T(8,128)(2,1)S(1)} %get-tuple-element.108.blocks, bf16[1056,256]{1,0:T(8,128)(2,1)S(1)} %get-tuple-element.109.refs_0_, ...), custom_call_target="tpu_custom_call" | custom-call | flops 10737418240 | bytes 20971520 | tf_op jit(solution)/shard_map/cond/branch_1_fun/pallas_call | solution.py:394
  44.9 2.8 %collective-permute-start.11 = (bf16[112,1024]{1,0:T(8,128)(2,1)S(1)}, bf16[112,1024]{1,0:T(8,128)(2,1)S(1)}, u32[]{:S(2)}, u32[]{:S(2)}) collective-permute-start(bf16[112,1024]{1,0:T(8,128)(2,1)S(1)} %get-tuple-element.123.refs_5_), channel_id=1, source_target_pairs={{0,12},{1,13},{2,14},{3,15},{4,8},{5,9},{6,10},{7,11},{8,4},{9,5},... | collective-permute-start | bytes 688136 | tf_op jit(solution)/shard_map/cond/branch_1_fun/ppermute | solution.py:323
  47.6 0.0 collective-permute-done.8.blocks.others
  47.6 4.4 %collective-permute-start.12 = (bf16[144,1024]{1,0:T(8,128)(2,1)S(1)}, bf16[144,1024]{1,0:T(8,128)(2,1)S(1)}, u32[]{:S(2)}, u32[]{:S(2)}) collective-permute-start(bf16[144,1024]{1,0:T(8,128)(2,1)S(1)} %get-tuple-element.124.refs_6_), channel_id=1, source_target_pairs={{4,8},{5,9},{6,10},{7,11},{8,4},{9,5},{10,6},{11,7},{20,24},{21,25... | collective-permute-start | bytes 884744 | tf_op jit(solution)/shard_map/cond/branch_1_fun/ppermute | solution.py:323
  52.1 5.4 %branch_1_fun.9 = (f32[4,1024,256]{2,1,0:T(8,128)S(1)}, f32[4,1024]{1,0:T(4,128)S(1)}) custom-call(bf16[1088,256]{1,0:T(8,128)(2,1)S(1)} %get-tuple-element.108.blocks, bf16[112,1024]{1,0:T(8,128)(2,1)S(1)} %get-tuple-element.117.refs_0_, bf16[144,1024]{1,0:T(8,128)(2,1)S(1)} %get-tuple-element.118.refs_1_, ...), custom_call_target="tpu_custom_call" | custom-call | flops 2147483648 | bytes 4194304 | tf_op jit(solution)/shard_map/cond/branch_1_fun/pallas_call | solution.py:419
  57.5 5.0 %branch_1_fun.10.soft = bf16[1024,1024]{1,0:T(8,128)(2,1)S(1)} custom-call(bf16[1088,256]{1,0:T(8,128)(2,1)S(1)} %collective-permute-done.8.blocks.others, bf16[1056,256]{1,0:T(8,128)(2,1)S(1)} %get-tuple-element.109.refs_0_, bf16[1056,256]{1,0:T(8,128)(2,1)S(1)} %get-tuple-element.110.refs_1_, bf16[1056,256]{1,0:T(8,128)(2,1)S(1)} %get-tuple-element.111.refs_2_, ...), custom_call_target="tpu_custom_call" | custom-call | tf_op jit(solution)/shard_map/cond/branch_1_fun/pallas_call | solution.py:428
  62.5 0.0 collective-permute-done.9.refs_3_
  62.5 0.0 collective-permute-done.10.refs_4_
  62.5 5.2 %branch_1_fun.12 = (f32[2,1024,256]{2,1,0:T(8,128)S(1)}, f32[2,4,256]{2,1,0:T(4,128)S(1)}, bf16[2,1040,256]{2,1,0:T(8,128)(2,1)S(1)}) custom-call(bf16[1088,256]{1,0:T(8,128)(2,1)S(1)} %collective-permute-done.8.blocks.others, bf16[1024,1024]{1,0:T(8,128)(2,1)S(1)} %branch_1_fun.10.soft, bf16[2,1024,256]{2,1,0:T(8,128)(2,1)S(1)} %get-tuple-element.130.centres, ...), custom_call_target="tpu_custom_call" | custom-call | flops 2147483648 | bytes 4194304 | tf_op jit(solution)/shard_map/cond/branch_1_fun/pallas_call | solution.py:437
  67.8 0.1 collective-permute-start.13
  67.8 0.0 collective-permute-done.11.refs_5_
  67.8 4.2 %collective-permute-done.12.refs_6_ = bf16[144,1024]{1,0:T(8,128)(2,1)S(1)} collective-permute-done((bf16[144,1024]{1,0:T(8,128)(2,1)S(1)}, bf16[144,1024]{1,0:T(8,128)(2,1)S(1)}, u32[]{:S(2)}, u32[]{:S(2)}) %collective-permute-start.12) | collective-permute-done | bytes 294944 | tf_op jit(solution)/shard_map/cond/branch_1_fun/ppermute | solution.py:323
  72.0 0.0 collective-permute-done.7.refs_2_
  72.0 2.5 %branch_1_fun.11 = bf16[512,1024]{1,0:T(8,128)(2,1)} custom-call(s32[512,1]{1,0:T(8,128)S(1)} %get-tuple-element.107.slot, bf16[112,1024]{1,0:T(8,128)(2,1)S(1)} %get-tuple-element.117.refs_0_, bf16[144,1024]{1,0:T(8,128)(2,1)S(1)} %get-tuple-element.118.refs_1_, bf16[256,1024]{1,0:T(8,128)(2,1)S(1)} %collective-permute-done.7.refs_2_, ...), custom_call_target="tpu_custom_call" | custom-call | flops 53687091200 | bytes 209715200 | tf_op jit(solution)/shard_map/cond/branch_1_fun/pallas_call | solution.py:456
  74.5 0.0 collective-permute-done.13.got
  74.5 2.0 %branch_1_fun.13 = f32[2,1024,256]{2,1,0:T(8,128)} custom-call(f32[2,1024,256]{2,1,0:T(8,128)S(1)} %get-tuple-element.133.mine, f32[2,4,256]{2,1,0:T(4,128)S(1)} %get-tuple-element.134.mass, bf16[2,1040,256]{2,1,0:T(8,128)(2,1)S(1)} %collective-permute-done.13.got), custom_call_target="tpu_custom_call" | custom-call | flops 2097152 | bytes 5242880 | tf_op jit(solution)/shard_map/cond/branch_1_fun/pallas_call | solution.py:463
  (16 shorter events, 0.3 us)
Async XLA Ops:
  0.6 0.7 copy-start
  1.3 3.2 %copy-start.3 = (bf16[2,1024,256]{2,1,0:T(8,128)(2,1)S(1)}, bf16[2,1024,256]{2,1,0:T(8,128)(2,1)}, u32[]{:S(2)}) copy-start(bf16[2,1024,256]{2,1,0:T(8,128)(2,1)} %centres.3) | copy-start | bytes 3145732
  1.3 4.3 %copy-start.1 = (f32[512,256]{1,0:T(8,128)S(1)}, f32[512,256]{1,0:T(8,128)}, u32[]{:S(2)}) copy-start(f32[512,256]{1,0:T(8,128)} %codes.1) | copy-start | bytes 1572868
  1.3 4.3 %copy-start.2 = (s32[512]{0:T(512)S(1)}, s32[512]{0:T(512)}, u32[]{:S(2)}) copy-start(s32[512]{0:T(512)} %param.8) | copy-start | bytes 6148
  2.9 20.5 %collective-permute-start.26 = (bf16[1056,256]{1,0:T(8,128)(2,1)S(1)}, bf16[1056,256]{1,0:T(8,128)(2,1)S(1)}, u32[]{:S(2)}, u32[]{:S(2)}) collective-permute-start(bf16[1056,256]{1,0:T(8,128)(2,1)S(1)} %shard_map.65.x), channel_id=1, source_target_pairs={{0,2},{1,3},{2,0},{3,1},{4,6},{5,7},{6,4},{7,5},{8,10},{9,11},{10,... | collective-permute-start | bytes 1622024 | tf_op jit(solution)/shard_map/ppermute | solution.py:328
  5.0 23.6 %collective-permute-start.27 = (bf16[1056,256]{1,0:T(8,128)(2,1)S(1)}, bf16[1056,256]{1,0:T(8,128)(2,1)S(1)}, u32[]{:S(2)}, u32[]{:S(2)}) collective-permute-start(bf16[1056,256]{1,0:T(8,128)(2,1)S(1)} %shard_map.67.x), channel_id=1, source_target_pairs={{0,2},{1,3},{2,0},{3,1},{4,6},{5,7},{6,4},{7,5},{8,10},{9,11},{10,... | collective-permute-start | bytes 1622024 | tf_op jit(solution)/shard_map/ppermute | solution.py:328
  7.2 6.1 %collective-permute-start.21 = (bf16[272,256]{1,0:T(8,128)(2,1)S(1)}, bf16[272,256]{1,0:T(8,128)(2,1)S(1)}, u32[]{:S(2)}, u32[]{:S(2)}) collective-permute-start(bf16[272,256]{1,0:T(8,128)(2,1)S(1)} %get-tuple-element.187), channel_id=1, source_target_pairs={{0,4},{1,5},{2,6},{3,7},{4,0},{5,1},{6,2},{7,3},{8,12},{9,13},{10,... | collective-permute-start | bytes 417800 | tf_op jit(solution)/shard_map/ppermute | solution.py:323
  7.3 12.6 %collective-permute-start.22 = (bf16[272,256]{1,0:T(8,128)(2,1)S(1)}, bf16[272,256]{1,0:T(8,128)(2,1)S(1)}, u32[]{:S(2)}, u32[]{:S(2)}) collective-permute-start(bf16[272,256]{1,0:T(8,128)(2,1)S(1)} %get-tuple-element.188), channel_id=1, source_target_pairs={{0,8},{1,9},{2,10},{3,11},{4,12},{5,13},{6,14},{7,15},{8,0},{9,1},... | collective-permute-start | bytes 417800 | tf_op jit(solution)/shard_map/ppermute | solution.py:323
  10.3 12.0 %collective-permute-start.23 = (bf16[272,256]{1,0:T(8,128)(2,1)S(1)}, bf16[272,256]{1,0:T(8,128)(2,1)S(1)}, u32[]{:S(2)}, u32[]{:S(2)}) collective-permute-start(bf16[272,256]{1,0:T(8,128)(2,1)S(1)} %get-tuple-element.189), channel_id=1, source_target_pairs={{0,12},{1,13},{2,14},{3,15},{4,8},{5,9},{6,10},{7,11},{8,4},{9,5},... | collective-permute-start | bytes 417800 | tf_op jit(solution)/shard_map/ppermute | solution.py:323
  22.3 7.2 %collective-permute-start.24 = (bf16[1056,256]{1,0:T(8,128)(2,1)S(1)}, bf16[1056,256]{1,0:T(8,128)(2,1)S(1)}, u32[]{:S(2)}, u32[]{:S(2)}) collective-permute-start(bf16[1056,256]{1,0:T(8,128)(2,1)S(1)} %shard_map.65.x), channel_id=1, source_target_pairs={{0,1},{1,0},{2,3},{3,2},{4,5},{5,4},{6,7},{7,6},{8,9},{9,8},{10,11... | collective-permute-start | bytes 1622024 | tf_op jit(solution)/shard_map/ppermute | solution.py:328
  22.3 7.2 %collective-permute-start.25 = (bf16[1056,256]{1,0:T(8,128)(2,1)S(1)}, bf16[1056,256]{1,0:T(8,128)(2,1)S(1)}, u32[]{:S(2)}, u32[]{:S(2)}) collective-permute-start(bf16[1056,256]{1,0:T(8,128)(2,1)S(1)} %shard_map.67.x), channel_id=1, source_target_pairs={{0,1},{1,0},{2,3},{3,2},{4,5},{5,4},{6,7},{7,6},{8,9},{9,8},{10,11... | collective-permute-start | bytes 1622024 | tf_op jit(solution)/shard_map/ppermute | solution.py:328
  23.5 6.1 %collective-permute-start.28 = (bf16[1056,256]{1,0:T(8,128)(2,1)S(1)}, bf16[1056,256]{1,0:T(8,128)(2,1)S(1)}, u32[]{:S(2)}, u32[]{:S(2)}) collective-permute-start(bf16[1056,256]{1,0:T(8,128)(2,1)S(1)} %collective-permute-done.26.x), channel_id=1, source_target_pairs={{0,1},{1,0},{2,3},{3,2},{4,5},{5,4},{6,7},{7,6},{8,9},{9,8},{10,11... | collective-permute-start | bytes 1622024 | tf_op jit(solution)/shard_map/ppermute | solution.py:328
  28.6 1.9 %collective-permute-start.29 = (bf16[1056,256]{1,0:T(8,128)(2,1)S(1)}, bf16[1056,256]{1,0:T(8,128)(2,1)S(1)}, u32[]{:S(2)}, u32[]{:S(2)}) collective-permute-start(bf16[1056,256]{1,0:T(8,128)(2,1)S(1)} %collective-permute-done.27.x), channel_id=1, source_target_pairs={{0,1},{1,0},{2,3},{3,2},{4,5},{5,4},{6,7},{7,6},{8,9},{9,8},{10,11... | collective-permute-start | bytes 1622024 | tf_op jit(solution)/shard_map/ppermute | solution.py:328
  30.5 1.8 %copy-start.4 = (bf16[2,1024,256]{2,1,0:T(8,128)(2,1)S(1)}, bf16[2,1024,256]{2,1,0:T(8,128)(2,1)}, u32[]{:S(2)}) copy-start(bf16[2,1024,256]{2,1,0:T(8,128)(2,1)} %centres.3) | copy-start | bytes 3145732
  32.6 39.4 %collective-permute-start.7 = (bf16[256,1024]{1,0:T(8,128)(2,1)S(1)}, bf16[256,1024]{1,0:T(8,128)(2,1)S(1)}, u32[]{:S(2)}, u32[]{:S(2)}) collective-permute-start(bf16[256,1024]{1,0:T(8,128)(2,1)S(1)} %get-tuple-element.119.refs_2_), channel_id=1, source_target_pairs={{0,4},{1,5},{2,6},{3,7},{4,0},{5,1},{6,2},{7,3},{8,12},{9,13},{10,... | collective-permute-start | bytes 1572872 | tf_op jit(solution)/shard_map/cond/branch_1_fun/ppermute | solution.py:323
  32.9 14.8 %collective-permute-start.8 = (bf16[1088,256]{1,0:T(8,128)(2,1)S(1)}, bf16[1088,256]{1,0:T(8,128)(2,1)S(1)}, u32[]{:S(2)}, u32[]{:S(2)}) collective-permute-start(bf16[1088,256]{1,0:T(8,128)(2,1)S(1)} %get-tuple-element.108.blocks), channel_id=1, source_target_pairs={{0,2},{1,3},{2,0},{3,1},{4,6},{5,7},{6,4},{7,5},{8,10},{9,11},{10,... | collective-permute-start | bytes 1671176 | tf_op jit(solution)/shard_map/cond/branch_1_fun/ppermute | solution.py:328
  36.4 26.1 %collective-permute-start.9 = (bf16[112,1024]{1,0:T(8,128)(2,1)S(1)}, bf16[112,1024]{1,0:T(8,128)(2,1)S(1)}, u32[]{:S(2)}, u32[]{:S(2)}) collective-permute-start(bf16[112,1024]{1,0:T(8,128)(2,1)S(1)} %get-tuple-element.121.refs_3_), channel_id=1, source_target_pairs={{0,8},{1,9},{2,10},{3,11},{4,12},{5,13},{6,14},{7,15},{8,0},{9,1},... | collective-permute-start | bytes 688136 | tf_op jit(solution)/shard_map/cond/branch_1_fun/ppermute | solution.py:323
  39.0 23.5 %collective-permute-start.10 = (bf16[144,1024]{1,0:T(8,128)(2,1)S(1)}, bf16[144,1024]{1,0:T(8,128)(2,1)S(1)}, u32[]{:S(2)}, u32[]{:S(2)}) collective-permute-start(bf16[144,1024]{1,0:T(8,128)(2,1)S(1)} %get-tuple-element.122.refs_4_), channel_id=1, source_target_pairs={{4,12},{5,13},{6,14},{7,15},{8,0},{9,1},{10,2},{11,3},{20,28},{21,... | collective-permute-start | bytes 884744 | tf_op jit(solution)/shard_map/cond/branch_1_fun/ppermute | solution.py:323
  44.9 23.0 %collective-permute-start.11 = (bf16[112,1024]{1,0:T(8,128)(2,1)S(1)}, bf16[112,1024]{1,0:T(8,128)(2,1)S(1)}, u32[]{:S(2)}, u32[]{:S(2)}) collective-permute-start(bf16[112,1024]{1,0:T(8,128)(2,1)S(1)} %get-tuple-element.123.refs_5_), channel_id=1, source_target_pairs={{0,12},{1,13},{2,14},{3,15},{4,8},{5,9},{6,10},{7,11},{8,4},{9,5},... | collective-permute-start | bytes 688136 | tf_op jit(solution)/shard_map/cond/branch_1_fun/ppermute | solution.py:323
  47.6 24.4 %collective-permute-start.12 = (bf16[144,1024]{1,0:T(8,128)(2,1)S(1)}, bf16[144,1024]{1,0:T(8,128)(2,1)S(1)}, u32[]{:S(2)}, u32[]{:S(2)}) collective-permute-start(bf16[144,1024]{1,0:T(8,128)(2,1)S(1)} %get-tuple-element.124.refs_6_), channel_id=1, source_target_pairs={{4,8},{5,9},{6,10},{7,11},{8,4},{9,5},{10,6},{11,7},{20,24},{21,25... | collective-permute-start | bytes 884744 | tf_op jit(solution)/shard_map/cond/branch_1_fun/ppermute | solution.py:323
  67.8 6.7 %collective-permute-start.13 = (bf16[2,1040,256]{2,1,0:T(8,128)(2,1)S(1)}, bf16[2,1040,256]{2,1,0:T(8,128)(2,1)S(1)}, u32[]{:S(2)}, u32[]{:S(2)}) collective-permute-start(bf16[2,1040,256]{2,1,0:T(8,128)(2,1)S(1)} %get-tuple-element.135), channel_id=1, source_target_pairs={{0,1},{1,0},{2,3},{3,2},{4,5},{5,4},{6,7},{7,6},{8,9},{9,8},{10,11... | collective-permute-start | bytes 3194888 | tf_op jit(solution)/shard_map/cond/branch_1_fun/ppermute | solution.py:328
